TPU v7x, 32 devices: a whole 2x2x4 slice. The times are simulated.
32 devices in a mesh: groups: 2 (over y), panel: 4 (over x, core), tok: 4 (over z).
Axes of the slice: x: 2, y: 2, z: 4, core: 2. Of those that a mesh axis runs over, the one named last changes fastest.
Arguments:
- grads: bfloat16 [768, 5120], P(('groups', 'tok'), 'panel'), parts along dimension 0, may hold values from -6 to 6
- acts: bfloat16 [768, 5120], P(('groups', 'panel'), 'tok'), parts along dimension 0, may hold values from -6 to 6
- out_basis: bfloat16 [5120, 5120], P('panel', 'tok'), may hold values from -0.078125 to 0.078125
- in_basis: bfloat16 [5120, 5120], P('tok', 'panel'), may hold values from -0.078125 to 0.078125
- query_rot: bfloat16 [5120, 8, 5120], P('tok', None, 'panel'), may hold values from -0.0011672974 to 0.0011672974
- eigvals: float32 [5120, 5120], P('tok', 'panel'), may hold values from 0.1 to 10
Outputs:
- influence: float32 [768, 8], P(('groups', 'panel', 'tok')), parts along dimension 0
There are 2 independent parts, one for each index of `groups`. A program takes and returns all parts, laid end to end along the dimension named above; an argument that names none is the same for every part. Nothing has to cross between parts.
All inputs are finite; a program needn't handle non-finite values.
Results may differ from a plain program's by a relative error of at most 0.0051.
Values may be sent and summed in bfloat16 or wider, within the bound.
No kernel may reach another device: no remote copies, remote signals or barrier semaphores. Data moves between devices by JAX's collectives and lax.ppermute only.
A program may use at most 256 MiB of HBM per device.

v0:
```python
import math

import jax
import jax.numpy as jnp
from jax import lax
from jax.sharding import PartitionSpec as P

DAMPING = 0.1


def per_device(grads, acts, out_basis, in_basis, query_rot, eigvals):
    grad_all_rows = lax.all_gather(grads, "tok", axis=0, tiled=True)
    grad_sub = lax.all_to_all(grad_all_rows, "panel", split_axis=0, concat_axis=1, tiled=True)
    segment = grad_sub
    grad_local = jnp.dot(
        segment,
        lax.all_gather(out_basis, "panel", axis=0, tiled=True),
        preferred_element_type=jnp.float32,
    ).astype(jnp.bfloat16)
    grad_rot = lax.all_gather(grad_local, "panel", axis=0, tiled=True)
    act_all_rows = lax.all_gather(acts, "panel", axis=0, tiled=True)
    act_sub = lax.all_to_all(act_all_rows, "tok", split_axis=0, concat_axis=1, tiled=True)
    segment = act_sub
    act_local = jnp.dot(
        segment,
        lax.all_gather(in_basis, "tok", axis=0, tiled=True),
        preferred_element_type=jnp.float32,
    ).astype(jnp.bfloat16)
    act_rot = lax.all_gather(act_local, "tok", axis=0, tiled=True)
    shifted = eigvals + DAMPING
    precond = (query_rot.astype(jnp.float32) / shifted[:, None, :]).astype(jnp.bfloat16)
    in_width = precond.shape[0]
    query_count = precond.shape[1]
    col_count = precond.shape[2]
    flattened = precond.reshape(in_width, query_count * col_count)
    row_count = grad_rot.shape[0]
    block_rows = math.gcd(row_count, 512)
    grad_blocks = grad_rot.reshape(row_count // block_rows, block_rows, in_width)
    act_blocks = act_rot.reshape(row_count // block_rows, block_rows, col_count)

    def score_block(members):
        grad_part, act_part = members
        mixed_terms = jnp.dot(grad_part, flattened, preferred_element_type=jnp.float32)
        mixed_terms = mixed_terms.reshape(block_rows, query_count, col_count)
        return jnp.sum(mixed_terms * act_part.astype(jnp.float32)[:, None, :], axis=2)

    partial_value = lax.map(score_block, (grad_blocks, act_blocks)).reshape(row_count, query_count)
    return lax.psum_scatter(partial_value, ("panel", "tok"), scatter_dimension=0, tiled=True)


def solution(mesh):
    placed = (
        P(("groups", "tok"), "panel"),
        P(("groups", "panel"), "tok"),
        P("panel", "tok"),
        P("tok", "panel"),
        P("tok", None, "panel"),
        P("tok", "panel"),
    )
    return jax.shard_map(
        per_device,
        mesh=mesh,
        in_specs=placed,
        out_specs=P(("groups", "panel", "tok"), None),
        check_vma=False,
    )
```

profile of v0, /device:TPU:0, one launch (start us, length us, event | category | flops | bytes accessed | tf_op | source)
XLA Modules:
  0.0 475.7 jit_solution(11862254417076660082)
XLA Ops:
  6.5 0.0 all-gather.5.cloned.1.call-start
  6.5 0.7 all-gather.5.cloned.1.call-update
  7.3 0.0 all-gather.3.cloned.1.call-start
  7.3 0.7 all-gather.3.cloned.1.call-update
  8.0 29.4 %all_gather.18 = bf16[384,1280]{1,0:T(8,128)(2,1)} all-gather(bf16[96,1280]{1,0:T(8,128)(2,1)} %param.8), channel_id=1, replica_groups=mesh['groups'=2,'panel'=4,'tok'=4] {'tok'}, dimensions={0}, use_global_device_ids=true | all-gather | bytes 1228800 | tf_op jit(solution)/shard_map/all_gather | solution.py:12
  37.4 3.5 all-to-all-start
  40.9 6.2 %broadcast_add_fusion = f32[1280,1280]{1,0:T(8,128)} fusion(f32[1280,1280]{1,0:T(8,128)} %param.13), kind=kLoop, calls=%fused_computation.7 | loop fusion | flops 1638400 | bytes 13107200 | tf_op jit(solution)/shard_map/add | solution.py:30
  47.1 0.0 copy-done
  47.1 14.1 %all_gather.21 = bf16[384,1280]{1,0:T(8,128)(2,1)} all-gather(bf16[96,1280]{1,0:T(8,128)(2,1)S(1)} %copy-done), channel_id=1, replica_groups=mesh['groups'=2,'panel'=4,'tok'=4] {'panel'}, dimensions={0}, use_global_device_ids=true | all-gather | bytes 1228800 | tf_op jit(solution)/shard_map/all_gather | solution.py:21
  61.3 0.0 all-to-all-done
  61.3 6.7 %all-to-all-start.1 = ((bf16[4,96,1280]{2,1,0:T(8,128)(2,1)}), bf16[4,96,1280]{2,1,0:T(8,128)(2,1)}, u32[]{:S(2)}, u32[]{:S(2)}) async-start(bf16[4,96,1280]{2,1,0:T(8,128)(2,1)} %bitcast.10), calls=%async_computation.1 | async-start | bytes 1966080 | tf_op jit(solution)/shard_map/all_to_all | solution.py:22
  67.9 21.1 %divide_convert_fusion = bf16[1280,8,1280]{2,1,0:T(8,128)(2,1)} fusion(bf16[1280,8,1280]{2,1,0:T(8,128)(2,1)} %param.12, f32[1280,1280]{1,0:T(8,128)} %broadcast_add_fusion), kind=kLoop, calls=%fused_computation.6 | loop fusion | flops 39321600 | bytes 58982400 | tf_op jit(solution)/shard_map/convert_element_type | solution.py:31
  89.0 0.0 copy-start.1
  89.0 39.3 %copy.12 = bf16[1280,8,1280]{0,2,1:T(8,128)(2,1)} copy(bf16[1280,8,1280]{2,1,0:T(8,128)(2,1)} %divide_convert_fusion) | data formatting | bytes 52428800 | tf_op jit(solution)/shard_map/convert_element_type | solution.py:31
  128.3 0.6 dynamic-slice
  129.6 0.1 copy.16
  129.7 0.0 all-to-all-done.1
  129.7 1.3 copy.17
  131.0 132.5 %all-gather.5.cloned.1.call-done = bf16[5120,1280]{1,0:T(8,128)(2,1)} async-done(((bf16[1280,1280]{1,0:T(8,128)(2,1)}), bf16[5120,1280]{1,0:T(8,128)(2,1)}) %all-gather.5.cloned.1.call-update) | async-done | bytes 13107216 | tf_op jit(solution)/shard_map/all_gather | solution.py:26
  263.5 6.9 %convolution_convert_fusion = bf16[96,1280]{1,0:T(8,128)(2,1)S(1)} fusion(bf16[96,5120]{1,0:T(8,128)(2,1)S(1)} %bitcast.47, bf16[5120,1280]{1,0:T(8,128)(2,1)} %all-gather.5.cloned.1.call-done), kind=kOutput, calls=%fused_computation.8 | convolution fusion | flops 1258414080 | bytes 14336000 | tf_op jit(solution)/shard_map/dot_general | solution.py:24
  270.4 20.6 %all_gather.23 = bf16[384,1280]{1,0:T(8,128)(2,1)S(1)} all-gather(bf16[96,1280]{1,0:T(8,128)(2,1)S(1)} %convolution_convert_fusion), channel_id=1, replica_groups=mesh['groups'=2,'panel'=4,'tok'=4] {'tok'}, dimensions={0}, use_global_device_ids=true | all-gather | bytes 1228800 | tf_op jit(solution)/shard_map/all_gather | solution.py:29
  291.0 58.5 %all-gather.3.cloned.1.call-done = bf16[5120,1280]{1,0:T(8,128)(2,1)} async-done(((bf16[1280,1280]{1,0:T(8,128)(2,1)}), bf16[5120,1280]{1,0:T(8,128)(2,1)}) %all-gather.3.cloned.1.call-update) | async-done | bytes 13107216 | tf_op jit(solution)/shard_map/all_gather | solution.py:17
  349.5 6.9 %convolution_convert_fusion.1 = bf16[96,1280]{1,0:T(8,128)(2,1)S(1)} fusion(bf16[96,5120]{1,0:T(8,128)(2,1)S(1)} %bitcast.46, bf16[5120,1280]{1,0:T(8,128)(2,1)} %all-gather.3.cloned.1.call-done), kind=kOutput, calls=%fused_computation.9 | convolution fusion | flops 1258414080 | bytes 14336000 | tf_op jit(solution)/shard_map/dot_general | solution.py:15
  356.4 9.7 %all_gather.20 = bf16[384,1280]{1,0:T(8,128)(2,1)S(1)} all-gather(bf16[96,1280]{1,0:T(8,128)(2,1)S(1)} %convolution_convert_fusion.1), channel_id=1, replica_groups=mesh['groups'=2,'panel'=4,'tok'=4] {'panel'}, dimensions={0}, use_global_device_ids=true | all-gather | bytes 1228800 | tf_op jit(solution)/shard_map/all_gather | solution.py:20
  366.1 41.0 %while.10 = (s32[]{:T(128)}, f32[3,128,8]{1,2,0:T(8,128)S(1)}, bf16[3,128,1280]{2,1,0:T(8,128)(2,1)S(1)}, bf16[1280,10240]{0,1:T(8,128)(2,1)}, bf16[3,128,1280]{2,1,0:T(8,128)(2,1)S(1)}, /*index=5*/s32[]{:T(128)}) while((s32[]{:T(128)}, f32[3,128,8]{1,2,0:T(8,128)S(1)}, bf16[3,128,1280]{2,1,0:T(8,128)(2,1)S(1)}, ...), condition=%wide.region_2.3_spmd, body=%wide.region_0.2_spmd.sunk | while | flops 3358227456 | bytes 28192848 | solution.py:47
  366.2 13.6 %multiply_reduce_fusion.2 = f32[128,8]{0,1:T(8,128)S(1)} fusion(bf16[8,1280,1280]{2,1,0:T(8,128)(2,1)} %bitcast.43, f32[128,1280]{1,0:T(8,128)S(1)} %bitcast_convert_fusion.2, bf16[3,128,1280]{2,1,0:T(8,128)(2,1)S(1)} %get-tuple-element.88, s32[]{:T(128)} %get-tuple-element.80), kind=kOutput, calls=%fused_computation.clone.1 | convolution fusion | flops 3358063616 | bytes 27201540 | tf_op jit(solution)/shard_map/while/body/eval_jaxpr/dot_general | solution.py:43
  379.8 0.1 bitcast_convert_fusion.2
  379.9 13.6 %multiply_reduce_fusion.2 = f32[128,8]{0,1:T(8,128)S(1)} fusion(bf16[8,1280,1280]{2,1,0:T(8,128)(2,1)} %bitcast.43, f32[128,1280]{1,0:T(8,128)S(1)} %bitcast_convert_fusion.2, bf16[3,128,1280]{2,1,0:T(8,128)(2,1)S(1)} %get-tuple-element.88, s32[]{:T(128)} %get-tuple-element.80), kind=kOutput, calls=%fused_computation.clone.1 | convolution fusion | flops 3358063616 | bytes 27201540 | tf_op jit(solution)/shard_map/while/body/eval_jaxpr/dot_general | solution.py:43
  393.5 0.1 bitcast_convert_fusion.2
  393.5 13.6 %multiply_reduce_fusion.2 = f32[128,8]{0,1:T(8,128)S(1)} fusion(bf16[8,1280,1280]{2,1,0:T(8,128)(2,1)} %bitcast.43, f32[128,1280]{1,0:T(8,128)S(1)} %bitcast_convert_fusion.2, bf16[3,128,1280]{2,1,0:T(8,128)(2,1)S(1)} %get-tuple-element.88, s32[]{:T(128)} %get-tuple-element.80), kind=kOutput, calls=%fused_computation.clone.1 | convolution fusion | flops 3358063616 | bytes 27201540 | tf_op jit(solution)/shard_map/while/body/eval_jaxpr/dot_general | solution.py:43
  407.1 61.1 %all-reduce = f32[384,8]{0,1:T(8,128)S(1)} all-reduce(f32[384,8]{0,1:T(8,128)S(1)} %bitcast.49), channel_id=2, replica_groups=mesh['groups'=2,'panel'=4,'tok'=4] {'panel','tok'}, use_global_device_ids=true, to_apply=%region_3.4.clone | all-reduce | flops 3072 | bytes 24576
  468.2 0.7 constant_dynamic-slice_fusion
  (7 shorter events, 0.1 us)
Async XLA Ops:
  6.5 40.6 %copy-start = (bf16[96,1280]{1,0:T(8,128)(2,1)S(1)}, bf16[96,1280]{1,0:T(8,128)(2,1)}, u32[]{:S(2)}) copy-start(bf16[96,1280]{1,0:T(8,128)(2,1)} %param.9) | copy-start | bytes 737284
  6.5 257.0 %all-gather.5.cloned.1.call-start = ((), (), s32[]{:S(2)}) async-start(), calls=%async_computation.3 | async-start | bytes 16384000 | tf_op jit(solution)/shard_map/all_gather | solution.py:26
  7.3 342.2 %all-gather.3.cloned.1.call-start = ((), (), s32[]{:S(2)}) async-start(), calls=%async_computation.2 | async-start | bytes 16384000 | tf_op jit(solution)/shard_map/all_gather | solution.py:17
  37.4 23.9 %all-to-all-start = ((bf16[4,96,1280]{2,1,0:T(8,128)(2,1)}), bf16[4,96,1280]{2,1,0:T(8,128)(2,1)S(1)}, u32[]{:S(2)}, u32[]{:S(2)}) async-start(bf16[4,96,1280]{2,1,0:T(8,128)(2,1)} %bitcast.6), calls=%async_computation | async-start | bytes 1966080 | tf_op jit(solution)/shard_map/all_to_all | solution.py:13
  61.3 68.4 %all-to-all-start.1 = ((bf16[4,96,1280]{2,1,0:T(8,128)(2,1)}), bf16[4,96,1280]{2,1,0:T(8,128)(2,1)}, u32[]{:S(2)}, u32[]{:S(2)}) async-start(bf16[4,96,1280]{2,1,0:T(8,128)(2,1)} %bitcast.10), calls=%async_computation.1 | async-start | bytes 1966080 | tf_op jit(solution)/shard_map/all_to_all | solution.py:22
  89.0 39.3 %copy-start.1 = (u32[32]{0:T(128)S(1)}, u32[32]{0:T(128)}, u32[]{:S(2)}) copy-start(u32[32]{0:T(128)} %constant.20) | copy-start | bytes 388
Sparse Core Ops, SparseCore 0:
  8.9 254.5 all-gather.4
  265.1 84.3 all-gather.2
where the time goes:
time: 477 us; the launch traced here: 476 us
  waiting for transfers between devices  192 us (40%)
  blocking collectives  135 us (28%)
  matrix products  54.6 us (11%)
  local copies, waits for them, and re-layouts  42 us (9%)
  other arithmetic  27.4 us (6%)
  between operations  14.1 us (3%)
  starting transfers between devices  10.2 us (2%)
    all_gather x1, waiting for transfers between devices, per_device(): lax.all_gather(in_basis, 'tok', axis=0, tiled=True)  133 us
    unnamed x1, blocking collectives  61.1 us
    all_gather x1, waiting for transfers between devices, per_device(): lax.all_gather(out_basis, 'panel', axis=0, tiled=True)  58.5 us
    dot_general x3, matrix products, score_block(): jnp.dot(grad_part, flattened, preferred_element_type=jnp.float32)  40.8 us
    convert_element_type x1, local copies, waits for them, and re-layouts, per_device(): (query_rot.astype(jnp.float32) / shifted[:, None, :]).astype(jnp.bfloat16)  39.3 us
    all_gather x1, blocking collectives, per_device(): grad_all_rows = lax.all_gather(grads, 'tok', axis=0, tiled=True)  29.4 us
    convert_element_type x1, other arithmetic, per_device(): (query_rot.astype(jnp.float32) / shifted[:, None, :]).astype(jnp.bfloat16)  21.1 us
    all_gather x1, blocking collectives, per_device(): act_rot = lax.all_gather(act_local, 'tok', axis=0, tiled=True)  20.6 us
  transfers between devices with their start and end apart: 4, of which 2 were waited for; matrix products, arithmetic and copies ran while one was open for 16% of the time, Pallas kernels for 0%

commit v1 on v0

v1 whole, which is shorter than its diff:
```python
import math

import jax
import jax.numpy as jnp
from jax import lax
from jax.experimental import pallas as pl
from jax.experimental.pallas import tpu as pltpu
from jax.sharding import PartitionSpec as P

DAMPING = 0.1
WIDE = jnp.float32
NARROW = jnp.bfloat16


def swap(value, axis, mask):
    size = lax.axis_size(axis)
    return lax.ppermute(value, axis, [(i, i ^ mask) for i in range(size)])


def gather_panel(acts):
    if lax.axis_size("panel") != 4:
        return lax.all_gather(acts, "panel", axis=0, tiled=True)
    near = swap(acts, "panel", 1)
    far = swap(acts, "panel", 2)
    both = swap(far, "panel", 1)
    place = lax.axis_index("panel")
    blocks = (acts, near, far, both)
    return jnp.concatenate([lax.select_n(place ^ b, *blocks) for b in range(4)], axis=0)


def gather_tok(grads):
    if lax.axis_size("tok") != 4:
        return lax.all_gather(grads, "tok", axis=0, tiled=True)
    up = lax.ppermute(grads, "tok", [(i, (i + 1) % 4) for i in range(4)])
    down = lax.ppermute(grads, "tok", [(i, (i + 3) % 4) for i in range(4)])
    half = grads.shape[0] // 2
    up_far = lax.ppermute(up[:half], "tok", [(i, (i + 1) % 4) for i in range(4)])
    down_far = lax.ppermute(down[half:], "tok", [(i, (i + 3) % 4) for i in range(4)])
    far = jnp.concatenate([up_far, down_far], axis=0)
    place = lax.axis_index("tok")
    blocks = (grads, down, far, up)
    return jnp.concatenate([lax.select_n((b - place + 4) % 4, *blocks) for b in range(4)], axis=0)


def sum_tok(part):
    if lax.axis_size("tok") != 4:
        return lax.psum(part, "tok").astype(NARROW)
    half = part.shape[0] // 2
    outs = []
    for rows, order in ((part[:half], (1, 3)), (part[half:], (3, 1))):
        for mask in order:
            rows = rows + swap(rows.astype(NARROW), "tok", mask).astype(WIDE)
        outs.append(rows.astype(NARROW))
    return jnp.concatenate(outs, axis=0)


def sum_panel(part):
    if lax.axis_size("panel") != 4:
        return lax.psum(part, "panel").astype(NARROW)
    half = part.shape[0] // 2
    core = lax.axis_index("panel") % 2
    top, bottom = part[:half], part[half:]
    first = core == 0
    mine = jnp.where(first, top, bottom)
    other = jnp.where(first, bottom, top).astype(NARROW)
    mine = mine + swap(other, "panel", 1).astype(WIDE)
    mine = mine + swap(mine.astype(NARROW), "panel", 2).astype(WIDE)
    mine = mine.astype(NARROW)
    other = swap(mine, "panel", 1)
    return jnp.concatenate([jnp.where(first, mine, other), jnp.where(first, other, mine)], axis=0)


def precond_kernel(query_ref, eig_ref, out_ref):
    rows, queries, cols = query_ref.shape
    scale = 1.0 / (eig_ref[...] + DAMPING)
    value = query_ref[...].astype(WIDE) * scale[:, None, :]
    out_ref[...] = value.reshape(rows * queries, cols).astype(NARROW)


def precondition(query_rot, eigvals):
    depth, queries, cols = query_rot.shape
    step = math.gcd(depth, 64)
    return pl.pallas_call(
        precond_kernel,
        grid=(depth // step,),
        in_specs=[
            pl.BlockSpec((step, queries, cols), lambda i: (i, 0, 0)),
            pl.BlockSpec((step, cols), lambda i: (i, 0)),
        ],
        out_specs=pl.BlockSpec((step * queries, cols), lambda i: (i, 0)),
        out_shape=jax.ShapeDtypeStruct((depth * queries, cols), NARROW),
        compiler_params=pltpu.CompilerParams(vmem_limit_bytes=40 * 1024 * 1024),
        cost_estimate=pl.CostEstimate(
            flops=2 * depth * queries * cols,
            bytes_accessed=4 * depth * queries * cols + 4 * depth * cols,
            transcendentals=0,
        ),
        name="precondition",
    )(query_rot, eigvals)


def score_kernel(pre_ref, act_ref, grad_ref, out_ref, act_turned, grad_turned):
    step = pl.program_id(0)
    queries, tokens = out_ref.shape
    block = pre_ref.shape[0] // queries

    @pl.when(step == 0)
    def _():
        act_turned[...] = act_ref[...].astype(WIDE).T.astype(NARROW)
        grad_turned[...] = grad_ref[...].astype(WIDE).T
        out_ref[...] = jnp.zeros_like(out_ref)

    mixed = jnp.dot(pre_ref[...], act_turned[...], preferred_element_type=WIDE)
    grad = grad_turned[pl.ds(pl.multiple_of(step * block, block), block), :]
    mixed = mixed.reshape(block, queries, tokens) * grad[:, None, :]
    out_ref[...] += jnp.sum(mixed, axis=0)


def scores(precond, act_rot, grad_rot, queries):
    total, cols = precond.shape
    tokens, depth = grad_rot.shape
    step = math.gcd(depth, 64)
    return pl.pallas_call(
        score_kernel,
        grid=(depth // step,),
        in_specs=[
            pl.BlockSpec((step * queries, cols), lambda i: (i, 0)),
            pl.BlockSpec((tokens, cols), lambda i: (0, 0)),
            pl.BlockSpec((tokens, depth), lambda i: (0, 0)),
        ],
        out_specs=pl.BlockSpec((queries, tokens), lambda i: (0, 0)),
        out_shape=jax.ShapeDtypeStruct((queries, tokens), WIDE),
        scratch_shapes=[pltpu.VMEM((cols, tokens), NARROW), pltpu.VMEM((depth, tokens), WIDE)],
        compiler_params=pltpu.CompilerParams(vmem_limit_bytes=40 * 1024 * 1024),
        cost_estimate=pl.CostEstimate(
            flops=2 * total * cols * tokens, bytes_accessed=2 * total * cols, transcendentals=0
        ),
        name="scores",
    )(precond, act_rot, grad_rot)


def per_device(grads, acts, out_basis, in_basis, query_rot, eigvals):
    acts_all = gather_panel(acts)
    grads_all = gather_tok(grads)
    precond = precondition(query_rot, eigvals)
    act_part = jnp.dot(acts_all, in_basis, preferred_element_type=WIDE)
    grad_part = jnp.dot(grads_all, out_basis, preferred_element_type=WIDE)
    act_rot = sum_tok(act_part)
    grad_rot = sum_panel(grad_part)
    queries = query_rot.shape[1]
    partial = scores(precond, act_rot, grad_rot, queries)
    owners = lax.axis_size("panel") * lax.axis_size("tok")
    tokens = partial.shape[1]
    split = partial.reshape(queries, owners, tokens // owners).transpose(1, 0, 2)
    got = lax.all_to_all(split, ("panel", "tok"), split_axis=0, concat_axis=0, tiled=True)
    return jnp.sum(got, axis=0).T


def solution(mesh):
    placed = (
        P(("groups", "tok"), "panel"),
        P(("groups", "panel"), "tok"),
        P("panel", "tok"),
        P("tok", "panel"),
        P("tok", None, "panel"),
        P("tok", "panel"),
    )
    return jax.shard_map(
        per_device,
        mesh=mesh,
        in_specs=placed,
        out_specs=P(("groups", "panel", "tok"), None),
        check_vma=False,
    )
```

time: 477 us -> 147 us (0.31)
  waiting for transfers between devices: 192 us -> 48.1 us
  blocking collectives: 135 us -> 10.7 us
  matrix products: 54.6 us -> 2.88 us
  Pallas kernels: 0 us -> 51.6 us
  local copies, waits for them, and re-layouts: 42 us -> 6.91 us
  other arithmetic: 27.4 us -> 4.8 us
  between operations: 14.1 us -> 0.23 us
  starting transfers between devices: 10.2 us -> 20.9 us
    all_gather x2 -> x0, waiting for transfers between devices: 191 us -> none  [the longest x1 133 us: per_device(): lax.all_gather(in_basis, 'tok', axis=0, tiled=True)]
    all_gather x4 -> x0, blocking collectives: 73.8 us -> none  [the longest x1 29.4 us: per_device(): grad_all_rows = lax.all_gather(grads, 'tok', axis=0, tiled=True)]
    unnamed x1 -> x0, blocking collectives: 61.1 us -> none
    dot_general x5 -> x2, matrix products: 54.6 us -> 2.88 us  [the longest x1 1.44 us: per_device(): grad_part = jnp.dot(grads_all, out_basis, preferred_element_type=WIDE)]
    pallas_call x0 -> x2, Pallas kernels: none -> 51.6 us  [the longest x1 27.6 us: precondition(): pl.pallas_call(precond_kernel, grid=(depth // step,), in_specs=[pl.BlockS...]
    ppermute x0 -> x14, waiting for transfers between devices: none -> 48.1 us  [the longest x10 40.5 us: swap(): return lax.ppermute(value, axis, [(i, i ^ mask) for i in range(size)])]
    convert_element_type x1 -> x0, local copies, waits for them, and re-layouts: 39.3 us -> none  [per_device(): (query_rot.astype(jnp.float32) / shifted[:, None, :]).astype(jnp.bfloat16)]
    ppermute x0 -> x14, starting transfers between devices: none -> 20.9 us  [the longest x10 10.5 us: swap(): return lax.ppermute(value, axis, [(i, i ^ mask) for i in range(size)])]
  transfers between devices with their start and end apart: 4 -> 14, of which waited for: 2 -> 6; matrix products, arithmetic and copies ran while one was open for 16% -> 6% of each run, Pallas kernels for 0% -> 19%
where the time goes in v1:
time: 147 us; the launch traced here: 146 us
  Pallas kernels  51.6 us (35%)
  waiting for transfers between devices  48.1 us (33%)
  starting transfers between devices  20.9 us (14%)
  blocking collectives  10.7 us (7%)
  local copies, waits for them, and re-layouts  6.91 us (5%)
  other arithmetic  4.8 us (3%)
  matrix products  2.88 us (2%)
    ppermute x10, waiting for transfers between devices, swap(): return lax.ppermute(value, axis, [(i, i ^ mask) for i in range(size)])  40.5 us
    pallas_call x1, Pallas kernels, precondition(): pl.pallas_call(precond_kernel, grid=(depth // step,), in_specs=[pl.BlockS...  27.6 us
    pallas_call x1, Pallas kernels, scores(): pl.pallas_call(score_kernel, grid=(depth // step,), in_specs=[pl.BlockSpe...  24 us
    all_to_all x1, blocking collectives, per_device(): lax.all_to_all(split, ('panel', 'tok'), split_axis=0, concat_axis=0, tile...  10.7 us
    ppermute x10, starting transfers between devices, swap(): return lax.ppermute(value, axis, [(i, i ^ mask) for i in range(size)])  10.5 us
    ppermute x1, waiting for transfers between devices, gather_tok(): up = lax.ppermute(grads, 'tok', [(i, (i + 1) % 4) for i in range(4)])  5.32 us
    ppermute x1, starting transfers between devices, gather_tok(): lax.ppermute(down[half:], 'tok', [(i, (i + 3) % 4) for i in range(4)])  5.22 us
    unnamed x15, local copies, waits for them, and re-layouts  4.59 us
  transfers between devices with their start and end apart: 14, of which 6 were waited for; matrix products, arithmetic and copies ran while one was open for 6% of the time, Pallas kernels for 19%

profile of v1, /device:TPU:0, one launch (start us, length us, event | category | flops | bytes accessed | tf_op | source)
XLA Modules:
  0.0 146.1 jit_solution(4288330177170310239)
XLA Ops:
  0.0 3.0 %collective-permute-start.8 = (bf16[96,1280]{1,0:T(8,128)(2,1)}, bf16[96,1280]{1,0:T(8,128)(2,1)S(1)}, u32[]{:S(2)}, u32[]{:S(2)}) collective-permute-start(bf16[96,1280]{1,0:T(8,128)(2,1)} %param.6), channel_id=1, source_target_pairs={{0,1},{1,2},{2,3},{3,0},{4,5},{5,6},{6,7},{7,4},{8,9},{9,10},{10,1... | collective-permute-start | bytes 737288 | tf_op jit(solution)/shard_map/ppermute | solution.py:34
  3.0 2.1 %collective-permute-start.7 = (bf16[96,1280]{1,0:T(8,128)(2,1)}, bf16[96,1280]{1,0:T(8,128)(2,1)}, u32[]{:S(2)}, u32[]{:S(2)}) collective-permute-start(bf16[96,1280]{1,0:T(8,128)(2,1)} %param.6), channel_id=1, source_target_pairs={{0,3},{1,0},{2,1},{3,2},{4,7},{5,4},{6,5},{7,6},{8,11},{9,8},{10,9... | collective-permute-start | bytes 737288 | tf_op jit(solution)/shard_map/ppermute | solution.py:35
  5.1 1.7 %collective-permute-start.1 = (bf16[96,1280]{1,0:T(8,128)(2,1)}, bf16[96,1280]{1,0:T(8,128)(2,1)}, u32[]{:S(2)}, u32[]{:S(2)}) collective-permute-start(bf16[96,1280]{1,0:T(8,128)(2,1)} %param.7), channel_id=1, source_target_pairs={{0,8},{4,12},{8,0},{12,4},{1,9},{5,13},{9,1},{13,5},{2,10},{6,14},... | collective-permute-start | bytes 737288 | tf_op jit(solution)/shard_map/ppermute | solution.py:17
  6.8 5.3 %collective-permute-done.8 = bf16[96,1280]{1,0:T(8,128)(2,1)S(1)} collective-permute-done((bf16[96,1280]{1,0:T(8,128)(2,1)}, bf16[96,1280]{1,0:T(8,128)(2,1)S(1)}, u32[]{:S(2)}, u32[]{:S(2)}) %collective-permute-start.8) | collective-permute-done | bytes 245792 | tf_op jit(solution)/shard_map/ppermute | solution.py:34
  12.1 0.7 slice.26
  12.8 2.9 %copy-done.2 = f32[1280,1280]{1,0:T(8,128)S(1)} copy-done((f32[1280,1280]{1,0:T(8,128)S(1)}, f32[1280,1280]{1,0:T(8,128)}, u32[]{:S(2)}) %copy-start.2) | copy-done | bytes 6553624
  15.6 27.6 %precondition.1.pre_ref = bf16[10240,1280]{1,0:T(8,128)(2,1)} custom-call(bf16[1280,8,1280]{2,1,0:T(8,128)(2,1)} %query_ref.1, f32[1280,1280]{1,0:T(8,128)S(1)} %copy-done.2), custom_call_target="tpu_custom_call" | custom-call | flops 26214400 | bytes 58982400 | tf_op jit(solution)/shard_map/precondition/pallas_call | solution.py:83
  43.3 0.9 slice.27
  44.2 5.2 %collective-permute-start.10 = (bf16[48,1280]{1,0:T(8,128)(2,1)S(1)}, bf16[48,1280]{1,0:T(8,128)(2,1)S(1)}, u32[]{:S(2)}, u32[]{:S(2)}) collective-permute-start(bf16[48,1280]{1,0:T(8,128)(2,1)S(1)} %slice.27), channel_id=1, source_target_pairs={{0,3},{1,0},{2,1},{3,2},{4,7},{5,4},{6,5},{7,6},{8,11},{9,8},{10,9... | collective-permute-start | bytes 368648 | tf_op jit(solution)/shard_map/ppermute | solution.py:38
  49.4 0.2 collective-permute-start.2
  49.6 0.9 constant_dynamic-update-slice_fusion.1
  50.6 2.3 %collective-permute-done.10 = bf16[48,1280]{1,0:T(8,128)(2,1)S(1)} collective-permute-done((bf16[48,1280]{1,0:T(8,128)(2,1)S(1)}, bf16[48,1280]{1,0:T(8,128)(2,1)S(1)}, u32[]{:S(2)}, u32[]{:S(2)}) %collective-permute-start.10) | collective-permute-done | bytes 122912 | tf_op jit(solution)/shard_map/ppermute | solution.py:38
  52.8 1.1 select_select_fusion.3
  53.9 1.4 fusion.8
  55.6 1.3 select_select_fusion.7
  56.9 0.6 copy-done.5
  57.5 1.4 fusion
  59.1 1.8 %collective-permute-start.3 = (bf16[192,1280]{1,0:T(8,128)(2,1)S(1)}, bf16[192,1280]{1,0:T(8,128)(2,1)S(1)}, u32[]{:S(2)}, u32[]{:S(2)}) collective-permute-start(bf16[192,1280]{1,0:T(8,128)(2,1)S(1)} %get-tuple-element.9), channel_id=1, source_target_pairs={{0,1},{1,0},{2,3},{3,2},{4,5},{5,4},{6,7},{7,6},{8,9},{9,8},{10,11... | collective-permute-start | bytes 1474568 | tf_op jit(solution)/shard_map/ppermute | solution.py:17
  60.9 2.6 %collective-permute-start.5 = (bf16[192,1280]{1,0:T(8,128)(2,1)S(1)}, bf16[192,1280]{1,0:T(8,128)(2,1)S(1)}, u32[]{:S(2)}, u32[]{:S(2)}) collective-permute-start(bf16[192,1280]{1,0:T(8,128)(2,1)S(1)} %get-tuple-element.10), channel_id=1, source_target_pairs={{0,3},{1,2},{2,1},{3,0},{4,7},{5,6},{6,5},{7,4},{8,11},{9,10},{10,... | collective-permute-start | bytes 1474568 | tf_op jit(solution)/shard_map/ppermute | solution.py:17
  63.6 1.6 %collective-permute-start.12 = (bf16[192,1280]{1,0:T(8,128)(2,1)S(1)}, bf16[192,1280]{1,0:T(8,128)(2,1)S(1)}, u32[]{:S(2)}, u32[]{:S(2)}) collective-permute-start(bf16[192,1280]{1,0:T(8,128)(2,1)S(1)} %fusion.18), channel_id=1, source_target_pairs={{0,8},{4,12},{8,0},{12,4},{1,9},{5,13},{9,1},{13,5},{2,10},{6,14},... | collective-permute-start | bytes 1474568 | tf_op jit(solution)/shard_map/ppermute | solution.py:17
  65.2 7.3 %collective-permute-done.3 = bf16[192,1280]{1,0:T(8,128)(2,1)S(1)} collective-permute-done((bf16[192,1280]{1,0:T(8,128)(2,1)S(1)}, bf16[192,1280]{1,0:T(8,128)(2,1)S(1)}, u32[]{:S(2)}, u32[]{:S(2)}) %collective-permute-start.3) | collective-permute-done | bytes 491552 | tf_op jit(solution)/shard_map/ppermute | solution.py:17
  72.5 12.5 %collective-permute-done.5 = bf16[192,1280]{1,0:T(8,128)(2,1)S(1)} collective-permute-done((bf16[192,1280]{1,0:T(8,128)(2,1)S(1)}, bf16[192,1280]{1,0:T(8,128)(2,1)S(1)}, u32[]{:S(2)}, u32[]{:S(2)}) %collective-permute-start.5) | collective-permute-done | bytes 491552 | tf_op jit(solution)/shard_map/ppermute | solution.py:17
  85.3 1.7 %collective-permute-start.4 = (bf16[192,1280]{1,0:T(8,128)(2,1)S(1)}, bf16[192,1280]{1,0:T(8,128)(2,1)S(1)}, u32[]{:S(2)}, u32[]{:S(2)}) collective-permute-start(bf16[192,1280]{1,0:T(8,128)(2,1)S(1)} %get-tuple-element.7), channel_id=1, source_target_pairs={{0,3},{1,2},{2,1},{3,0},{4,7},{5,6},{6,5},{7,4},{8,11},{9,10},{10,... | collective-permute-start | bytes 1474568 | tf_op jit(solution)/shard_map/ppermute | solution.py:17
  87.0 0.8 collective-permute-start.6
  88.1 13.2 %collective-permute-done.4 = bf16[192,1280]{1,0:T(8,128)(2,1)S(1)} collective-permute-done((bf16[192,1280]{1,0:T(8,128)(2,1)S(1)}, bf16[192,1280]{1,0:T(8,128)(2,1)S(1)}, u32[]{:S(2)}, u32[]{:S(2)}) %collective-permute-start.4) | collective-permute-done | bytes 491552 | tf_op jit(solution)/shard_map/ppermute | solution.py:17
  101.3 7.4 %collective-permute-done.6 = bf16[192,1280]{1,0:T(8,128)(2,1)S(1)} collective-permute-done((bf16[192,1280]{1,0:T(8,128)(2,1)S(1)}, bf16[192,1280]{1,0:T(8,128)(2,1)S(1)}, u32[]{:S(2)}, u32[]{:S(2)}) %collective-permute-start.6) | collective-permute-done | bytes 491552 | tf_op jit(solution)/shard_map/ppermute | solution.py:17
  108.7 0.3 add_convert_fusion.2
  109.2 24.0 %scores.1 = f32[8,384]{1,0:T(8,128)S(1)} custom-call(bf16[10240,1280]{1,0:T(8,128)(2,1)} %precondition.1.pre_ref, bf16[384,1280]{1,0:T(8,128)(2,1)S(1)} %get-tuple-element.21.act_ref, bf16[384,1280]{1,0:T(8,128)(2,1)S(1)} %get-tuple-element.22.grad_ref), custom_call_target="tpu_custom_call" | custom-call | flops 10066329600 | bytes 26214400 | tf_op jit(solution)/shard_map/scores/pallas_call | solution.py:123
  133.4 10.7 %all_to_all.5 = f32[16,1,192]{2,1,0:T(1,128)S(1)} all-to-all(f32[16,1,192]{2,1,0:T(1,128)S(1)} %reshape.4), channel_id=1, replica_groups=mesh['groups'=2,'panel'=4,'tok'=4] {'panel','tok'}, dimensions={0} | all-to-all | bytes 24576 | tf_op jit(solution)/shard_map/all_to_all | solution.py:155
  144.1 0.5 broadcast.5
  144.7 0.7 reduce
  145.4 0.6 reduce_sum.9
  (34 shorter events, 1.4 us)
Async XLA Ops:
  0.0 53.9 %copy-start = (bf16[1280,1280]{1,0:T(8,128)(2,1)S(1)}, bf16[1280,1280]{1,0:T(8,128)(2,1)}, u32[]{:S(2)}) copy-start(bf16[1280,1280]{1,0:T(8,128)(2,1)} %param.8) | copy-start | bytes 9830404
  0.0 12.1 %collective-permute-start.8 = (bf16[96,1280]{1,0:T(8,128)(2,1)}, bf16[96,1280]{1,0:T(8,128)(2,1)S(1)}, u32[]{:S(2)}, u32[]{:S(2)}) collective-permute-start(bf16[96,1280]{1,0:T(8,128)(2,1)} %param.6), channel_id=1, source_target_pairs={{0,1},{1,2},{2,3},{3,0},{4,5},{5,6},{6,7},{7,4},{8,9},{9,10},{10,1... | collective-permute-start | bytes 737288 | tf_op jit(solution)/shard_map/ppermute | solution.py:34
  3.0 40.3 %collective-permute-start.7 = (bf16[96,1280]{1,0:T(8,128)(2,1)}, bf16[96,1280]{1,0:T(8,128)(2,1)}, u32[]{:S(2)}, u32[]{:S(2)}) collective-permute-start(bf16[96,1280]{1,0:T(8,128)(2,1)} %param.6), channel_id=1, source_target_pairs={{0,3},{1,0},{2,1},{3,2},{4,7},{5,4},{6,5},{7,6},{8,11},{9,8},{10,9... | collective-permute-start | bytes 737288 | tf_op jit(solution)/shard_map/ppermute | solution.py:35
  5.1 44.3 %collective-permute-start.1 = (bf16[96,1280]{1,0:T(8,128)(2,1)}, bf16[96,1280]{1,0:T(8,128)(2,1)}, u32[]{:S(2)}, u32[]{:S(2)}) collective-permute-start(bf16[96,1280]{1,0:T(8,128)(2,1)} %param.7), channel_id=1, source_target_pairs={{0,8},{4,12},{8,0},{12,4},{1,9},{5,13},{9,1},{13,5},{2,10},{6,14},... | collective-permute-start | bytes 737288 | tf_op jit(solution)/shard_map/ppermute | solution.py:17
  12.8 36.9 %collective-permute-start.9 = (bf16[48,1280]{1,0:T(8,128)(2,1)}, bf16[48,1280]{1,0:T(8,128)(2,1)}, u32[]{:S(2)}, u32[]{:S(2)}) collective-permute-start(bf16[48,1280]{1,0:T(8,128)(2,1)} %slice.26), channel_id=1, source_target_pairs={{0,1},{1,2},{2,3},{3,0},{4,5},{5,6},{6,7},{7,4},{8,9},{9,10},{10,1... | collective-permute-start | bytes 368648 | tf_op jit(solution)/shard_map/ppermute | solution.py:37
  12.8 42.8 %collective-permute-start = (bf16[96,1280]{1,0:T(8,128)(2,1)}, bf16[96,1280]{1,0:T(8,128)(2,1)}, u32[]{:S(2)}, u32[]{:S(2)}) collective-permute-start(bf16[96,1280]{1,0:T(8,128)(2,1)} %param.7), channel_id=1, source_target_pairs={{0,4},{4,0},{8,12},{12,8},{1,5},{5,1},{9,13},{13,9},{2,6},{6,2},{1... | collective-permute-start | bytes 737288 | tf_op jit(solution)/shard_map/ppermute | solution.py:17
  12.8 2.9 %copy-start.2 = (f32[1280,1280]{1,0:T(8,128)S(1)}, f32[1280,1280]{1,0:T(8,128)}, u32[]{:S(2)}) copy-start(f32[1280,1280]{1,0:T(8,128)} %eig_ref.1) | copy-start | bytes 19660804
  15.6 37.2 %copy-start.3 = (bf16[96,1280]{1,0:T(8,128)(2,1)S(1)}, bf16[96,1280]{1,0:T(8,128)(2,1)}, u32[]{:S(2)}) copy-start(bf16[96,1280]{1,0:T(8,128)(2,1)} %param.6) | copy-start | bytes 737284
  44.2 8.6 %collective-permute-start.10 = (bf16[48,1280]{1,0:T(8,128)(2,1)S(1)}, bf16[48,1280]{1,0:T(8,128)(2,1)S(1)}, u32[]{:S(2)}, u32[]{:S(2)}) collective-permute-start(bf16[48,1280]{1,0:T(8,128)(2,1)S(1)} %slice.27), channel_id=1, source_target_pairs={{0,3},{1,0},{2,1},{3,2},{4,7},{5,4},{6,5},{7,6},{8,11},{9,8},{10,9... | collective-permute-start | bytes 368648 | tf_op jit(solution)/shard_map/ppermute | solution.py:38
  49.4 6.2 %collective-permute-start.2 = (bf16[96,1280]{1,0:T(8,128)(2,1)}, bf16[96,1280]{1,0:T(8,128)(2,1)S(1)}, u32[]{:S(2)}, u32[]{:S(2)}) collective-permute-start(bf16[96,1280]{1,0:T(8,128)(2,1)} %collective-permute-done.1), channel_id=1, source_target_pairs={{0,4},{4,0},{8,12},{12,8},{1,5},{5,1},{9,13},{13,9},{2,6},{6,2},{1... | collective-permute-start | bytes 737288 | tf_op jit(solution)/shard_map/ppermute | solution.py:17
  53.9 1.7 %copy-start.4 = (bf16[96,1280]{1,0:T(8,128)(2,1)S(1)}, bf16[96,1280]{1,0:T(8,128)(2,1)}, u32[]{:S(2)}) copy-start(bf16[96,1280]{1,0:T(8,128)(2,1)} %param.7) | copy-start | bytes 737284
  55.4 2.2 %copy-start.5 = (bf16[1280,1280]{1,0:T(8,128)(2,1)S(1)}, bf16[1280,1280]{1,0:T(8,128)(2,1)}, u32[]{:S(2)}) copy-start(bf16[1280,1280]{1,0:T(8,128)(2,1)} %param.9) | copy-start | bytes 9830404
  55.5 8.0 %collective-permute-start.11 = (bf16[192,1280]{1,0:T(8,128)(2,1)S(1)}, bf16[192,1280]{1,0:T(8,128)(2,1)S(1)}, u32[]{:S(2)}, u32[]{:S(2)}) collective-permute-start(bf16[192,1280]{1,0:T(8,128)(2,1)S(1)} %select_convert_fusion), channel_id=1, source_target_pairs={{0,4},{4,0},{8,12},{12,8},{1,5},{5,1},{9,13},{13,9},{2,6},{6,2},{1... | collective-permute-start | bytes 1474568 | tf_op jit(solution)/shard_map/ppermute | solution.py:17
  59.1 13.5 %collective-permute-start.3 = (bf16[192,1280]{1,0:T(8,128)(2,1)S(1)}, bf16[192,1280]{1,0:T(8,128)(2,1)S(1)}, u32[]{:S(2)}, u32[]{:S(2)}) collective-permute-start(bf16[192,1280]{1,0:T(8,128)(2,1)S(1)} %get-tuple-element.9), channel_id=1, source_target_pairs={{0,1},{1,0},{2,3},{3,2},{4,5},{5,4},{6,7},{7,6},{8,9},{9,8},{10,11... | collective-permute-start | bytes 1474568 | tf_op jit(solution)/shard_map/ppermute | solution.py:17
  60.9 24.2 %collective-permute-start.5 = (bf16[192,1280]{1,0:T(8,128)(2,1)S(1)}, bf16[192,1280]{1,0:T(8,128)(2,1)S(1)}, u32[]{:S(2)}, u32[]{:S(2)}) collective-permute-start(bf16[192,1280]{1,0:T(8,128)(2,1)S(1)} %get-tuple-element.10), channel_id=1, source_target_pairs={{0,3},{1,2},{2,1},{3,0},{4,7},{5,6},{6,5},{7,4},{8,11},{9,10},{10,... | collective-permute-start | bytes 1474568 | tf_op jit(solution)/shard_map/ppermute | solution.py:17
  63.6 24.2 %collective-permute-start.12 = (bf16[192,1280]{1,0:T(8,128)(2,1)S(1)}, bf16[192,1280]{1,0:T(8,128)(2,1)S(1)}, u32[]{:S(2)}, u32[]{:S(2)}) collective-permute-start(bf16[192,1280]{1,0:T(8,128)(2,1)S(1)} %fusion.18), channel_id=1, source_target_pairs={{0,8},{4,12},{8,0},{12,4},{1,9},{5,13},{9,1},{13,5},{2,10},{6,14},... | collective-permute-start | bytes 1474568 | tf_op jit(solution)/shard_map/ppermute | solution.py:17
  85.3 16.0 %collective-permute-start.4 = (bf16[192,1280]{1,0:T(8,128)(2,1)S(1)}, bf16[192,1280]{1,0:T(8,128)(2,1)S(1)}, u32[]{:S(2)}, u32[]{:S(2)}) collective-permute-start(bf16[192,1280]{1,0:T(8,128)(2,1)S(1)} %get-tuple-element.7), channel_id=1, source_target_pairs={{0,3},{1,2},{2,1},{3,0},{4,7},{5,6},{6,5},{7,4},{8,11},{9,10},{10,... | collective-permute-start | bytes 1474568 | tf_op jit(solution)/shard_map/ppermute | solution.py:17
  87.0 21.7 %collective-permute-start.6 = (bf16[192,1280]{1,0:T(8,128)(2,1)S(1)}, bf16[192,1280]{1,0:T(8,128)(2,1)S(1)}, u32[]{:S(2)}, u32[]{:S(2)}) collective-permute-start(bf16[192,1280]{1,0:T(8,128)(2,1)S(1)} %get-tuple-element.8), channel_id=1, source_target_pairs={{0,1},{1,0},{2,3},{3,2},{4,5},{5,4},{6,7},{7,6},{8,9},{9,8},{10,11... | collective-permute-start | bytes 1474568 | tf_op jit(solution)/shard_map/ppermute | solution.py:17
  88.0 21.0 %collective-permute-start.13 = (bf16[192,1280]{1,0:T(8,128)(2,1)S(1)}, bf16[192,1280]{1,0:T(8,128)(2,1)S(1)}, u32[]{:S(2)}, u32[]{:S(2)}) collective-permute-start(bf16[192,1280]{1,0:T(8,128)(2,1)S(1)} %add_convert_fusion), channel_id=1, source_target_pairs={{0,4},{4,0},{8,12},{12,8},{1,5},{5,1},{9,13},{13,9},{2,6},{6,2},{1... | collective-permute-start | bytes 1474568 | tf_op jit(solution)/shard_map/ppermute | solution.py:17
  109.2 36.8 %copy-start.1 = (bf16[1280,1280]{1,0:T(8,128)(2,1)S(1)}, bf16[1280,1280]{1,0:T(8,128)(2,1)}, u32[]{:S(2)}) copy-start(bf16[1280,1280]{1,0:T(8,128)(2,1)} %param.8) | copy-start | bytes 9830404

commit v2 on v0

v2 whole, which is shorter than its diff:
```python
import functools
import math

import jax
import jax.numpy as jnp
from jax import lax
from jax.experimental import pallas as pl
from jax.experimental.pallas import tpu as pltpu
from jax.sharding import PartitionSpec as P

DAMPING = 0.1
WIDE = jnp.float32
NARROW = jnp.bfloat16
ROOM = 48 * 1024 * 1024


def swap(value, axis, mask):
    return lax.ppermute(value, axis, [(i, i ^ mask) for i in range(lax.axis_size(axis))])


def dot(a, b):
    return jnp.dot(a, b, preferred_element_type=WIDE)


def chain_sum(part):
    into = lax.ppermute(part.astype(NARROW), "tok", [(0, 1), (3, 2)])
    half = part + into.astype(WIDE)
    across = lax.ppermute(half.astype(NARROW), "tok", [(1, 2), (2, 1)])
    total = (half + across.astype(WIDE)).astype(NARROW)
    back = lax.ppermute(total, "tok", [(1, 0), (2, 3)])
    return total, back


def rotate_kernel(place_ref, b0, b1, b2, b3, basis_ref, mine_ref, other_ref, rows_ref):
    size = b0.shape[0]
    half = mine_ref.shape[0]
    for k, block in enumerate((b0, b1, b2, b3)):
        rows_ref[pl.ds(pl.multiple_of(place_ref[k] * size, size), size), :] = block[...]
    core = place_ref[4]
    mine = rows_ref[pl.ds(pl.multiple_of(core * half, half), half), :]
    other = rows_ref[pl.ds(pl.multiple_of((1 - core) * half, half), half), :]
    other_ref[...] = dot(other, basis_ref[...]).astype(NARROW)
    mine_ref[...] = dot(mine, basis_ref[...])


def rotate(places, blocks, basis):
    size, depth = blocks[0].shape
    width = basis.shape[1]
    whole = pl.BlockSpec(memory_space=pltpu.VMEM)
    return pl.pallas_call(
        rotate_kernel,
        in_specs=[pl.BlockSpec(memory_space=pltpu.SMEM)] + [whole] * 5,
        out_specs=[whole, whole],
        out_shape=[
            jax.ShapeDtypeStruct((2 * size, width), WIDE),
            jax.ShapeDtypeStruct((2 * size, width), NARROW),
        ],
        scratch_shapes=[pltpu.VMEM((4 * size, depth), NARROW)],
        compiler_params=pltpu.CompilerParams(vmem_limit_bytes=ROOM),
        cost_estimate=pl.CostEstimate(
            flops=8 * size * depth * width, bytes_accessed=2 * depth * width, transcendentals=0
        ),
        name="rotate",
    )(places, *blocks, basis)


def sum_panel(mine, other):
    mine = mine + swap(other, "panel", 1).astype(WIDE)
    mine = (mine + swap(mine.astype(NARROW), "panel", 2).astype(WIDE)).astype(NARROW)
    return mine, swap(mine, "panel", 1)


def score_kernel(chunks, spot_ref, query_ref, eig_ref, *refs):
    act_refs, (grad_mine, grad_other), (out_ref, act_rows, act_turned, grad_rows, grad_turned) = (
        refs[: 2 * chunks],
        refs[2 * chunks : 2 * chunks + 2],
        refs[2 * chunks + 2 :],
    )
    step = pl.program_id(0)
    block, queries, cols = query_ref.shape
    tokens = out_ref.shape[1]
    piece = math.gcd(block, 32)

    @pl.when(step == 0)
    def _():
        for k in range(chunks):
            size = act_refs[k].shape[0]
            rows = pl.ds(pl.multiple_of(spot_ref[k] * size, size), size)

            @pl.when(spot_ref[chunks] == 1)
            def _():
                act_rows[rows, :] = act_refs[k][...].astype(WIDE)

            @pl.when(spot_ref[chunks] == 0)
            def _():
                act_rows[rows, :] = act_refs[chunks + k][...].astype(WIDE)

        act_turned[...] = act_rows[...].T.astype(NARROW)
        half = grad_mine.shape[0]
        core = spot_ref[chunks + 1]
        grad_rows[pl.ds(pl.multiple_of(core * half, half), half), :] = grad_mine[...].astype(WIDE)
        grad_rows[pl.ds(pl.multiple_of((1 - core) * half, half), half), :] = grad_other[...].astype(WIDE)
        grad_turned[...] = grad_rows[...].T
        out_ref[...] = jnp.zeros_like(out_ref)

    total = out_ref[...]
    for k in range(block // piece):
        scale = 1.0 / (eig_ref[k * piece : (k + 1) * piece, :] + DAMPING)
        query = query_ref[k * piece : (k + 1) * piece].astype(WIDE) * scale[:, None, :]
        precond = query.reshape(piece * queries, cols).astype(NARROW)
        mixed = dot(precond, act_turned[...]).reshape(piece, queries, tokens)
        grad = grad_turned[pl.ds(pl.multiple_of(step * block + k * piece, piece), piece), :]
        total = total + jnp.sum(mixed * grad[:, None, :], axis=0)
    out_ref[...] = total


def scores(spots, acts, grads, query_rot, eigvals):
    depth, queries, cols = query_rot.shape
    chunks = len(acts) // 2
    tokens = chunks * acts[0].shape[0]
    step = math.gcd(depth, 256)
    whole = pl.BlockSpec(memory_space=pltpu.VMEM)
    return pl.pallas_call(
        functools.partial(score_kernel, chunks),
        grid=(depth // step,),
        in_specs=[
            pl.BlockSpec(memory_space=pltpu.SMEM),
            pl.BlockSpec((step, queries, cols), lambda i: (i, 0, 0)),
            pl.BlockSpec((step, cols), lambda i: (i, 0)),
        ]
        + [whole] * (len(acts) + 2),
        out_specs=pl.BlockSpec((queries, tokens), lambda i: (0, 0)),
        out_shape=jax.ShapeDtypeStruct((queries, tokens), WIDE),
        scratch_shapes=[
            pltpu.VMEM((tokens, cols), WIDE),
            pltpu.VMEM((cols, tokens), NARROW),
            pltpu.VMEM((tokens, depth), WIDE),
            pltpu.VMEM((depth, tokens), WIDE),
        ],
        compiler_params=pltpu.CompilerParams(vmem_limit_bytes=ROOM),
        cost_estimate=pl.CostEstimate(
            flops=2 * depth * queries * cols * tokens,
            bytes_accessed=2 * depth * queries * cols + 4 * depth * cols,
            transcendentals=0,
        ),
        name="scores",
    )(spots, query_rot, eigvals, *acts, *grads)


def on_lines_of_four(grads, acts, out_basis, in_basis):
    panel, tok = lax.axis_index("panel"), lax.axis_index("tok")
    near = swap(acts, "panel", 1)
    far = swap(acts, "panel", 2)
    grad_blocks = [grads] + [swap(grads, "tok", mask) for mask in (1, 3, 2)]
    act_chunks = [acts, near, far, swap(far, "panel", 1)]
    sums = [chain_sum(dot(chunk, in_basis)) for chunk in act_chunks]
    act_rot = [total for total, _ in sums] + [back for _, back in sums]
    places = jnp.stack([tok, tok ^ 1, tok ^ 3, tok ^ 2, panel % 2]).astype(jnp.int32)
    grad_rot = sum_panel(*rotate(places, grad_blocks, out_basis))
    middle = ((tok == 1) | (tok == 2)).astype(jnp.int32)
    spots = jnp.stack([panel, panel ^ 1, panel ^ 2, panel ^ 3, middle, panel % 2]).astype(jnp.int32)
    return spots, act_rot, grad_rot


def on_any(grads, acts, out_basis, in_basis):
    acts_all = lax.all_gather(acts, "panel", axis=0, tiled=True)
    grads_all = lax.all_gather(grads, "tok", axis=0, tiled=True)
    act_rot = lax.psum(dot(acts_all, in_basis), "tok").astype(NARROW)
    grad_rot = lax.psum(dot(grads_all, out_basis), "panel").astype(NARROW)
    half = grad_rot.shape[0] // 2
    spots = jnp.array([0, 1, 0], jnp.int32)
    return spots, [act_rot, act_rot], (grad_rot[:half], grad_rot[half:])


def per_device(grads, acts, out_basis, in_basis, query_rot, eigvals):
    small = lax.axis_size("panel") == 4 and lax.axis_size("tok") == 4
    rotated = on_lines_of_four if small else on_any
    spots, act_rot, grad_rot = rotated(grads, acts, out_basis, in_basis)
    partial = scores(spots, act_rot, grad_rot, query_rot, eigvals)
    queries, tokens = partial.shape
    owners = lax.axis_size("panel") * lax.axis_size("tok")
    split = partial.reshape(queries, owners, tokens // owners).transpose(1, 0, 2)
    got = lax.all_to_all(split, ("panel", "tok"), split_axis=0, concat_axis=0, tiled=True)
    return jnp.sum(got, axis=0).T


def solution(mesh):
    placed = (
        P(("groups", "tok"), "panel"),
        P(("groups", "panel"), "tok"),
        P("panel", "tok"),
        P("tok", "panel"),
        P("tok", None, "panel"),
        P("tok", "panel"),
    )
    return jax.shard_map(
        per_device,
        mesh=mesh,
        in_specs=placed,
        out_specs=P(("groups", "panel", "tok"), None),
        check_vma=False,
    )
```

time: 477 us -> 110 us (0.23)
  waiting for transfers between devices: 192 us -> 36 us
  blocking collectives: 135 us -> 9.73 us
  matrix products: 54.6 us -> 6.43 us
  local copies, waits for them, and re-layouts: 42 us -> 2.91 us
  other arithmetic: 27.4 us -> 4.9 us
  Pallas kernels: 0 us -> 22.3 us
  starting transfers between devices: 10.2 us -> 26.5 us
  between operations: 14.1 us -> 0.31 us
    all_gather x2 -> x0, waiting for transfers between devices: 191 us -> none  [the longest x1 133 us: per_device(): lax.all_gather(in_basis, 'tok', axis=0, tiled=True)]
    all_gather x4 -> x0, blocking collectives: 73.8 us -> none  [the longest x1 29.4 us: per_device(): grad_all_rows = lax.all_gather(grads, 'tok', axis=0, tiled=True)]
    unnamed x1 -> x0, blocking collectives: 61.1 us -> none
    dot_general x5 -> x4, matrix products: 54.6 us -> 6.43 us  [dot(): return jnp.dot(a, b, preferred_element_type=WIDE)]
    convert_element_type x1 -> x0, local copies, waits for them, and re-layouts: 39.3 us -> none  [per_device(): (query_rot.astype(jnp.float32) / shifted[:, None, :]).astype(jnp.bfloat16)]
    ppermute x0 -> x21, waiting for transfers between devices: none -> 36 us  [the longest x9 19.1 us: swap(): lax.ppermute(value, axis, [(i, i ^ mask) for i in range(lax.axis_size(axi...]
    ppermute x0 -> x21, starting transfers between devices: none -> 26.5 us  [the longest x4 9.69 us: chain_sum(): into = lax.ppermute(part.astype(NARROW), 'tok', [(0, 1), (3, 2)])]
    pallas_call x0 -> x2, Pallas kernels: none -> 22.3 us  [the longest x1 19.7 us: scores(): pl.pallas_call(functools.partial(score_kernel, chunks), grid=(depth // st...]
  transfers between devices with their start and end apart: 4 -> 21, of which waited for: 2 -> 9; matrix products, arithmetic and copies ran while one was open for 16% -> 9% of each run, Pallas kernels for 0% -> 2%
where the time goes in v2:
time: 110 us; the launch traced here: 109 us
  waiting for transfers between devices  36 us (33%)
  starting transfers between devices  26.5 us (24%)
  Pallas kernels  22.3 us (20%)
  blocking collectives  9.73 us (9%)
  matrix products  6.43 us (6%)
  other arithmetic  4.9 us (4%)
  local copies, waits for them, and re-layouts  2.91 us (3%)
    pallas_call x1, Pallas kernels, scores(): pl.pallas_call(functools.partial(score_kernel, chunks), grid=(depth // st...  19.7 us
    ppermute x9, waiting for transfers between devices, swap(): lax.ppermute(value, axis, [(i, i ^ mask) for i in range(lax.axis_size(axi...  19.1 us
    ppermute x4, waiting for transfers between devices, chain_sum(): back = lax.ppermute(total, 'tok', [(1, 0), (2, 3)])  12.8 us
    all_to_all x1, blocking collectives, per_device(): lax.all_to_all(split, ('panel', 'tok'), split_axis=0, concat_axis=0, tile...  9.73 us
    ppermute x4, starting transfers between devices, chain_sum(): into = lax.ppermute(part.astype(NARROW), 'tok', [(0, 1), (3, 2)])  9.69 us
    ppermute x9, starting transfers between devices, swap(): lax.ppermute(value, axis, [(i, i ^ mask) for i in range(lax.axis_size(axi...  8.95 us
    dot_general x4, matrix products, dot(): return jnp.dot(a, b, preferred_element_type=WIDE)  6.43 us
    ppermute x4, starting transfers between devices, chain_sum(): back = lax.ppermute(total, 'tok', [(1, 0), (2, 3)])  5.13 us
  transfers between devices with their start and end apart: 21, of which 9 were waited for; matrix products, arithmetic and copies ran while one was open for 9% of the time, Pallas kernels for 2%

profile of v2, /device:TPU:0, one launch (start us, length us, event | category | flops | bytes accessed | tf_op | source)
XLA Modules:
  0.0 109.1 jit_solution(17843501747308336835)
XLA Ops:
  0.0 3.0 %collective-permute-start.15 = (bf16[96,1280]{1,0:T(8,128)(2,1)}, bf16[96,1280]{1,0:T(8,128)(2,1)}, u32[]{:S(2)}, u32[]{:S(2)}) collective-permute-start(bf16[96,1280]{1,0:T(8,128)(2,1)} %b0.1), channel_id=1, source_target_pairs={{0,1},{1,0},{2,3},{3,2},{4,5},{5,4},{6,7},{7,6},{8,9},{9,8},{10,11... | collective-permute-start | bytes 737288 | tf_op jit(solution)/shard_map/ppermute | solution.py:18
  3.0 2.5 %collective-permute-start.16 = (bf16[96,1280]{1,0:T(8,128)(2,1)}, bf16[96,1280]{1,0:T(8,128)(2,1)}, u32[]{:S(2)}, u32[]{:S(2)}) collective-permute-start(bf16[96,1280]{1,0:T(8,128)(2,1)} %b0.1), channel_id=1, source_target_pairs={{0,3},{1,2},{2,1},{3,0},{4,7},{5,6},{6,5},{7,4},{8,11},{9,10},{10,... | collective-permute-start | bytes 737288 | tf_op jit(solution)/shard_map/ppermute | solution.py:18
  5.6 1.5 %collective-permute-start.5 = (bf16[96,1280]{1,0:T(8,128)(2,1)}, bf16[96,1280]{1,0:T(8,128)(2,1)}, u32[]{:S(2)}, u32[]{:S(2)}) collective-permute-start(bf16[96,1280]{1,0:T(8,128)(2,1)} %param.7), channel_id=1, source_target_pairs={{0,8},{4,12},{8,0},{12,4},{1,9},{5,13},{9,1},{13,5},{2,10},{6,14},... | collective-permute-start | bytes 737288 | tf_op jit(solution)/shard_map/ppermute | solution.py:18
  7.1 2.5 %fusion.5 = (bf16[96,1280]{1,0:T(8,128)(2,1)}, f32[96,1280]{1,0:T(8,128)}) fusion(bf16[96,1280]{1,0:T(8,128)(2,1)} %param.7, bf16[1280,1280]{1,0:T(8,128)(2,1)S(1)} %copy-done), kind=kOutput, calls=%fused_computation.16 | convolution fusion | flops 314695680 | bytes 4259840 | tf_op jit(solution)/shard_map/dot_general | solution.py:22
  9.7 4.4 %collective-permute-start = (bf16[96,1280]{1,0:T(8,128)(2,1)}, bf16[96,1280]{1,0:T(8,128)(2,1)S(1)}, u32[]{:S(2)}, u32[]{:S(2)}) collective-permute-start(bf16[96,1280]{1,0:T(8,128)(2,1)} %get-tuple-element.9), channel_id=1, source_target_pairs={{0,1},{3,2},{4,5},{7,6},{8,9},{11,10},{12,13},{15,14},{16,17},{19,... | collective-permute-start | bytes 737288 | tf_op jit(solution)/shard_map/ppermute | solution.py:26
  14.1 3.9 %collective-permute-done.16.b2 = bf16[96,1280]{1,0:T(8,128)(2,1)} collective-permute-done((bf16[96,1280]{1,0:T(8,128)(2,1)}, bf16[96,1280]{1,0:T(8,128)(2,1)}, u32[]{:S(2)}, u32[]{:S(2)}) %collective-permute-start.16) | collective-permute-done | bytes 245792 | tf_op jit(solution)/shard_map/ppermute | solution.py:18
  18.0 9.4 %collective-permute-done.17.b3 = bf16[96,1280]{1,0:T(8,128)(2,1)} collective-permute-done((bf16[96,1280]{1,0:T(8,128)(2,1)}, bf16[96,1280]{1,0:T(8,128)(2,1)}, u32[]{:S(2)}, u32[]{:S(2)}) %collective-permute-start.17) | collective-permute-done | bytes 245792 | tf_op jit(solution)/shard_map/ppermute | solution.py:18
  27.4 1.9 %copy-done.1 = bf16[1280,1280]{1,0:T(8,128)(2,1)S(1)} copy-done((bf16[1280,1280]{1,0:T(8,128)(2,1)S(1)}, bf16[1280,1280]{1,0:T(8,128)(2,1)}, u32[]{:S(2)}) %copy-start.1) | copy-done | bytes 3276824
  29.4 2.7 %rotate.1 = (f32[192,1280]{1,0:T(8,128)S(1)}, bf16[192,1280]{1,0:T(8,128)(2,1)S(1)}) custom-call(s32[5]{0:T(128)S(1)} %stack.52.place_ref, bf16[96,1280]{1,0:T(8,128)(2,1)S(1)} %copy-done.2, bf16[96,1280]{1,0:T(8,128)(2,1)} %collective-permute-done.15.b1, bf16[96,1280]{1,0:T(8,128)(2,1)} %collective-permute-done.16.b2, ...), custom_call_target="tpu_custom_call" | custom-call | flops 1258291200 | bytes 3276800 | tf_op jit(solution)/shard_map/rotate/pallas_call | solution.py:50
  32.1 1.7 %fusion.7 = (bf16[96,1280]{1,0:T(8,128)(2,1)S(1)}, f32[96,1280]{1,0:T(8,128)S(1)}) fusion(bf16[96,1280]{1,0:T(8,128)(2,1)} %collective-permute-done.5, bf16[1280,1280]{1,0:T(8,128)(2,1)S(1)} %copy-done), kind=kOutput, calls=%fused_computation.18 | convolution fusion | flops 314695680 | bytes 4259840 | tf_op jit(solution)/shard_map/dot_general | solution.py:22
  33.8 1.7 %collective-permute-start.6 = (bf16[96,1280]{1,0:T(8,128)(2,1)S(1)}, bf16[96,1280]{1,0:T(8,128)(2,1)S(1)}, u32[]{:S(2)}, u32[]{:S(2)}) collective-permute-start(bf16[96,1280]{1,0:T(8,128)(2,1)S(1)} %get-tuple-element.13), channel_id=1, source_target_pairs={{0,1},{3,2},{4,5},{7,6},{8,9},{11,10},{12,13},{15,14},{16,17},{19,... | collective-permute-start | bytes 737288 | tf_op jit(solution)/shard_map/ppermute | solution.py:26
  35.5 1.6 %fusion.6 = (bf16[96,1280]{1,0:T(8,128)(2,1)S(1)}, f32[96,1280]{1,0:T(8,128)S(1)}) fusion(bf16[96,1280]{1,0:T(8,128)(2,1)} %collective-permute-done.2, bf16[1280,1280]{1,0:T(8,128)(2,1)S(1)} %copy-done), kind=kOutput, calls=%fused_computation.17 | convolution fusion | flops 314695680 | bytes 4259840 | tf_op jit(solution)/shard_map/dot_general | solution.py:22
  37.2 1.3 %collective-permute-start.3 = (bf16[96,1280]{1,0:T(8,128)(2,1)S(1)}, bf16[96,1280]{1,0:T(8,128)(2,1)S(1)}, u32[]{:S(2)}, u32[]{:S(2)}) collective-permute-start(bf16[96,1280]{1,0:T(8,128)(2,1)S(1)} %get-tuple-element.11), channel_id=1, source_target_pairs={{0,1},{3,2},{4,5},{7,6},{8,9},{11,10},{12,13},{15,14},{16,17},{19,... | collective-permute-start | bytes 737288 | tf_op jit(solution)/shard_map/ppermute | solution.py:26
  39.4 0.8 collective-permute-done.8
  40.9 2.3 %collective-permute-start.9 = (bf16[96,1280]{1,0:T(8,128)(2,1)S(1)}, bf16[96,1280]{1,0:T(8,128)(2,1)S(1)}, u32[]{:S(2)}, u32[]{:S(2)}) collective-permute-start(bf16[96,1280]{1,0:T(8,128)(2,1)S(1)} %get-tuple-element.15), channel_id=1, source_target_pairs={{0,1},{3,2},{4,5},{7,6},{8,9},{11,10},{12,13},{15,14},{16,17},{19,... | collective-permute-start | bytes 737288 | tf_op jit(solution)/shard_map/ppermute | solution.py:26
  44.0 3.1 %collective-permute-done.3 = bf16[96,1280]{1,0:T(8,128)(2,1)S(1)} collective-permute-done((bf16[96,1280]{1,0:T(8,128)(2,1)S(1)}, bf16[96,1280]{1,0:T(8,128)(2,1)S(1)}, u32[]{:S(2)}, u32[]{:S(2)}) %collective-permute-start.3) | collective-permute-done | bytes 245792 | tf_op jit(solution)/shard_map/ppermute | solution.py:26
  47.9 1.3 %collective-permute-start.11 = (bf16[96,1280]{1,0:T(8,128)(2,1)S(1)}, bf16[96,1280]{1,0:T(8,128)(2,1)}, u32[]{:S(2)}, u32[]{:S(2)}) collective-permute-start(bf16[96,1280]{1,0:T(8,128)(2,1)S(1)} %add_convert_fusion.4.refs_0_), channel_id=1, source_target_pairs={{1,0},{2,3},{5,4},{6,7},{9,8},{10,11},{13,12},{14,15},{17,16},{18,... | collective-permute-start | bytes 737288 | tf_op jit(solution)/shard_map/ppermute | solution.py:30
  49.3 1.5 %collective-permute-start.19 = (bf16[192,1280]{1,0:T(8,128)(2,1)S(1)}, bf16[192,1280]{1,0:T(8,128)(2,1)S(1)}, u32[]{:S(2)}, u32[]{:S(2)}) collective-permute-start(bf16[192,1280]{1,0:T(8,128)(2,1)S(1)} %fusion), channel_id=1, source_target_pairs={{0,8},{4,12},{8,0},{12,4},{1,9},{5,13},{9,1},{13,5},{2,10},{6,14},... | collective-permute-start | bytes 1474568 | tf_op jit(solution)/shard_map/ppermute | solution.py:18
  50.8 1.0 collective-permute-done.9
  52.6 0.8 add_convert_fusion.2.refs_2_
  53.4 1.3 %collective-permute-start.13 = (bf16[96,1280]{1,0:T(8,128)(2,1)}, bf16[96,1280]{1,0:T(8,128)(2,1)}, u32[]{:S(2)}, u32[]{:S(2)}) collective-permute-start(bf16[96,1280]{1,0:T(8,128)(2,1)} %add_convert_fusion.2.refs_2_), channel_id=1, source_target_pairs={{1,0},{2,3},{5,4},{6,7},{9,8},{10,11},{13,12},{14,15},{17,16},{18,... | collective-permute-start | bytes 737288 | tf_op jit(solution)/shard_map/ppermute | solution.py:30
  54.6 0.8 add_convert_fusion.3.refs_1_
  55.4 1.3 %collective-permute-start.12 = (bf16[96,1280]{1,0:T(8,128)(2,1)}, bf16[96,1280]{1,0:T(8,128)(2,1)}, u32[]{:S(2)}, u32[]{:S(2)}) collective-permute-start(bf16[96,1280]{1,0:T(8,128)(2,1)} %add_convert_fusion.3.refs_1_), channel_id=1, source_target_pairs={{1,0},{2,3},{5,4},{6,7},{9,8},{10,11},{13,12},{14,15},{17,16},{18,... | collective-permute-start | bytes 737288 | tf_op jit(solution)/shard_map/ppermute | solution.py:30
  56.7 4.9 %collective-permute-done.19 = bf16[192,1280]{1,0:T(8,128)(2,1)S(1)} collective-permute-done((bf16[192,1280]{1,0:T(8,128)(2,1)S(1)}, bf16[192,1280]{1,0:T(8,128)(2,1)S(1)}, u32[]{:S(2)}, u32[]{:S(2)}) %collective-permute-start.19) | collective-permute-done | bytes 491552 | tf_op jit(solution)/shard_map/ppermute | solution.py:18
  61.6 0.9 add_convert_fusion.refs_8_
  62.6 0.8 add_convert_fusion.1.refs_3_
  63.4 1.3 %collective-permute-start.14 = (bf16[96,1280]{1,0:T(8,128)(2,1)}, bf16[96,1280]{1,0:T(8,128)(2,1)}, u32[]{:S(2)}, u32[]{:S(2)}) collective-permute-start(bf16[96,1280]{1,0:T(8,128)(2,1)} %add_convert_fusion.1.refs_3_), channel_id=1, source_target_pairs={{1,0},{2,3},{5,4},{6,7},{9,8},{10,11},{13,12},{14,15},{17,16},{18,... | collective-permute-start | bytes 737288 | tf_op jit(solution)/shard_map/ppermute | solution.py:30
  64.7 3.7 %collective-permute-done.13.refs_6_ = bf16[96,1280]{1,0:T(8,128)(2,1)} collective-permute-done((bf16[96,1280]{1,0:T(8,128)(2,1)}, bf16[96,1280]{1,0:T(8,128)(2,1)}, u32[]{:S(2)}, u32[]{:S(2)}) %collective-permute-start.13) | collective-permute-done | bytes 245792 | tf_op jit(solution)/shard_map/ppermute | solution.py:30
  68.5 2.9 %collective-permute-done.12.refs_5_ = bf16[96,1280]{1,0:T(8,128)(2,1)} collective-permute-done((bf16[96,1280]{1,0:T(8,128)(2,1)}, bf16[96,1280]{1,0:T(8,128)(2,1)}, u32[]{:S(2)}, u32[]{:S(2)}) %collective-permute-start.12) | collective-permute-done | bytes 245792 | tf_op jit(solution)/shard_map/ppermute | solution.py:30
  71.4 6.1 %collective-permute-done.14.refs_7_ = bf16[96,1280]{1,0:T(8,128)(2,1)} collective-permute-done((bf16[96,1280]{1,0:T(8,128)(2,1)}, bf16[96,1280]{1,0:T(8,128)(2,1)}, u32[]{:S(2)}, u32[]{:S(2)}) %collective-permute-start.14) | collective-permute-done | bytes 245792 | tf_op jit(solution)/shard_map/ppermute | solution.py:30
  77.5 19.7 %scores.1 = f32[8,384]{1,0:T(8,128)S(1)} custom-call(s32[6]{0:T(128)S(1)} %stack.47.spot_ref, bf16[1280,8,1280]{2,1,0:T(8,128)(2,1)} %query_ref.1, f32[1280,1280]{1,0:T(8,128)} %eig_ref.1, bf16[96,1280]{1,0:T(8,128)(2,1)S(1)} %add_convert_fusion.4.refs_0_, bf16[96,1280]{1,0:T(8,128)(2,1)} %add_convert_fusion.3.refs_1_, ...), custom_call_target="tpu_custom_call" | custom-call | flops 10066329600 | bytes 32768000 | tf_op jit(solution)/shard_map/scores/pallas_call | solution.py:123
  97.4 9.7 %all_to_all.5 = f32[16,1,192]{2,1,0:T(1,128)S(1)} all-to-all(f32[16,1,192]{2,1,0:T(1,128)S(1)} %reshape.5), channel_id=1, replica_groups=mesh['groups'=2,'panel'=4,'tok'=4] {'panel','tok'}, dimensions={0} | all-to-all | bytes 24576 | tf_op jit(solution)/shard_map/all_to_all | solution.py:183
  (44 shorter events, 6.4 us)
Async XLA Ops:
  0.0 7.1 %copy-start = (bf16[1280,1280]{1,0:T(8,128)(2,1)S(1)}, bf16[1280,1280]{1,0:T(8,128)(2,1)}, u32[]{:S(2)}) copy-start(bf16[1280,1280]{1,0:T(8,128)(2,1)} %param.9) | copy-start | bytes 9830404
  0.0 27.4 %copy-start.2 = (bf16[96,1280]{1,0:T(8,128)(2,1)S(1)}, bf16[96,1280]{1,0:T(8,128)(2,1)}, u32[]{:S(2)}) copy-start(bf16[96,1280]{1,0:T(8,128)(2,1)} %b0.1) | copy-start | bytes 737284
  0.0 9.7 %collective-permute-start.15 = (bf16[96,1280]{1,0:T(8,128)(2,1)}, bf16[96,1280]{1,0:T(8,128)(2,1)}, u32[]{:S(2)}, u32[]{:S(2)}) collective-permute-start(bf16[96,1280]{1,0:T(8,128)(2,1)} %b0.1), channel_id=1, source_target_pairs={{0,1},{1,0},{2,3},{3,2},{4,5},{5,4},{6,7},{7,6},{8,9},{9,8},{10,11... | collective-permute-start | bytes 737288 | tf_op jit(solution)/shard_map/ppermute | solution.py:18
  3.0 15.0 %collective-permute-start.16 = (bf16[96,1280]{1,0:T(8,128)(2,1)}, bf16[96,1280]{1,0:T(8,128)(2,1)}, u32[]{:S(2)}, u32[]{:S(2)}) collective-permute-start(bf16[96,1280]{1,0:T(8,128)(2,1)} %b0.1), channel_id=1, source_target_pairs={{0,3},{1,2},{2,1},{3,0},{4,7},{5,6},{6,5},{7,4},{8,11},{9,10},{10,... | collective-permute-start | bytes 737288 | tf_op jit(solution)/shard_map/ppermute | solution.py:18
  5.5 21.9 %collective-permute-start.17 = (bf16[96,1280]{1,0:T(8,128)(2,1)}, bf16[96,1280]{1,0:T(8,128)(2,1)}, u32[]{:S(2)}, u32[]{:S(2)}) collective-permute-start(bf16[96,1280]{1,0:T(8,128)(2,1)} %b0.1), channel_id=1, source_target_pairs={{0,2},{1,3},{2,0},{3,1},{4,6},{5,7},{6,4},{7,5},{8,10},{9,11},{10,... | collective-permute-start | bytes 737288 | tf_op jit(solution)/shard_map/ppermute | solution.py:18
  5.6 26.5 %collective-permute-start.5 = (bf16[96,1280]{1,0:T(8,128)(2,1)}, bf16[96,1280]{1,0:T(8,128)(2,1)}, u32[]{:S(2)}, u32[]{:S(2)}) collective-permute-start(bf16[96,1280]{1,0:T(8,128)(2,1)} %param.7), channel_id=1, source_target_pairs={{0,8},{4,12},{8,0},{12,4},{1,9},{5,13},{9,1},{13,5},{2,10},{6,14},... | collective-permute-start | bytes 737288 | tf_op jit(solution)/shard_map/ppermute | solution.py:18
  7.1 28.4 %collective-permute-start.2 = (bf16[96,1280]{1,0:T(8,128)(2,1)}, bf16[96,1280]{1,0:T(8,128)(2,1)}, u32[]{:S(2)}, u32[]{:S(2)}) collective-permute-start(bf16[96,1280]{1,0:T(8,128)(2,1)} %param.7), channel_id=1, source_target_pairs={{0,4},{4,0},{8,12},{12,8},{1,5},{5,1},{9,13},{13,9},{2,6},{6,2},{1... | collective-permute-start | bytes 737288 | tf_op jit(solution)/shard_map/ppermute | solution.py:18
  9.7 29.0 %collective-permute-start = (bf16[96,1280]{1,0:T(8,128)(2,1)}, bf16[96,1280]{1,0:T(8,128)(2,1)S(1)}, u32[]{:S(2)}, u32[]{:S(2)}) collective-permute-start(bf16[96,1280]{1,0:T(8,128)(2,1)} %get-tuple-element.9), channel_id=1, source_target_pairs={{0,1},{3,2},{4,5},{7,6},{8,9},{11,10},{12,13},{15,14},{16,17},{19,... | collective-permute-start | bytes 737288 | tf_op jit(solution)/shard_map/ppermute | solution.py:26
  27.4 1.9 %copy-start.1 = (bf16[1280,1280]{1,0:T(8,128)(2,1)S(1)}, bf16[1280,1280]{1,0:T(8,128)(2,1)}, u32[]{:S(2)}) copy-start(bf16[1280,1280]{1,0:T(8,128)(2,1)} %basis_ref.1) | copy-start | bytes 9830404
  32.0 6.6 %copy-start.3 = (f32[96,1280]{1,0:T(8,128)S(1)}, f32[96,1280]{1,0:T(8,128)}, u32[]{:S(2)}) copy-start(f32[96,1280]{1,0:T(8,128)} %get-tuple-element.10) | copy-start | bytes 1474564
  32.1 17.1 %collective-permute-start.18 = (bf16[192,1280]{1,0:T(8,128)(2,1)S(1)}, bf16[192,1280]{1,0:T(8,128)(2,1)S(1)}, u32[]{:S(2)}, u32[]{:S(2)}) collective-permute-start(bf16[192,1280]{1,0:T(8,128)(2,1)S(1)} %get-tuple-element.8), channel_id=1, source_target_pairs={{0,4},{4,0},{8,12},{12,8},{1,5},{5,1},{9,13},{13,9},{2,6},{6,2},{1... | collective-permute-start | bytes 1474568 | tf_op jit(solution)/shard_map/ppermute | solution.py:18
  33.8 9.4 %collective-permute-start.6 = (bf16[96,1280]{1,0:T(8,128)(2,1)S(1)}, bf16[96,1280]{1,0:T(8,128)(2,1)S(1)}, u32[]{:S(2)}, u32[]{:S(2)}) collective-permute-start(bf16[96,1280]{1,0:T(8,128)(2,1)S(1)} %get-tuple-element.13), channel_id=1, source_target_pairs={{0,1},{3,2},{4,5},{7,6},{8,9},{11,10},{12,13},{15,14},{16,17},{19,... | collective-permute-start | bytes 737288 | tf_op jit(solution)/shard_map/ppermute | solution.py:26
  37.2 9.9 %collective-permute-start.3 = (bf16[96,1280]{1,0:T(8,128)(2,1)S(1)}, bf16[96,1280]{1,0:T(8,128)(2,1)S(1)}, u32[]{:S(2)}, u32[]{:S(2)}) collective-permute-start(bf16[96,1280]{1,0:T(8,128)(2,1)S(1)} %get-tuple-element.11), channel_id=1, source_target_pairs={{0,1},{3,2},{4,5},{7,6},{8,9},{11,10},{12,13},{15,14},{16,17},{19,... | collective-permute-start | bytes 737288 | tf_op jit(solution)/shard_map/ppermute | solution.py:26
  38.5 1.8 %collective-permute-start.8 = (bf16[96,1280]{1,0:T(8,128)(2,1)}, bf16[96,1280]{1,0:T(8,128)(2,1)S(1)}, u32[]{:S(2)}, u32[]{:S(2)}) collective-permute-start(bf16[96,1280]{1,0:T(8,128)(2,1)} %collective-permute-done.5), channel_id=1, source_target_pairs={{0,4},{4,0},{8,12},{12,8},{1,5},{5,1},{9,13},{13,9},{2,6},{6,2},{1... | collective-permute-start | bytes 737288 | tf_op jit(solution)/shard_map/ppermute | solution.py:18
  38.7 9.0 %collective-permute-start.1 = (bf16[96,1280]{1,0:T(8,128)(2,1)S(1)}, bf16[96,1280]{1,0:T(8,128)(2,1)S(1)}, u32[]{:S(2)}, u32[]{:S(2)}) collective-permute-start(bf16[96,1280]{1,0:T(8,128)(2,1)S(1)} %fusion.1), channel_id=1, source_target_pairs={{1,2},{2,1},{5,6},{6,5},{9,10},{10,9},{13,14},{14,13},{17,18},{18,... | collective-permute-start | bytes 737288 | tf_op jit(solution)/shard_map/ppermute | solution.py:28
  40.9 10.9 %collective-permute-start.9 = (bf16[96,1280]{1,0:T(8,128)(2,1)S(1)}, bf16[96,1280]{1,0:T(8,128)(2,1)S(1)}, u32[]{:S(2)}, u32[]{:S(2)}) collective-permute-start(bf16[96,1280]{1,0:T(8,128)(2,1)S(1)} %get-tuple-element.15), channel_id=1, source_target_pairs={{0,1},{3,2},{4,5},{7,6},{8,9},{11,10},{12,13},{15,14},{16,17},{19,... | collective-permute-start | bytes 737288 | tf_op jit(solution)/shard_map/ppermute | solution.py:26
  43.3 9.3 %collective-permute-start.7 = (bf16[96,1280]{1,0:T(8,128)(2,1)S(1)}, bf16[96,1280]{1,0:T(8,128)(2,1)S(1)}, u32[]{:S(2)}, u32[]{:S(2)}) collective-permute-start(bf16[96,1280]{1,0:T(8,128)(2,1)S(1)} %fusion.3), channel_id=1, source_target_pairs={{1,2},{2,1},{5,6},{6,5},{9,10},{10,9},{13,14},{14,13},{17,18},{18,... | collective-permute-start | bytes 737288 | tf_op jit(solution)/shard_map/ppermute | solution.py:28
  47.1 7.6 %collective-permute-start.4 = (bf16[96,1280]{1,0:T(8,128)(2,1)S(1)}, bf16[96,1280]{1,0:T(8,128)(2,1)S(1)}, u32[]{:S(2)}, u32[]{:S(2)}) collective-permute-start(bf16[96,1280]{1,0:T(8,128)(2,1)S(1)} %fusion.2), channel_id=1, source_target_pairs={{1,2},{2,1},{5,6},{6,5},{9,10},{10,9},{13,14},{14,13},{17,18},{18,... | collective-permute-start | bytes 737288 | tf_op jit(solution)/shard_map/ppermute | solution.py:28
  47.9 16.9 %collective-permute-start.11 = (bf16[96,1280]{1,0:T(8,128)(2,1)S(1)}, bf16[96,1280]{1,0:T(8,128)(2,1)}, u32[]{:S(2)}, u32[]{:S(2)}) collective-permute-start(bf16[96,1280]{1,0:T(8,128)(2,1)S(1)} %add_convert_fusion.4.refs_0_), channel_id=1, source_target_pairs={{1,0},{2,3},{5,4},{6,7},{9,8},{10,11},{13,12},{14,15},{17,16},{18,... | collective-permute-start | bytes 737288 | tf_op jit(solution)/shard_map/ppermute | solution.py:30
  49.3 12.4 %collective-permute-start.19 = (bf16[192,1280]{1,0:T(8,128)(2,1)S(1)}, bf16[192,1280]{1,0:T(8,128)(2,1)S(1)}, u32[]{:S(2)}, u32[]{:S(2)}) collective-permute-start(bf16[192,1280]{1,0:T(8,128)(2,1)S(1)} %fusion), channel_id=1, source_target_pairs={{0,8},{4,12},{8,0},{12,4},{1,9},{5,13},{9,1},{13,5},{2,10},{6,14},... | collective-permute-start | bytes 1474568 | tf_op jit(solution)/shard_map/ppermute | solution.py:18
  51.9 10.7 %collective-permute-start.10 = (bf16[96,1280]{1,0:T(8,128)(2,1)S(1)}, bf16[96,1280]{1,0:T(8,128)(2,1)S(1)}, u32[]{:S(2)}, u32[]{:S(2)}) collective-permute-start(bf16[96,1280]{1,0:T(8,128)(2,1)S(1)} %fusion.4), channel_id=1, source_target_pairs={{1,2},{2,1},{5,6},{6,5},{9,10},{10,9},{13,14},{14,13},{17,18},{18,... | collective-permute-start | bytes 737288 | tf_op jit(solution)/shard_map/ppermute | solution.py:28
  53.4 15.1 %collective-permute-start.13 = (bf16[96,1280]{1,0:T(8,128)(2,1)}, bf16[96,1280]{1,0:T(8,128)(2,1)}, u32[]{:S(2)}, u32[]{:S(2)}) collective-permute-start(bf16[96,1280]{1,0:T(8,128)(2,1)} %add_convert_fusion.2.refs_2_), channel_id=1, source_target_pairs={{1,0},{2,3},{5,4},{6,7},{9,8},{10,11},{13,12},{14,15},{17,16},{18,... | collective-permute-start | bytes 737288 | tf_op jit(solution)/shard_map/ppermute | solution.py:30
  55.4 16.0 %collective-permute-start.12 = (bf16[96,1280]{1,0:T(8,128)(2,1)}, bf16[96,1280]{1,0:T(8,128)(2,1)}, u32[]{:S(2)}, u32[]{:S(2)}) collective-permute-start(bf16[96,1280]{1,0:T(8,128)(2,1)} %add_convert_fusion.3.refs_1_), channel_id=1, source_target_pairs={{1,0},{2,3},{5,4},{6,7},{9,8},{10,11},{13,12},{14,15},{17,16},{18,... | collective-permute-start | bytes 737288 | tf_op jit(solution)/shard_map/ppermute | solution.py:30
  62.6 14.9 %collective-permute-start.20 = (bf16[192,1280]{1,0:T(8,128)(2,1)}, bf16[192,1280]{1,0:T(8,128)(2,1)}, u32[]{:S(2)}, u32[]{:S(2)}) collective-permute-start(bf16[192,1280]{1,0:T(8,128)(2,1)} %add_convert_fusion.refs_8_), channel_id=1, source_target_pairs={{0,4},{4,0},{8,12},{12,8},{1,5},{5,1},{9,13},{13,9},{2,6},{6,2},{1... | collective-permute-start | bytes 1474568 | tf_op jit(solution)/shard_map/ppermute | solution.py:18
  63.4 14.2 %collective-permute-start.14 = (bf16[96,1280]{1,0:T(8,128)(2,1)}, bf16[96,1280]{1,0:T(8,128)(2,1)}, u32[]{:S(2)}, u32[]{:S(2)}) collective-permute-start(bf16[96,1280]{1,0:T(8,128)(2,1)} %add_convert_fusion.1.refs_3_), channel_id=1, source_target_pairs={{1,0},{2,3},{5,4},{6,7},{9,8},{10,11},{13,12},{14,15},{17,16},{18,... | collective-permute-start | bytes 737288 | tf_op jit(solution)/shard_map/ppermute | solution.py:30

commit v3 on v0

v3 whole, which is shorter than its diff:
```python
import functools
import math

import jax
import jax.numpy as jnp
from jax import lax
from jax.experimental import pallas as pl
from jax.experimental.pallas import tpu as pltpu
from jax.sharding import PartitionSpec as P

DAMPING = 0.1
WIDE = jnp.float32
NARROW = jnp.bfloat16
ROOM = 48 * 1024 * 1024
LANES = 128
SLOTS = 3
KEPT = 1 << 20
IN_VMEM = pl.BlockSpec(memory_space=pltpu.VMEM)
IN_SMEM = pl.BlockSpec(memory_space=pltpu.SMEM)
ANYWHERE = pl.BlockSpec(memory_space=pl.ANY)


def swap(value, axis, mask):
    return lax.ppermute(value, axis, [(i, i ^ mask) for i in range(lax.axis_size(axis))])


def dot(a, b):
    return jnp.dot(a, b, preferred_element_type=WIDE)


class Steps:
    def __init__(self):
        self.last = None

    def __call__(self, name, body, ins, outs, scalars=None, scratch=(), room=16 * 1024 * 1024, flops=0, streamed=(), after=()):
        def block(x):
            if math.prod(x.shape) > KEPT:
                return IN_VMEM
            return pl.BlockSpec(x.shape, lambda i: (0,) * len(x.shape))

        def home(x):
            if math.prod(x.shape) > KEPT:
                return pltpu.with_memory_space_constraint(x, pltpu.VMEM)
            return pltpu.with_memory_space_constraint(x, pltpu.HBM) if x.dtype == WIDE else x

        def result(x):
            if math.prod(x.shape) > KEPT:
                return pltpu.VMEM(x.shape, x.dtype)
            return x

        streamed = [pltpu.with_memory_space_constraint(x, pltpu.HBM) for x in streamed]
        specs, args = [], []
        if scalars is not None:
            specs.append(IN_SMEM)
            args.append(scalars)
        specs += [block(x) for x in ins] + [ANYWHERE] * len(streamed)
        args += [home(x) for x in ins] + streamed
        kept = len(args)
        ties = list(after) + ([] if self.last is None else [self.last])
        specs += [ANYWHERE] * len(ties)
        args += ties
        given = len(args)

        def kernel(*refs):
            body(*refs[:kept], *refs[given:])

        moved = sum(math.prod(x.shape) * x.dtype.itemsize for x in [*ins, *outs, *streamed])
        results = pl.pallas_call(
            kernel,
            grid=(1,),
            in_specs=specs,
            out_specs=[block(x) for x in outs],
            out_shape=[result(x) for x in outs],
            scratch_shapes=list(scratch),
            compiler_params=pltpu.CompilerParams(vmem_limit_bytes=room),
            cost_estimate=pl.CostEstimate(flops=flops, bytes_accessed=moved, transcendentals=0),
            name=name,
        )(*args)
        self.last = results[-1]
        return results


def load_body(*refs):
    count = len(refs) // 2
    sems = refs[-1]
    copies = [pltpu.make_async_copy(refs[k], refs[count + k], sems.at[k]) for k in range(count)]
    for copy in copies:
        copy.start()
    for copy in copies:
        copy.wait()


def send_body(turn_ref, a_ref, b_ref, basis_ref, send_ref, rows_ref):
    pick(turn_ref[0], b_ref, a_ref, rows_ref)
    send_ref[...] = dot(rows_ref[...], basis_ref[...]).astype(NARROW)


def pick(turn, zero_ref, one_ref, rows_ref):
    @pl.when(turn == 0)
    def _():
        rows_ref[...] = zero_ref[...]

    @pl.when(turn == 1)
    def _():
        rows_ref[...] = one_ref[...]


def pair_body(turn_ref, a_ref, b_ref, basis_ref, got_ref, out_ref, rows_ref):
    pick(turn_ref[0], a_ref, b_ref, rows_ref)
    out_ref[...] = (dot(rows_ref[...], basis_ref[...]) + got_ref[...].astype(WIDE)).astype(NARROW)


def pass_body(a_ref, out_ref):
    out_ref[...] = a_ref[...]


def mark_body(out_ref):
    out_ref[...] = jnp.zeros_like(out_ref)


def add_body(a_ref, b_ref, out_ref):
    out_ref[...] = (a_ref[...].astype(WIDE) + b_ref[...].astype(WIDE)).astype(NARROW)


def rotate_body(place_ref, b0, b1, b2, b3, basis_ref, mine_ref, top_ref, low_ref, rows_ref):
    size = b0.shape[0]
    half = 2 * size
    for k, block in enumerate((b0, b1, b2, b3)):
        rows_ref[pl.ds(pl.multiple_of(place_ref[k] * size, size), size), :] = block[...]
    core = place_ref[4]
    other = dot(rows_ref[pl.ds(pl.multiple_of((1 - core) * half, half), half), :], basis_ref[...])
    top_ref[...] = other[:size].astype(NARROW)
    low_ref[...] = other[size:].astype(NARROW)
    mine_ref[...] = dot(rows_ref[pl.ds(pl.multiple_of(core * half, half), half), :], basis_ref[...])


def chip_sum_body(core_ref, mine_ref, top_pair, low_pair, wide_ref, top_out, low_out):
    size = top_out.shape[0]
    source = pl.ds(pl.multiple_of((1 - core_ref[0]) * size, size), size)
    for k, (pair, out) in enumerate(((top_pair, top_out), (low_pair, low_out))):
        rows = slice(k * size, (k + 1) * size)
        value = mine_ref[rows, :] + pair[source, :].astype(WIDE)
        wide_ref[rows, :] = value
        out[...] = value.astype(NARROW)


def panel_sum_body(wide_ref, top_ref, low_ref, top_out, low_out):
    half = top_ref.shape[0]
    top_out[...] = (wide_ref[:half, :] + top_ref[...].astype(WIDE)).astype(NARROW)
    low_out[...] = (wide_ref[half:, :] + low_ref[...].astype(WIDE)).astype(NARROW)


def score_body(
    spot_ref, a0, a1, a2, a3, mine_top, mine_low, other_top, other_low, query_ref, eig_ref, out_ref,
    act_ref, grad_ref, query_buf, eig_buf, sems
):
    depth, queries, cols = query_ref.shape
    tokens = out_ref.shape[1]
    count = depth // LANES

    def copies(k):
        slot = lax.rem(k, SLOTS)
        rows = pl.ds(pl.multiple_of(k * LANES, LANES), LANES)
        return (
            pltpu.make_async_copy(query_ref.at[rows], query_buf.at[slot], sems.at[slot, 0]),
            pltpu.make_async_copy(eig_ref.at[rows], eig_buf.at[slot], sems.at[slot, 1]),
        )

    for k in range(SLOTS - 1):
        for copy in copies(k):
            copy.start()

    size = tokens // 4
    for k, block in enumerate((a0, a1, a2, a3)):
        act_ref[pl.ds(pl.multiple_of(spot_ref[k] * size, size), size), :] = block[...]
    core = spot_ref[4]
    for first, refs in ((core, (mine_top, mine_low)), (1 - core, (other_top, other_low))):
        for k, ref in enumerate(refs):
            grad_ref[pl.ds(pl.multiple_of((2 * first + k) * size, size), size), :] = ref[...]

    group = LANES // queries
    lane = lax.broadcasted_iota(jnp.int32, (tokens, LANES), 1) // queries

    def step(k, total):
        @pl.when(k + SLOTS - 1 < count)
        def _():
            for copy in copies(k + SLOTS - 1):
                copy.start()

        for copy in copies(k):
            copy.wait()
        slot = lax.rem(k, SLOTS)
        start = pl.multiple_of(k * LANES, LANES)
        scale = 1.0 / (eig_buf[slot] + DAMPING)
        query = query_buf[slot].astype(WIDE) * scale[:, None, :]
        precond = query.reshape(LANES * queries, cols).astype(NARROW)
        mixed = lax.dot_general(
            act_ref[...], precond, (((1,), (1,)), ((), ())), preferred_element_type=WIDE
        )
        grad = grad_ref[:, pl.ds(start, LANES)].astype(WIDE)
        for part in range(queries):
            spread = jnp.take_along_axis(grad, lane + part * group, axis=1)
            total = total + mixed[:, part * LANES : (part + 1) * LANES] * spread
        return total

    total = lax.fori_loop(0, count, step, jnp.zeros((tokens, LANES), WIDE))
    shift = LANES // 2
    while shift >= queries:
        total = total + pltpu.roll(total, shift, 1)
        shift //= 2
    out_ref[...] = total.T[:queries, :]


def spread_out(partial):
    queries, tokens = partial.shape
    owners = lax.axis_size("panel") * lax.axis_size("tok")
    split = partial.reshape(queries, owners, tokens // owners).transpose(1, 0, 2)
    return lax.all_to_all(split, ("panel", "tok"), split_axis=0, concat_axis=0, tiled=True)


def on_lines_of_four(grads, acts, out_basis, in_basis, query_rot, eigvals):
    size, feats = grads.shape
    depth, queries, cols = query_rot.shape
    panel, tok = lax.axis_index("panel"), lax.axis_index("tok")
    core, turn = panel % 2, tok % 2
    steps = Steps()

    def wide(rows, width):
        return jax.ShapeDtypeStruct((rows, width), WIDE)

    def narrow(rows, width):
        return jax.ShapeDtypeStruct((rows, width), NARROW)

    def scalars(*values):
        return jnp.stack(values).astype(jnp.int32)

    g1, g3 = swap(grads, "tok", 1), swap(grads, "tok", 3)
    near = swap(acts, "panel", 1)
    far = swap(acts, "panel", 2)
    most = swap(acts, "panel", 3)

    def loaded(name, *arrays):
        return steps(
            name, load_body, [], [narrow(*x.shape) for x in arrays],
            scratch=[pltpu.SemaphoreType.DMA((len(arrays),))], streamed=arrays,
        )

    (in_basis,) = loaded("load_in", in_basis)
    one = [pltpu.VMEM((size, feats), NARROW)]
    cost = 2 * size * feats * cols
    (send1,) = steps(
        "send_near", send_body, [acts, near, in_basis], [narrow(size, cols)], scalars=scalars(turn), scratch=one, flops=cost
    )
    got1 = swap(send1, "tok", 1)
    (send2,) = steps(
        "send_far", send_body, [far, most, in_basis], [narrow(size, cols)], scalars=scalars(turn), scratch=one, flops=cost
    )
    got2 = swap(send2, "tok", 1)
    (g3,) = steps("pass", pass_body, [g3], [narrow(size, feats)], after=[g1])
    g2 = swap(g3, "tok", 1)
    (pair1,) = steps(
        "pair_near", pair_body, [acts, near, in_basis, got1], [narrow(size, cols)], scalars=scalars(turn), scratch=one, flops=cost
    )
    got1 = swap(pair1, "tok", 2)
    (pair2,) = steps(
        "pair_far", pair_body, [far, most, in_basis, got2], [narrow(size, cols)], scalars=scalars(turn), scratch=one, flops=cost
    )
    got2 = swap(pair2, "tok", 2)
    (out_basis,) = loaded("load_out", out_basis)
    mine, top, low = steps(
        "rotate", rotate_body, [grads, g1, g3, g2, out_basis],
        [wide(2 * size, depth), narrow(size, depth), narrow(size, depth)],
        scalars=scalars(tok, tok ^ 1, tok ^ 3, tok ^ 2, core),
        scratch=[pltpu.VMEM((4 * size, feats), NARROW)], flops=8 * size * feats * depth,
    )
    chips = [[2 * k, 2 * k + 1] for k in range(2)]
    top, low = (lax.all_gather(x, "panel", axis=0, tiled=True, axis_index_groups=chips) for x in (top, low))
    mine, top, low = steps(
        "chip_sum", chip_sum_body, [mine, top, low],
        [wide(2 * size, depth), narrow(size, depth), narrow(size, depth)], scalars=scalars(core),
    )
    top, low = swap(top, "panel", 2), swap(low, "panel", 2)
    (total1,) = steps("total_near", add_body, [pair1, got1], [narrow(size, cols)])
    back1 = swap(total1, "tok", 1)
    (total2,) = steps("total_far", add_body, [pair2, got2], [narrow(size, cols)])
    back2 = swap(total2, "tok", 1)
    mine_top, mine_low = steps("panel_sum", panel_sum_body, [mine, top, low], [narrow(size, depth)] * 2)
    other_top, other_low = swap(mine_top, "panel", 1), swap(mine_low, "panel", 1)
    steps("mark", mark_body, [], [wide(8, LANES)], after=[back1, back2])
    (partial,) = steps(
        "scores", score_body, [total1, back1, total2, back2, mine_top, mine_low, other_top, other_low],
        [wide(queries, 4 * size)],
        scalars=scalars(panel ^ turn, panel ^ turn ^ 1, panel ^ turn ^ 2, panel ^ turn ^ 3, core),
        scratch=[
            pltpu.VMEM((4 * size, cols), NARROW),
            pltpu.VMEM((4 * size, depth), NARROW),
            pltpu.VMEM((SLOTS, LANES, queries, cols), NARROW),
            pltpu.VMEM((SLOTS, LANES, cols), WIDE),
            pltpu.SemaphoreType.DMA((SLOTS, 2)),
        ],
        room=28 * 1024 * 1024, flops=8 * size * depth * queries * cols, streamed=[query_rot, eigvals],
    )
    return jnp.sum(spread_out(partial), axis=0).T


def any_score_kernel(query_ref, eig_ref, act_ref, grad_ref, out_ref, act_turned, grad_turned):
    step = pl.program_id(0)
    block, queries, cols = query_ref.shape
    tokens = out_ref.shape[1]
    piece = math.gcd(block, 32)

    @pl.when(step == 0)
    def _():
        act_turned[...] = act_ref[...].astype(WIDE).T.astype(NARROW)
        grad_turned[...] = grad_ref[...].astype(WIDE).T
        out_ref[...] = jnp.zeros_like(out_ref)

    total = out_ref[...]
    for k in range(block // piece):
        scale = 1.0 / (eig_ref[k * piece : (k + 1) * piece, :] + DAMPING)
        query = query_ref[k * piece : (k + 1) * piece].astype(WIDE) * scale[:, None, :]
        precond = query.reshape(piece * queries, cols).astype(NARROW)
        mixed = dot(precond, act_turned[...]).reshape(piece, queries, tokens)
        grad = grad_turned[pl.ds(pl.multiple_of(step * block + k * piece, piece), piece), :]
        total = total + jnp.sum(mixed * grad[:, None, :], axis=0)
    out_ref[...] = total


def on_any(grads, acts, out_basis, in_basis, query_rot, eigvals):
    acts_all = lax.all_gather(acts, "panel", axis=0, tiled=True)
    grads_all = lax.all_gather(grads, "tok", axis=0, tiled=True)
    act_rot = lax.psum(dot(acts_all, in_basis), "tok").astype(NARROW)
    grad_rot = lax.psum(dot(grads_all, out_basis), "panel").astype(NARROW)
    depth, queries, cols = query_rot.shape
    tokens = act_rot.shape[0]
    step = math.gcd(depth, 256)
    partial = pl.pallas_call(
        any_score_kernel,
        grid=(depth // step,),
        in_specs=[
            pl.BlockSpec((step, queries, cols), lambda i: (i, 0, 0)),
            pl.BlockSpec((step, cols), lambda i: (i, 0)),
            IN_VMEM,
            IN_VMEM,
        ],
        out_specs=pl.BlockSpec((queries, tokens), lambda i: (0, 0)),
        out_shape=jax.ShapeDtypeStruct((queries, tokens), WIDE),
        scratch_shapes=[pltpu.VMEM((cols, tokens), NARROW), pltpu.VMEM((depth, tokens), WIDE)],
        compiler_params=pltpu.CompilerParams(vmem_limit_bytes=ROOM),
        name="any_scores",
    )(query_rot, eigvals, act_rot, grad_rot)
    return jnp.sum(spread_out(partial), axis=0).T


def per_device(*arrays):
    four = lax.axis_size("panel") == 4 and lax.axis_size("tok") == 4
    return (on_lines_of_four if four else on_any)(*arrays)


def solution(mesh):
    placed = (
        P(("groups", "tok"), "panel"),
        P(("groups", "panel"), "tok"),
        P("panel", "tok"),
        P("tok", "panel"),
        P("tok", None, "panel"),
        P("tok", "panel"),
    )
    return jax.shard_map(
        per_device,
        mesh=mesh,
        in_specs=placed,
        out_specs=P(("groups", "panel", "tok"), None),
        check_vma=False,
    )
```

time: 477 us -> 92.5 us (0.19)
  waiting for transfers between devices: 192 us -> 24.3 us
  blocking collectives: 135 us -> 14.1 us
  matrix products: 54.6 us -> 0 us
  local copies, waits for them, and re-layouts: 42 us -> 2.87 us
  Pallas kernels: 0 us -> 34.4 us
  other arithmetic: 27.4 us -> 1.3 us
  between operations: 14.1 us -> 0.23 us
    all_gather x2 -> x0, waiting for transfers between devices: 191 us -> none  [the longest x1 133 us: per_device(): lax.all_gather(in_basis, 'tok', axis=0, tiled=True)]
    all_gather x4 -> x2, blocking collectives: 73.8 us -> 4.3 us  [on_lines_of_four(): lax.all_gather(x, 'panel', axis=0, tiled=True, axis_index_groups=chips)]
    unnamed x1 -> x0, blocking collectives: 61.1 us -> none
    dot_general x5 -> x0, matrix products: 54.6 us -> none  [the longest x3 40.8 us: score_block(): jnp.dot(grad_part, flattened, preferred_element_type=jnp.float32)]
    convert_element_type x1 -> x0, local copies, waits for them, and re-layouts: 39.3 us -> none  [per_device(): (query_rot.astype(jnp.float32) / shifted[:, None, :]).astype(jnp.bfloat16)]
    pallas_call x0 -> x14, Pallas kernels: none -> 34.4 us  [__call__(): pl.pallas_call(kernel, grid=(1,), in_specs=specs, out_specs=[block(x) for...]
    ppermute x0 -> x16, waiting for transfers between devices: none -> 24.3 us  [swap(): lax.ppermute(value, axis, [(i, i ^ mask) for i in range(lax.axis_size(axi...]
    convert_element_type x4 -> x0, other arithmetic: 21.2 us -> none  [the longest x1 21.1 us: per_device(): (query_rot.astype(jnp.float32) / shifted[:, None, :]).astype(jnp.bfloat16)]
  transfers between devices with their start and end apart: 4 -> 16, of which waited for: 2 -> 10; matrix products, arithmetic and copies ran while one was open for 16% -> 0% of each run, Pallas kernels for 0% -> 20%
where the time goes in v3:
time: 92.5 us; the launch traced here: 92 us
  Pallas kernels  34.4 us (37%)
  waiting for transfers between devices  24.3 us (26%)
  starting transfers between devices  14.9 us (16%)
  blocking collectives  14.1 us (15%)
  local copies, waits for them, and re-layouts  2.87 us (3%)
  other arithmetic  1.3 us (1%)
    pallas_call x14, Pallas kernels, __call__(): pl.pallas_call(kernel, grid=(1,), in_specs=specs, out_specs=[block(x) for...  34.4 us
    ppermute x16, waiting for transfers between devices, swap(): lax.ppermute(value, axis, [(i, i ^ mask) for i in range(lax.axis_size(axi...  24.3 us
    ppermute x16, starting transfers between devices, swap(): lax.ppermute(value, axis, [(i, i ^ mask) for i in range(lax.axis_size(axi...  14.9 us
    all_to_all x1, blocking collectives, spread_out(): lax.all_to_all(split, ('panel', 'tok'), split_axis=0, concat_axis=0, tile...  9.76 us
    all_gather x2, blocking collectives, on_lines_of_four(): lax.all_gather(x, 'panel', axis=0, tiled=True, axis_index_groups=chips)  4.3 us
    unnamed x16, local copies, waits for them, and re-layouts  2.09 us
  transfers between devices with their start and end apart: 16, of which 10 were waited for; matrix products, arithmetic and copies ran while one was open for 0% of the time, Pallas kernels for 20%

profile of v3, /device:TPU:0, one launch (start us, length us, event | category | flops | bytes accessed | tf_op | source)
XLA Modules:
  0.0 92.0 jit_solution(10718877724992708074)
XLA Ops:
  0.5 2.5 %collective-permute-start.4 = (bf16[96,1280]{1,0:T(8,128)(2,1)}, bf16[96,1280]{1,0:T(8,128)(2,1)S(1)}, u32[]{:S(2)}, u32[]{:S(2)}) collective-permute-start(bf16[96,1280]{1,0:T(8,128)(2,1)} %refs_1_.4), channel_id=1, source_target_pairs={{0,8},{4,12},{8,0},{12,4},{1,9},{5,13},{9,1},{13,5},{2,10},{6,14},... | collective-permute-start | bytes 737288 | tf_op jit(solution)/shard_map/ppermute | solution.py:24
  3.1 1.8 %collective-permute-start.3 = (bf16[96,1280]{1,0:T(8,128)(2,1)}, bf16[96,1280]{1,0:T(8,128)(2,1)}, u32[]{:S(2)}, u32[]{:S(2)}) collective-permute-start(bf16[96,1280]{1,0:T(8,128)(2,1)} %refs_1_.5), channel_id=1, source_target_pairs={{0,1},{1,0},{2,3},{3,2},{4,5},{5,4},{6,7},{7,6},{8,9},{9,8},{10,11... | collective-permute-start | bytes 737288 | tf_op jit(solution)/shard_map/ppermute | solution.py:24
  4.9 2.5 %collective-permute-start.2 = (bf16[96,1280]{1,0:T(8,128)(2,1)}, bf16[96,1280]{1,0:T(8,128)(2,1)}, u32[]{:S(2)}, u32[]{:S(2)}) collective-permute-start(bf16[96,1280]{1,0:T(8,128)(2,1)} %refs_1_.5), channel_id=1, source_target_pairs={{0,3},{1,2},{2,1},{3,0},{4,7},{5,6},{6,5},{7,4},{8,11},{9,10},{10,... | collective-permute-start | bytes 737288 | tf_op jit(solution)/shard_map/ppermute | solution.py:24
  7.4 1.9 %load_in.1.refs_3_.refs_4_ = bf16[1280,1280]{1,0:T(8,128)(2,1)S(1)} custom-call(bf16[1280,1280]{1,0:T(8,128)(2,1)} %refs_0_.2), custom_call_target="tpu_custom_call" | custom-call | bytes 6553600 | tf_op jit(solution)/shard_map/load_in/pallas_call | solution.py:68
  9.3 0.9 %copy-done.4 = bf16[96,1280]{1,0:T(8,128)(2,1)S(1)} copy-done((bf16[96,1280]{1,0:T(8,128)(2,1)S(1)}, bf16[96,1280]{1,0:T(8,128)(2,1)}, u32[]{:S(2)}) %copy-start.4) | copy-done | bytes 245784
  10.3 2.3 %send_near.1.refs_4_ = bf16[96,1280]{1,0:T(8,128)(2,1)} custom-call(s32[1]{0:T(128)} %bitcast.5.refs_0_, bf16[96,1280]{1,0:T(8,128)(2,1)S(1)} %copy-done.4, bf16[96,1280]{1,0:T(8,128)(2,1)} %collective-permute-done.refs_2_, bf16[1280,1280]{1,0:T(8,128)(2,1)S(1)} %load_in.1.refs_3_.refs_4_, bf16[1280,1280]{1,0:T(8,128)(2,1)S(1)} %load_in.1.refs_3_.refs_4_), custom_call_target="tpu_custom_call" | custom-call | flops 314572800 | bytes 4014080 | tf_op jit(solution)/shard_map/send_near/pallas_call | solution.py:68
  13.3 1.7 %collective-permute-done.5.refs_2_ = bf16[96,1280]{1,0:T(8,128)(2,1)} collective-permute-done((bf16[96,1280]{1,0:T(8,128)(2,1)}, bf16[96,1280]{1,0:T(8,128)(2,1)}, u32[]{:S(2)}, u32[]{:S(2)}) %collective-permute-start.5) | collective-permute-done | bytes 245792 | tf_op jit(solution)/shard_map/ppermute | solution.py:24
  15.0 2.3 %send_far.1.refs_2_ = bf16[96,1280]{1,0:T(8,128)(2,1)} custom-call(s32[1]{0:T(128)} %bitcast.5.refs_0_, bf16[96,1280]{1,0:T(8,128)(2,1)S(1)} %collective-permute-done.4.refs_1_, bf16[96,1280]{1,0:T(8,128)(2,1)} %collective-permute-done.5.refs_2_, bf16[1280,1280]{1,0:T(8,128)(2,1)S(1)} %load_in.1.refs_3_.refs_4_, bf16[96,1280]{1,0:T(8,128)(2,1)} %send_near.1.refs_4_), custom_call_target="tpu_custom_call" | custom-call | flops 314572800 | bytes 4014080 | tf_op jit(solution)/shard_map/send_far/pallas_call | solution.py:68
  17.3 1.6 %collective-permute-start.8 = (bf16[96,1280]{1,0:T(8,128)(2,1)}, bf16[96,1280]{1,0:T(8,128)(2,1)}, u32[]{:S(2)}, u32[]{:S(2)}) collective-permute-start(bf16[96,1280]{1,0:T(8,128)(2,1)} %send_far.1.refs_2_), channel_id=1, source_target_pairs={{0,1},{1,0},{2,3},{3,2},{4,5},{5,4},{6,7},{7,6},{8,9},{9,8},{10,11... | collective-permute-start | bytes 737288 | tf_op jit(solution)/shard_map/ppermute | solution.py:24
  18.9 0.9 collective-permute-done.2.refs_0_
  19.8 1.0 %pass.1.refs_5_.refs_3_ = bf16[96,1280]{1,0:T(8,128)(2,1)S(1)} custom-call(bf16[96,1280]{1,0:T(8,128)(2,1)} %collective-permute-done.2.refs_0_, bf16[96,1280]{1,0:T(8,128)(2,1)} %collective-permute-done.3.refs_1_.refs_2_, bf16[96,1280]{1,0:T(8,128)(2,1)} %send_far.1.refs_2_), custom_call_target="tpu_custom_call" | custom-call | bytes 491520 | tf_op jit(solution)/shard_map/pass/pallas_call | solution.py:68
  20.9 3.6 %collective-permute-done.1.refs_4_ = bf16[96,1280]{1,0:T(8,128)(2,1)} collective-permute-done((bf16[96,1280]{1,0:T(8,128)(2,1)}, bf16[96,1280]{1,0:T(8,128)(2,1)}, u32[]{:S(2)}, u32[]{:S(2)}) %collective-permute-start.1) | collective-permute-done | bytes 245792 | tf_op jit(solution)/shard_map/ppermute | solution.py:24
  24.5 0.9 %copy-done.5 = bf16[96,1280]{1,0:T(8,128)(2,1)S(1)} copy-done((bf16[96,1280]{1,0:T(8,128)(2,1)S(1)}, bf16[96,1280]{1,0:T(8,128)(2,1)}, u32[]{:S(2)}) %copy-start.5) | copy-done | bytes 245784
  25.5 1.7 %pair_near.1.refs_5_.refs_0_ = bf16[96,1280]{1,0:T(8,128)(2,1)S(1)} custom-call(s32[1]{0:T(128)} %bitcast.5.refs_0_, bf16[96,1280]{1,0:T(8,128)(2,1)S(1)} %copy-done.5, bf16[96,1280]{1,0:T(8,128)(2,1)} %collective-permute-done.refs_2_, bf16[1280,1280]{1,0:T(8,128)(2,1)S(1)} %load_in.1.refs_3_.refs_4_, bf16[96,1280]{1,0:T(8,128)(2,1)} %collective-permute-done.1.refs_4_, ...), custom_call_target="tpu_custom_call" | custom-call | flops 314572800 | bytes 4259840 | tf_op jit(solution)/shard_map/pair_near/pallas_call | solution.py:68
  27.2 1.2 %collective-permute-start.6 = (bf16[96,1280]{1,0:T(8,128)(2,1)S(1)}, bf16[96,1280]{1,0:T(8,128)(2,1)S(1)}, u32[]{:S(2)}, u32[]{:S(2)}) collective-permute-start(bf16[96,1280]{1,0:T(8,128)(2,1)S(1)} %pair_near.1.refs_5_.refs_0_), channel_id=1, source_target_pairs={{0,2},{1,3},{2,0},{3,1},{4,6},{5,7},{6,4},{7,5},{8,10},{9,11},{10,... | collective-permute-start | bytes 737288 | tf_op jit(solution)/shard_map/ppermute | solution.py:24
  28.4 1.4 %collective-permute-done.8.refs_4_ = bf16[96,1280]{1,0:T(8,128)(2,1)} collective-permute-done((bf16[96,1280]{1,0:T(8,128)(2,1)}, bf16[96,1280]{1,0:T(8,128)(2,1)}, u32[]{:S(2)}, u32[]{:S(2)}) %collective-permute-start.8) | collective-permute-done | bytes 245792 | tf_op jit(solution)/shard_map/ppermute | solution.py:24
  29.8 1.7 %pair_far.1.refs_1_.refs_0_ = bf16[96,1280]{1,0:T(8,128)(2,1)S(1)} custom-call(s32[1]{0:T(128)} %bitcast.5.refs_0_, bf16[96,1280]{1,0:T(8,128)(2,1)S(1)} %copy-done.3, bf16[96,1280]{1,0:T(8,128)(2,1)} %collective-permute-done.5.refs_2_, bf16[1280,1280]{1,0:T(8,128)(2,1)S(1)} %load_in.1.refs_3_.refs_4_, bf16[96,1280]{1,0:T(8,128)(2,1)} %collective-permute-done.8.refs_4_, ...), custom_call_target="tpu_custom_call" | custom-call | flops 314572800 | bytes 4259840 | tf_op jit(solution)/shard_map/pair_far/pallas_call | solution.py:68
  31.5 1.2 %collective-permute-start.10 = (bf16[96,1280]{1,0:T(8,128)(2,1)S(1)}, bf16[96,1280]{1,0:T(8,128)(2,1)S(1)}, u32[]{:S(2)}, u32[]{:S(2)}) collective-permute-start(bf16[96,1280]{1,0:T(8,128)(2,1)S(1)} %pair_far.1.refs_1_.refs_0_), channel_id=1, source_target_pairs={{0,2},{1,3},{2,0},{3,1},{4,6},{5,7},{6,4},{7,5},{8,10},{9,11},{10,... | collective-permute-start | bytes 737288 | tf_op jit(solution)/shard_map/ppermute | solution.py:24
  32.7 1.9 %load_out.1.refs_5_.refs_6_ = bf16[1280,1280]{1,0:T(8,128)(2,1)S(1)} custom-call(bf16[1280,1280]{1,0:T(8,128)(2,1)} %refs_0_.3, bf16[96,1280]{1,0:T(8,128)(2,1)S(1)} %pair_far.1.refs_1_.refs_0_), custom_call_target="tpu_custom_call" | custom-call | bytes 6553600 | tf_op jit(solution)/shard_map/load_out/pallas_call | solution.py:68
  34.7 4.5 %collective-permute-done.7.refs_4_ = bf16[96,1280]{1,0:T(8,128)(2,1)} collective-permute-done((bf16[96,1280]{1,0:T(8,128)(2,1)S(1)}, bf16[96,1280]{1,0:T(8,128)(2,1)}, u32[]{:S(2)}, u32[]{:S(2)}) %collective-permute-start.7) | collective-permute-done | bytes 245792 | tf_op jit(solution)/shard_map/ppermute | solution.py:24
  39.2 2.6 %rotate.1 = (f32[192,1280]{1,0:T(8,128)S(1)}, bf16[96,1280]{1,0:T(8,128)(2,1)S(1)}, bf16[96,1280]{1,0:T(8,128)(2,1)S(1)}) custom-call(s32[5]{0:T(128)S(1)} %stack.52.refs_0_, bf16[96,1280]{1,0:T(8,128)(2,1)S(1)} %copy-done.6, bf16[96,1280]{1,0:T(8,128)(2,1)} %collective-permute-done.3.refs_1_.refs_2_, bf16[96,1280]{1,0:T(8,128)(2,1)S(1)} %pass.1.refs_5_.refs_3_, ...), custom_call_target="tpu_custom_call" | custom-call | flops 1258291200 | bytes 5734400 | tf_op jit(solution)/shard_map/rotate/pallas_call | solution.py:68
  41.7 2.2 %all_gather.6.refs_2_ = bf16[192,1280]{1,0:T(8,128)(2,1)S(1)} all-gather(bf16[96,1280]{1,0:T(8,128)(2,1)S(1)} %get-tuple-element.14), channel_id=1, replica_groups={{0,4},{8,12},{1,5},{9,13},{2,6},{10,14},{3,7},{11,15},{16,20},{24,28},{..., dimensions={0}, use_global_device_ids=true | all-gather | bytes 737280 | tf_op jit(solution)/shard_map/all_gather | solution.py:277
  43.9 2.1 %all_gather.7.refs_3_ = bf16[192,1280]{1,0:T(8,128)(2,1)S(1)} all-gather(bf16[96,1280]{1,0:T(8,128)(2,1)S(1)} %get-tuple-element.15.refs_4_), channel_id=1, replica_groups={{0,4},{8,12},{1,5},{9,13},{2,6},{10,14},{3,7},{11,15},{16,20},{24,28},{..., dimensions={0}, use_global_device_ids=true | all-gather | bytes 737280 | tf_op jit(solution)/shard_map/all_gather | solution.py:277
  46.0 1.4 %chip_sum.1 = (f32[192,1280]{1,0:T(8,128)S(1)}, bf16[96,1280]{1,0:T(8,128)(2,1)S(1)}, bf16[96,1280]{1,0:T(8,128)(2,1)S(1)}) custom-call(s32[1]{0:T(128)} %bitcast.4.refs_0_, f32[192,1280]{1,0:T(8,128)} %copy-done, bf16[192,1280]{1,0:T(8,128)(2,1)S(1)} %all_gather.6.refs_2_, bf16[192,1280]{1,0:T(8,128)(2,1)S(1)} %all_gather.7.refs_3_, ...), custom_call_target="tpu_custom_call" | custom-call | bytes 3440640 | tf_op jit(solution)/shard_map/chip_sum/pallas_call | solution.py:68
  47.4 1.6 %collective-permute-start.12 = (bf16[96,1280]{1,0:T(8,128)(2,1)S(1)}, bf16[96,1280]{1,0:T(8,128)(2,1)S(1)}, u32[]{:S(2)}, u32[]{:S(2)}) collective-permute-start(bf16[96,1280]{1,0:T(8,128)(2,1)S(1)} %get-tuple-element.18), channel_id=1, source_target_pairs={{0,8},{4,12},{8,0},{12,4},{1,9},{5,13},{9,1},{13,5},{2,10},{6,14},... | collective-permute-start | bytes 737288 | tf_op jit(solution)/shard_map/ppermute | solution.py:24
  49.7 2.1 %collective-permute-done.10.refs_1_ = bf16[96,1280]{1,0:T(8,128)(2,1)S(1)} collective-permute-done((bf16[96,1280]{1,0:T(8,128)(2,1)S(1)}, bf16[96,1280]{1,0:T(8,128)(2,1)S(1)}, u32[]{:S(2)}, u32[]{:S(2)}) %collective-permute-start.10) | collective-permute-done | bytes 245792 | tf_op jit(solution)/shard_map/ppermute | solution.py:24
  51.9 4.3 %collective-permute-done.12.refs_1_ = bf16[96,1280]{1,0:T(8,128)(2,1)S(1)} collective-permute-done((bf16[96,1280]{1,0:T(8,128)(2,1)S(1)}, bf16[96,1280]{1,0:T(8,128)(2,1)S(1)}, u32[]{:S(2)}, u32[]{:S(2)}) %collective-permute-start.12) | collective-permute-done | bytes 245792 | tf_op jit(solution)/shard_map/ppermute | solution.py:24
  56.3 4.5 %collective-permute-done.13.refs_2_ = bf16[96,1280]{1,0:T(8,128)(2,1)S(1)} collective-permute-done((bf16[96,1280]{1,0:T(8,128)(2,1)S(1)}, bf16[96,1280]{1,0:T(8,128)(2,1)S(1)}, u32[]{:S(2)}, u32[]{:S(2)}) %collective-permute-start.13) | collective-permute-done | bytes 245792 | tf_op jit(solution)/shard_map/ppermute | solution.py:24
  60.8 1.3 %panel_sum.1 = (bf16[96,1280]{1,0:T(8,128)(2,1)S(1)}, bf16[96,1280]{1,0:T(8,128)(2,1)S(1)}) custom-call(f32[192,1280]{1,0:T(8,128)} %copy-done.1, bf16[96,1280]{1,0:T(8,128)(2,1)S(1)} %collective-permute-done.12.refs_1_, bf16[96,1280]{1,0:T(8,128)(2,1)S(1)} %collective-permute-done.13.refs_2_, bf16[96,1280]{1,0:T(8,128)(2,1)S(1)} %total_far.1.refs_3_), custom_call_target="tpu_custom_call" | custom-call | bytes 1966080 | tf_op jit(solution)/shard_map/panel_sum/pallas_call | solution.py:68
  62.7 0.9 collective-permute-done.14.refs_7_
  64.0 16.1 %scores.1 = f32[8,384]{1,0:T(8,128)S(1)} custom-call(s32[5]{0:T(128)S(1)} %stack.46.refs_0_, bf16[96,1280]{1,0:T(8,128)(2,1)S(1)} %total_near.1.refs_2_.refs_1_, bf16[96,1280]{1,0:T(8,128)(2,1)S(1)} %collective-permute-done.9.refs_0_.refs_2_, bf16[96,1280]{1,0:T(8,128)(2,1)S(1)} %total_far.1.refs_3_, ...), custom_call_target="tpu_custom_call" | custom-call | flops 10066329600 | bytes 34746368 | tf_op jit(solution)/shard_map/scores/pallas_call | solution.py:68
  80.3 9.8 %all_to_all.5 = f32[16,1,192]{2,1,0:T(1,128)S(1)} all-to-all(f32[16,1,192]{2,1,0:T(1,128)S(1)} %reshape.4), channel_id=1, replica_groups=mesh['groups'=2,'panel'=4,'tok'=4] {'panel','tok'}, dimensions={0} | all-to-all | bytes 24576 | tf_op jit(solution)/shard_map/all_to_all | solution.py:218
  (40 shorter events, 5.3 us)
Async XLA Ops:
  0.0 9.3 %collective-permute-start = (bf16[96,1280]{1,0:T(8,128)(2,1)}, bf16[96,1280]{1,0:T(8,128)(2,1)}, u32[]{:S(2)}, u32[]{:S(2)}) collective-permute-start(bf16[96,1280]{1,0:T(8,128)(2,1)} %refs_1_.4), channel_id=1, source_target_pairs={{0,4},{4,0},{8,12},{12,8},{1,5},{5,1},{9,13},{13,9},{2,6},{6,2},{1... | collective-permute-start | bytes 737288 | tf_op jit(solution)/shard_map/ppermute | solution.py:24
  0.5 12.8 %collective-permute-start.4 = (bf16[96,1280]{1,0:T(8,128)(2,1)}, bf16[96,1280]{1,0:T(8,128)(2,1)S(1)}, u32[]{:S(2)}, u32[]{:S(2)}) collective-permute-start(bf16[96,1280]{1,0:T(8,128)(2,1)} %refs_1_.4), channel_id=1, source_target_pairs={{0,8},{4,12},{8,0},{12,4},{1,9},{5,13},{9,1},{13,5},{2,10},{6,14},... | collective-permute-start | bytes 737288 | tf_op jit(solution)/shard_map/ppermute | solution.py:24
  2.9 12.0 %collective-permute-start.5 = (bf16[96,1280]{1,0:T(8,128)(2,1)}, bf16[96,1280]{1,0:T(8,128)(2,1)}, u32[]{:S(2)}, u32[]{:S(2)}) collective-permute-start(bf16[96,1280]{1,0:T(8,128)(2,1)} %refs_1_.4), channel_id=1, source_target_pairs={{0,12},{4,8},{8,4},{12,0},{1,13},{5,9},{9,5},{13,1},{2,14},{6,10},... | collective-permute-start | bytes 737288 | tf_op jit(solution)/shard_map/ppermute | solution.py:24
  3.1 15.8 %collective-permute-start.3 = (bf16[96,1280]{1,0:T(8,128)(2,1)}, bf16[96,1280]{1,0:T(8,128)(2,1)}, u32[]{:S(2)}, u32[]{:S(2)}) collective-permute-start(bf16[96,1280]{1,0:T(8,128)(2,1)} %refs_1_.5), channel_id=1, source_target_pairs={{0,1},{1,0},{2,3},{3,2},{4,5},{5,4},{6,7},{7,6},{8,9},{9,8},{10,11... | collective-permute-start | bytes 737288 | tf_op jit(solution)/shard_map/ppermute | solution.py:24
  4.9 14.9 %collective-permute-start.2 = (bf16[96,1280]{1,0:T(8,128)(2,1)}, bf16[96,1280]{1,0:T(8,128)(2,1)}, u32[]{:S(2)}, u32[]{:S(2)}) collective-permute-start(bf16[96,1280]{1,0:T(8,128)(2,1)} %refs_1_.5), channel_id=1, source_target_pairs={{0,3},{1,2},{2,1},{3,0},{4,7},{5,6},{6,5},{7,4},{8,11},{9,10},{10,... | collective-permute-start | bytes 737288 | tf_op jit(solution)/shard_map/ppermute | solution.py:24
  9.3 0.9 %copy-start.4 = (bf16[96,1280]{1,0:T(8,128)(2,1)S(1)}, bf16[96,1280]{1,0:T(8,128)(2,1)}, u32[]{:S(2)}) copy-start(bf16[96,1280]{1,0:T(8,128)(2,1)} %refs_1_.4) | copy-start | bytes 737284
  12.6 11.9 %collective-permute-start.1 = (bf16[96,1280]{1,0:T(8,128)(2,1)}, bf16[96,1280]{1,0:T(8,128)(2,1)}, u32[]{:S(2)}, u32[]{:S(2)}) collective-permute-start(bf16[96,1280]{1,0:T(8,128)(2,1)} %send_near.1.refs_4_), channel_id=1, source_target_pairs={{0,1},{1,0},{2,3},{3,2},{4,5},{5,4},{6,7},{7,6},{8,9},{9,8},{10,11... | collective-permute-start | bytes 737288 | tf_op jit(solution)/shard_map/ppermute | solution.py:24
  13.3 5.6 %copy-start.2 = (bf16[96,1280]{1,0:T(8,128)(2,1)}, bf16[96,1280]{1,0:T(8,128)(2,1)S(1)}, u32[]{:S(2)}) copy-start(bf16[96,1280]{1,0:T(8,128)(2,1)S(1)} %collective-permute-done.4.refs_1_) | copy-start | bytes 737284
  17.3 12.5 %collective-permute-start.8 = (bf16[96,1280]{1,0:T(8,128)(2,1)}, bf16[96,1280]{1,0:T(8,128)(2,1)}, u32[]{:S(2)}, u32[]{:S(2)}) collective-permute-start(bf16[96,1280]{1,0:T(8,128)(2,1)} %send_far.1.refs_2_), channel_id=1, source_target_pairs={{0,1},{1,0},{2,3},{3,2},{4,5},{5,4},{6,7},{7,6},{8,9},{9,8},{10,11... | collective-permute-start | bytes 737288 | tf_op jit(solution)/shard_map/ppermute | solution.py:24
  20.8 18.4 %collective-permute-start.7 = (bf16[96,1280]{1,0:T(8,128)(2,1)S(1)}, bf16[96,1280]{1,0:T(8,128)(2,1)}, u32[]{:S(2)}, u32[]{:S(2)}) collective-permute-start(bf16[96,1280]{1,0:T(8,128)(2,1)S(1)} %pass.1.refs_5_.refs_3_), channel_id=1, source_target_pairs={{0,1},{1,0},{2,3},{3,2},{4,5},{5,4},{6,7},{7,6},{8,9},{9,8},{10,11... | collective-permute-start | bytes 737288 | tf_op jit(solution)/shard_map/ppermute | solution.py:24
  20.9 8.9 %copy-start.3 = (bf16[96,1280]{1,0:T(8,128)(2,1)S(1)}, bf16[96,1280]{1,0:T(8,128)(2,1)}, u32[]{:S(2)}) copy-start(bf16[96,1280]{1,0:T(8,128)(2,1)} %copy-done.2) | copy-start | bytes 737284
  24.5 0.9 %copy-start.5 = (bf16[96,1280]{1,0:T(8,128)(2,1)S(1)}, bf16[96,1280]{1,0:T(8,128)(2,1)}, u32[]{:S(2)}) copy-start(bf16[96,1280]{1,0:T(8,128)(2,1)} %refs_1_.4) | copy-start | bytes 737284
  27.2 22.3 %collective-permute-start.6 = (bf16[96,1280]{1,0:T(8,128)(2,1)S(1)}, bf16[96,1280]{1,0:T(8,128)(2,1)S(1)}, u32[]{:S(2)}, u32[]{:S(2)}) collective-permute-start(bf16[96,1280]{1,0:T(8,128)(2,1)S(1)} %pair_near.1.refs_5_.refs_0_), channel_id=1, source_target_pairs={{0,2},{1,3},{2,0},{3,1},{4,6},{5,7},{6,4},{7,5},{8,10},{9,11},{10,... | collective-permute-start | bytes 737288 | tf_op jit(solution)/shard_map/ppermute | solution.py:24
  31.5 7.6 %copy-start.6 = (bf16[96,1280]{1,0:T(8,128)(2,1)S(1)}, bf16[96,1280]{1,0:T(8,128)(2,1)}, u32[]{:S(2)}) copy-start(bf16[96,1280]{1,0:T(8,128)(2,1)} %refs_1_.5) | copy-start | bytes 737284
  31.5 20.3 %collective-permute-start.10 = (bf16[96,1280]{1,0:T(8,128)(2,1)S(1)}, bf16[96,1280]{1,0:T(8,128)(2,1)S(1)}, u32[]{:S(2)}, u32[]{:S(2)}) collective-permute-start(bf16[96,1280]{1,0:T(8,128)(2,1)S(1)} %pair_far.1.refs_1_.refs_0_), channel_id=1, source_target_pairs={{0,2},{1,3},{2,0},{3,1},{4,6},{5,7},{6,4},{7,5},{8,10},{9,11},{10,... | collective-permute-start | bytes 737288 | tf_op jit(solution)/shard_map/ppermute | solution.py:24
  41.7 4.3 %copy-start = (f32[192,1280]{1,0:T(8,128)}, f32[192,1280]{1,0:T(8,128)S(1)}, u32[]{:S(2)}) copy-start(f32[192,1280]{1,0:T(8,128)S(1)} %get-tuple-element.13.refs_1_) | copy-start | bytes 2949124
  47.4 13.3 %copy-start.1 = (f32[192,1280]{1,0:T(8,128)}, f32[192,1280]{1,0:T(8,128)S(1)}, u32[]{:S(2)}) copy-start(f32[192,1280]{1,0:T(8,128)S(1)} %get-tuple-element.17.refs_0_) | copy-start | bytes 2949124
  47.4 8.9 %collective-permute-start.12 = (bf16[96,1280]{1,0:T(8,128)(2,1)S(1)}, bf16[96,1280]{1,0:T(8,128)(2,1)S(1)}, u32[]{:S(2)}, u32[]{:S(2)}) collective-permute-start(bf16[96,1280]{1,0:T(8,128)(2,1)S(1)} %get-tuple-element.18), channel_id=1, source_target_pairs={{0,8},{4,12},{8,0},{12,4},{1,9},{5,13},{9,1},{13,5},{2,10},{6,14},... | collective-permute-start | bytes 737288 | tf_op jit(solution)/shard_map/ppermute | solution.py:24
  49.0 11.7 %collective-permute-start.13 = (bf16[96,1280]{1,0:T(8,128)(2,1)S(1)}, bf16[96,1280]{1,0:T(8,128)(2,1)S(1)}, u32[]{:S(2)}, u32[]{:S(2)}) collective-permute-start(bf16[96,1280]{1,0:T(8,128)(2,1)S(1)} %get-tuple-element.16.refs_2_), channel_id=1, source_target_pairs={{0,8},{4,12},{8,0},{12,4},{1,9},{5,13},{9,1},{13,5},{2,10},{6,14},... | collective-permute-start | bytes 737288 | tf_op jit(solution)/shard_map/ppermute | solution.py:24
  49.6 13.1 %collective-permute-start.9 = (bf16[96,1280]{1,0:T(8,128)(2,1)S(1)}, bf16[96,1280]{1,0:T(8,128)(2,1)S(1)}, u32[]{:S(2)}, u32[]{:S(2)}) collective-permute-start(bf16[96,1280]{1,0:T(8,128)(2,1)S(1)} %total_near.1.refs_2_.refs_1_), channel_id=1, source_target_pairs={{0,1},{1,0},{2,3},{3,2},{4,5},{5,4},{6,7},{7,6},{8,9},{9,8},{10,11... | collective-permute-start | bytes 737288 | tf_op jit(solution)/shard_map/ppermute | solution.py:24
  51.9 10.8 %collective-permute-start.11 = (bf16[96,1280]{1,0:T(8,128)(2,1)S(1)}, bf16[96,1280]{1,0:T(8,128)(2,1)S(1)}, u32[]{:S(2)}, u32[]{:S(2)}) collective-permute-start(bf16[96,1280]{1,0:T(8,128)(2,1)S(1)} %total_far.1.refs_3_), channel_id=1, source_target_pairs={{0,1},{1,0},{2,3},{3,2},{4,5},{5,4},{6,7},{7,6},{8,9},{9,8},{10,11... | collective-permute-start | bytes 737288 | tf_op jit(solution)/shard_map/ppermute | solution.py:24
  62.0 1.6 %collective-permute-start.14 = (bf16[96,1280]{1,0:T(8,128)(2,1)S(1)}, bf16[96,1280]{1,0:T(8,128)(2,1)S(1)}, u32[]{:S(2)}, u32[]{:S(2)}) collective-permute-start(bf16[96,1280]{1,0:T(8,128)(2,1)S(1)} %get-tuple-element.19.refs_5_), channel_id=1, source_target_pairs={{0,4},{4,0},{8,12},{12,8},{1,5},{5,1},{9,13},{13,9},{2,6},{6,2},{1... | collective-permute-start | bytes 737288 | tf_op jit(solution)/shard_map/ppermute | solution.py:24
  62.1 1.9 %collective-permute-start.15 = (bf16[96,1280]{1,0:T(8,128)(2,1)S(1)}, bf16[96,1280]{1,0:T(8,128)(2,1)S(1)}, u32[]{:S(2)}, u32[]{:S(2)}) collective-permute-start(bf16[96,1280]{1,0:T(8,128)(2,1)S(1)} %get-tuple-element.20.refs_2_.refs_6_), channel_id=1, source_target_pairs={{0,4},{4,0},{8,12},{12,8},{1,5},{5,1},{9,13},{13,9},{2,6},{6,2},{1... | collective-permute-start | bytes 737288 | tf_op jit(solution)/shard_map/ppermute | solution.py:24

commit v4 on v3

--- a/solution.py
+++ b/solution.py
@@ -14,7 +14,7 @@
 ROOM = 48 * 1024 * 1024
 LANES = 128
 SLOTS = 3
-KEPT = 1 << 20
+KEPT = 1 << 19
 IN_VMEM = pl.BlockSpec(memory_space=pltpu.VMEM)
 IN_SMEM = pl.BlockSpec(memory_space=pltpu.SMEM)
 ANYWHERE = pl.BlockSpec(memory_space=pl.ANY)
@@ -32,7 +32,7 @@
     def __init__(self):
         self.last = None
 
-    def __call__(self, name, body, ins, outs, scalars=None, scratch=(), room=16 * 1024 * 1024, flops=0, streamed=(), after=()):
+    def __call__(self, name, body, ins, outs, scalars=None, scratch=(), room=16 * 1024 * 1024, flops=0, streamed=(), where=(), after=(), weight=0):
         def block(x):
             if math.prod(x.shape) > KEPT:
                 return IN_VMEM
@@ -41,7 +41,7 @@
         def home(x):
             if math.prod(x.shape) > KEPT:
                 return pltpu.with_memory_space_constraint(x, pltpu.VMEM)
-            return pltpu.with_memory_space_constraint(x, pltpu.HBM) if x.dtype == WIDE else x
+            return x
 
         def result(x):
             if math.prod(x.shape) > KEPT:
@@ -53,8 +53,8 @@
         if scalars is not None:
             specs.append(IN_SMEM)
             args.append(scalars)
-        specs += [block(x) for x in ins] + [ANYWHERE] * len(streamed)
-        args += [home(x) for x in ins] + streamed
+        specs += [block(x) for x in ins] + [ANYWHERE] * (len(streamed) + len(where))
+        args += [home(x) for x in ins] + streamed + list(where)
         kept = len(args)
         ties = list(after) + ([] if self.last is None else [self.last])
         specs += [ANYWHERE] * len(ties)
@@ -64,7 +64,7 @@
         def kernel(*refs):
             body(*refs[:kept], *refs[given:])
 
-        moved = sum(math.prod(x.shape) * x.dtype.itemsize for x in [*ins, *outs, *streamed])
+        moved = weight + sum(math.prod(x.shape) * x.dtype.itemsize for x in [*ins, *outs, *streamed])
         results = pl.pallas_call(
             kernel,
             grid=(1,),
@@ -90,23 +90,50 @@
         copy.wait()
 
 
-def send_body(turn_ref, a_ref, b_ref, basis_ref, send_ref, rows_ref):
-    pick(turn_ref[0], b_ref, a_ref, rows_ref)
+def load_send_body(turn_ref, basis_ref, a_ref, b_ref, held, send_ref, rows_ref, sem, sems):
+    blocks = fetch(basis_ref, held, sems)
+    pick(turn_ref[0], b_ref, a_ref, rows_ref, sem)
+    total = None
+    for rows, copy in blocks:
+        copy.wait()
+        value = dot(rows_ref[:, rows], held[rows, :])
+        total = value if total is None else total + value
+    send_ref[...] = total.astype(NARROW)
+
+
+def fetch(source, held, sems):
+    count = sems.shape[0]
+    size = source.shape[0] // count
+    found = []
+    for k in range(count):
+        rows = pl.ds(k * size, size)
+        copy = pltpu.make_async_copy(source.at[rows], held.at[rows], sems.at[k])
+        copy.start()
+        found.append((rows, copy))
+    return found
+
+
+def send_body(turn_ref, basis_ref, a_ref, b_ref, send_ref, rows_ref, sem):
+    pick(turn_ref[0], b_ref, a_ref, rows_ref, sem)
     send_ref[...] = dot(rows_ref[...], basis_ref[...]).astype(NARROW)
 
 
-def pick(turn, zero_ref, one_ref, rows_ref):
+def pick(turn, zero_ref, one_ref, rows_ref, sem):
     @pl.when(turn == 0)
     def _():
-        rows_ref[...] = zero_ref[...]
+        copy = pltpu.make_async_copy(zero_ref, rows_ref, sem)
+        copy.start()
+        copy.wait()
 
     @pl.when(turn == 1)
     def _():
-        rows_ref[...] = one_ref[...]
-
-
-def pair_body(turn_ref, a_ref, b_ref, basis_ref, got_ref, out_ref, rows_ref):
-    pick(turn_ref[0], a_ref, b_ref, rows_ref)
+        copy = pltpu.make_async_copy(one_ref, rows_ref, sem)
+        copy.start()
+        copy.wait()
+
+
+def pair_body(turn_ref, basis_ref, got_ref, a_ref, b_ref, out_ref, rows_ref, sem):
+    pick(turn_ref[0], a_ref, b_ref, rows_ref, sem)
     out_ref[...] = (dot(rows_ref[...], basis_ref[...]) + got_ref[...].astype(WIDE)).astype(NARROW)
 
 
@@ -122,7 +149,7 @@
     out_ref[...] = (a_ref[...].astype(WIDE) + b_ref[...].astype(WIDE)).astype(NARROW)
 
 
-def rotate_body(place_ref, b0, b1, b2, b3, basis_ref, mine_ref, top_ref, low_ref, rows_ref):
+def rotate_body(place_ref, b0, b1, b2, b3, basis_ref, mine_top, mine_low, top_ref, low_ref, rows_ref):
     size = b0.shape[0]
     half = 2 * size
     for k, block in enumerate((b0, b1, b2, b3)):
@@ -131,23 +158,25 @@
     other = dot(rows_ref[pl.ds(pl.multiple_of((1 - core) * half, half), half), :], basis_ref[...])
     top_ref[...] = other[:size].astype(NARROW)
     low_ref[...] = other[size:].astype(NARROW)
-    mine_ref[...] = dot(rows_ref[pl.ds(pl.multiple_of(core * half, half), half), :], basis_ref[...])
-
-
-def chip_sum_body(core_ref, mine_ref, top_pair, low_pair, wide_ref, top_out, low_out):
-    size = top_out.shape[0]
+    mine = dot(rows_ref[pl.ds(pl.multiple_of(core * half, half), half), :], basis_ref[...])
+    mine_top[...] = mine[:size]
+    mine_low[...] = mine[size:]
+
+
+def chip_sum_body(core_ref, mine_ref, pair_ref, *refs):
+    given = (len(refs) - 2) // 2
+    wide_ref, out_ref = refs[given], refs[given + 1]
+    size = out_ref.shape[0]
     source = pl.ds(pl.multiple_of((1 - core_ref[0]) * size, size), size)
-    for k, (pair, out) in enumerate(((top_pair, top_out), (low_pair, low_out))):
-        rows = slice(k * size, (k + 1) * size)
-        value = mine_ref[rows, :] + pair[source, :].astype(WIDE)
-        wide_ref[rows, :] = value
-        out[...] = value.astype(NARROW)
-
-
-def panel_sum_body(wide_ref, top_ref, low_ref, top_out, low_out):
-    half = top_ref.shape[0]
-    top_out[...] = (wide_ref[:half, :] + top_ref[...].astype(WIDE)).astype(NARROW)
-    low_out[...] = (wide_ref[half:, :] + low_ref[...].astype(WIDE)).astype(NARROW)
+    value = mine_ref[...] + pair_ref[source, :].astype(WIDE)
+    wide_ref[...] = value
+    out_ref[...] = value.astype(NARROW)
+    for k in range(given):
+        refs[given + 2 + k][...] = refs[k][...]
+
+
+def panel_sum_body(wide_ref, got_ref, out_ref):
+    out_ref[...] = (wide_ref[...] + got_ref[...].astype(WIDE)).astype(NARROW)
 
 
 def score_body(
@@ -155,7 +184,8 @@
     act_ref, grad_ref, query_buf, eig_buf, sems
 ):
     depth, queries, cols = query_ref.shape
-    tokens = out_ref.shape[1]
+    owners = out_ref.shape[0]
+    tokens = 4 * a0.shape[0]
     count = depth // LANES
 
     def copies(k):
@@ -208,7 +238,14 @@
     while shift >= queries:
         total = total + pltpu.roll(total, shift, 1)
         shift //= 2
-    out_ref[...] = total.T[:queries, :]
+    turned = total.T[:queries, :]
+    owned = tokens // owners
+    for k in range(owners):
+        out_ref[k, :, :owned] = turned[:, k * owned : (k + 1) * owned]
+
+
+def final_body(got_ref, out_ref):
+    out_ref[...] = jnp.sum(got_ref[...], axis=0)[:, : out_ref.shape[1]]
 
 
 def spread_out(partial):
@@ -225,16 +262,16 @@
     core, turn = panel % 2, tok % 2
     steps = Steps()
 
-    def wide(rows, width):
-        return jax.ShapeDtypeStruct((rows, width), WIDE)
-
-    def narrow(rows, width):
-        return jax.ShapeDtypeStruct((rows, width), NARROW)
+    def wide(*shape):
+        return jax.ShapeDtypeStruct(shape, WIDE)
+
+    def narrow(*shape):
+        return jax.ShapeDtypeStruct(shape, NARROW)
 
     def scalars(*values):
         return jnp.stack(values).astype(jnp.int32)
 
-    g1, g3 = swap(grads, "tok", 1), swap(grads, "tok", 3)
+    g1, g3 = swap(grads, "tok", 1), swap(grads, "tok", 2)
     near = swap(acts, "panel", 1)
     far = swap(acts, "panel", 2)
     most = swap(acts, "panel", 3)
@@ -245,51 +282,54 @@
             scratch=[pltpu.SemaphoreType.DMA((len(arrays),))], streamed=arrays,
         )
 
-    (in_basis,) = loaded("load_in", in_basis)
-    one = [pltpu.VMEM((size, feats), NARROW)]
+    one = [pltpu.VMEM((size, feats), NARROW), pltpu.SemaphoreType.DMA]
     cost = 2 * size * feats * cols
-    (send1,) = steps(
-        "send_near", send_body, [acts, near, in_basis], [narrow(size, cols)], scalars=scalars(turn), scratch=one, flops=cost
+    options = dict(scalars=scalars(turn), scratch=one, flops=cost)
+    acts = pltpu.with_memory_space_constraint(acts, pltpu.HBM)
+    in_basis, send1 = steps(
+        "send_near", load_send_body, [], [narrow(*in_basis.shape), narrow(size, cols)], scalars=scalars(turn),
+        scratch=one + [pltpu.SemaphoreType.DMA((4,))], flops=cost, streamed=[in_basis], where=[acts, pltpu.with_memory_space_constraint(near, pltpu.HBM)],
     )
     got1 = swap(send1, "tok", 1)
-    (send2,) = steps(
-        "send_far", send_body, [far, most, in_basis], [narrow(size, cols)], scalars=scalars(turn), scratch=one, flops=cost
-    )
-    got2 = swap(send2, "tok", 1)
     (g3,) = steps("pass", pass_body, [g3], [narrow(size, feats)], after=[g1])
     g2 = swap(g3, "tok", 1)
-    (pair1,) = steps(
-        "pair_near", pair_body, [acts, near, in_basis, got1], [narrow(size, cols)], scalars=scalars(turn), scratch=one, flops=cost
-    )
+    (send2,) = steps("send_far", send_body, [in_basis], [narrow(size, cols)], where=[far, most], **options)
+    got2 = swap(send2, "tok", 1)
+    (pair1,) = steps("pair_near", pair_body, [in_basis, got1], [narrow(size, cols)], where=[acts, pltpu.with_memory_space_constraint(near, pltpu.HBM)], **options)
     got1 = swap(pair1, "tok", 2)
-    (pair2,) = steps(
-        "pair_far", pair_body, [far, most, in_basis, got2], [narrow(size, cols)], scalars=scalars(turn), scratch=one, flops=cost
-    )
-    got2 = swap(pair2, "tok", 2)
     (out_basis,) = loaded("load_out", out_basis)
-    mine, top, low = steps(
-        "rotate", rotate_body, [grads, g1, g3, g2, out_basis],
-        [wide(2 * size, depth), narrow(size, depth), narrow(size, depth)],
-        scalars=scalars(tok, tok ^ 1, tok ^ 3, tok ^ 2, core),
+    mine_top, mine_low, top, low = steps(
+        "rotate", rotate_body, [grads, g1, g3, g2, out_basis], [wide(size, depth)] * 2 + [narrow(size, depth)] * 2,
+        scalars=scalars(tok, tok ^ 1, tok ^ 2, tok ^ 3, core),
         scratch=[pltpu.VMEM((4 * size, feats), NARROW)], flops=8 * size * feats * depth,
     )
+    (pair2,) = steps("pair_far", pair_body, [in_basis, got2], [narrow(size, cols)], where=[far, most], **options)
+    got2 = swap(pair2, "tok", 2)
     chips = [[2 * k, 2 * k + 1] for k in range(2)]
-    top, low = (lax.all_gather(x, "panel", axis=0, tiled=True, axis_index_groups=chips) for x in (top, low))
-    mine, top, low = steps(
-        "chip_sum", chip_sum_body, [mine, top, low],
-        [wide(2 * size, depth), narrow(size, depth), narrow(size, depth)], scalars=scalars(core),
-    )
-    top, low = swap(top, "panel", 2), swap(low, "panel", 2)
+
+    def chip_sum(name, mine, other, *handed):
+        both = lax.all_gather(other, "panel", axis=0, tiled=True, axis_index_groups=chips)
+        mine, other, *handed = steps(
+            name, chip_sum_body, [mine, both, *handed],
+            [wide(size, depth), narrow(size, depth)] + [narrow(size, depth)] * len(handed), scalars=scalars(core),
+        )
+        return mine, swap(other, "panel", 2), *handed
+
+    mine_top, top, low = chip_sum("chip_sum_top", mine_top, top, low)
     (total1,) = steps("total_near", add_body, [pair1, got1], [narrow(size, cols)])
     back1 = swap(total1, "tok", 1)
+    mine_low, low = chip_sum("chip_sum_low", mine_low, low)
     (total2,) = steps("total_far", add_body, [pair2, got2], [narrow(size, cols)])
     back2 = swap(total2, "tok", 1)
-    mine_top, mine_low = steps("panel_sum", panel_sum_body, [mine, top, low], [narrow(size, depth)] * 2)
-    other_top, other_low = swap(mine_top, "panel", 1), swap(mine_low, "panel", 1)
+    (mine_top,) = steps("panel_sum_top", panel_sum_body, [mine_top, top], [narrow(size, depth)], weight=8_000_000)
+    other_top = swap(mine_top, "panel", 1)
+    (mine_low,) = steps("panel_sum_low", panel_sum_body, [mine_low, low], [narrow(size, depth)])
+    other_low = swap(mine_low, "panel", 1)
     steps("mark", mark_body, [], [wide(8, LANES)], after=[back1, back2])
+    owners = lax.axis_size("panel") * lax.axis_size("tok")
     (partial,) = steps(
         "scores", score_body, [total1, back1, total2, back2, mine_top, mine_low, other_top, other_low],
-        [wide(queries, 4 * size)],
+        [wide(owners, queries, LANES)],
         scalars=scalars(panel ^ turn, panel ^ turn ^ 1, panel ^ turn ^ 2, panel ^ turn ^ 3, core),
         scratch=[
             pltpu.VMEM((4 * size, cols), NARROW),
@@ -300,7 +340,9 @@
         ],
         room=28 * 1024 * 1024, flops=8 * size * depth * queries * cols, streamed=[query_rot, eigvals],
     )
-    return jnp.sum(spread_out(partial), axis=0).T
+    got = lax.all_to_all(partial, ("panel", "tok"), split_axis=0, concat_axis=0, tiled=True)
+    (out,) = steps("final", final_body, [got], [wide(queries, 4 * size // owners)])
+    return out.T
 
 
 def any_score_kernel(query_ref, eig_ref, act_ref, grad_ref, out_ref, act_turned, grad_turned):

time: 92.5 us -> 89.3 us (0.965)
  waiting for transfers between devices: 24.3 us -> 21.2 us
  other arithmetic: 1.3 us -> 0 us
  blocking collectives: 14.1 us -> 15.2 us
  starting transfers between devices: 14.9 us -> 15.9 us
    ppermute x16, waiting for transfers between devices: 24.3 us -> 21.2 us  [swap(): lax.ppermute(value, axis, [(i, i ^ mask) for i in range(lax.axis_size(axi...]
    all_to_all x1, blocking collectives: 9.76 us -> 10.9 us  [on_lines_of_four(): lax.all_to_all(partial, ('panel', 'tok'), split_axis=0, concat_axis=0, ti...]
    ppermute x16, starting transfers between devices: 14.9 us -> 15.9 us  [swap(): lax.ppermute(value, axis, [(i, i ^ mask) for i in range(lax.axis_size(axi...]
    pallas_call x14 -> x16, Pallas kernels: 34.4 us -> 33.8 us  [__call__(): pl.pallas_call(kernel, grid=(1,), in_specs=specs, out_specs=[block(x) for...]
    unnamed x16 -> x10, local copies, waits for them, and re-layouts: 2.09 us -> 2.34 us
  transfers between devices with their start and end apart: 16 -> 16, of which waited for: 10 -> 7; matrix products, arithmetic and copies ran while one was open for 0% -> 0% of each run, Pallas kernels for 20% -> 19%
where the time goes in v4:
time: 89.3 us; the launch traced here: 88.9 us
  Pallas kernels  33.8 us (38%)
  waiting for transfers between devices  21.2 us (24%)
  starting transfers between devices  15.9 us (18%)
  blocking collectives  15.2 us (17%)
  local copies, waits for them, and re-layouts  2.51 us (3%)
    pallas_call x16, Pallas kernels, __call__(): pl.pallas_call(kernel, grid=(1,), in_specs=specs, out_specs=[block(x) for...  33.8 us
    ppermute x16, waiting for transfers between devices, swap(): lax.ppermute(value, axis, [(i, i ^ mask) for i in range(lax.axis_size(axi...  21.2 us
    ppermute x16, starting transfers between devices, swap(): lax.ppermute(value, axis, [(i, i ^ mask) for i in range(lax.axis_size(axi...  15.9 us
    all_to_all x1, blocking collectives, on_lines_of_four(): lax.all_to_all(partial, ('panel', 'tok'), split_axis=0, concat_axis=0, ti...  10.9 us
    all_gather x2, blocking collectives, chip_sum(): lax.all_gather(other, 'panel', axis=0, tiled=True, axis_index_groups=chips)  4.32 us
    unnamed x10, local copies, waits for them, and re-layouts  2.34 us
  transfers between devices with their start and end apart: 16, of which 7 were waited for; matrix products, arithmetic and copies ran while one was open for 0% of the time, Pallas kernels for 19%

profile of v4, /device:TPU:0, one launch (start us, length us, event | category | flops | bytes accessed | tf_op | source)
XLA Modules:
  0.0 88.9 jit_solution(935611244551208028)
XLA Ops:
  0.5 2.6 %collective-permute-start.5 = (bf16[96,1280]{1,0:T(8,128)(2,1)}, bf16[96,1280]{1,0:T(8,128)(2,1)S(1)}, u32[]{:S(2)}, u32[]{:S(2)}) collective-permute-start(bf16[96,1280]{1,0:T(8,128)(2,1)} %refs_1_.3), channel_id=1, source_target_pairs={{0,1},{1,0},{2,3},{3,2},{4,5},{5,4},{6,7},{7,6},{8,9},{9,8},{10,11... | collective-permute-start | bytes 737288 | tf_op jit(solution)/shard_map/ppermute | solution.py:24
  3.0 2.6 %collective-permute-start.4 = (bf16[96,1280]{1,0:T(8,128)(2,1)}, bf16[96,1280]{1,0:T(8,128)(2,1)}, u32[]{:S(2)}, u32[]{:S(2)}) collective-permute-start(bf16[96,1280]{1,0:T(8,128)(2,1)} %refs_1_.3), channel_id=1, source_target_pairs={{0,2},{1,3},{2,0},{3,1},{4,6},{5,7},{6,4},{7,5},{8,10},{9,11},{10,... | collective-permute-start | bytes 737288 | tf_op jit(solution)/shard_map/ppermute | solution.py:24
  5.6 1.5 %collective-permute-start.2 = (bf16[96,1280]{1,0:T(8,128)(2,1)}, bf16[96,1280]{1,0:T(8,128)(2,1)}, u32[]{:S(2)}, u32[]{:S(2)}) collective-permute-start(bf16[96,1280]{1,0:T(8,128)(2,1)} %refs_3_.1), channel_id=1, source_target_pairs={{0,8},{4,12},{8,0},{12,4},{1,9},{5,13},{9,1},{13,5},{2,10},{6,14},... | collective-permute-start | bytes 737288 | tf_op jit(solution)/shard_map/ppermute | solution.py:24
  7.1 0.7 copy-done.4
  7.8 3.8 %send_near.1 = (bf16[1280,1280]{1,0:T(8,128)(2,1)S(1)}, bf16[96,1280]{1,0:T(8,128)(2,1)}) custom-call(s32[1]{0:T(128)} %bitcast.5.refs_0_, bf16[1280,1280]{1,0:T(8,128)(2,1)} %refs_1_.2, bf16[96,1280]{1,0:T(8,128)(2,1)} %refs_3_.1, bf16[96,1280]{1,0:T(8,128)(2,1)} %copy-done.4), custom_call_target="tpu_custom_call" | custom-call | flops 314572800 | bytes 6799360 | tf_op jit(solution)/shard_map/send_near/pallas_call | solution.py:68
  11.6 0.5 collective-permute-start.1
  12.1 2.9 %collective-permute-done.5.refs_1_.refs_2_ = bf16[96,1280]{1,0:T(8,128)(2,1)S(1)} collective-permute-done((bf16[96,1280]{1,0:T(8,128)(2,1)}, bf16[96,1280]{1,0:T(8,128)(2,1)S(1)}, u32[]{:S(2)}, u32[]{:S(2)}) %collective-permute-start.5) | collective-permute-done | bytes 245792 | tf_op jit(solution)/shard_map/ppermute | solution.py:24
  15.0 0.7 copy-done
  15.7 1.8 %collective-permute-done.4.refs_0_ = bf16[96,1280]{1,0:T(8,128)(2,1)} collective-permute-done((bf16[96,1280]{1,0:T(8,128)(2,1)}, bf16[96,1280]{1,0:T(8,128)(2,1)}, u32[]{:S(2)}, u32[]{:S(2)}) %collective-permute-start.4) | collective-permute-done | bytes 245792 | tf_op jit(solution)/shard_map/ppermute | solution.py:24
  17.5 0.9 %copy-done.1 = bf16[96,1280]{1,0:T(8,128)(2,1)S(1)} copy-done((bf16[96,1280]{1,0:T(8,128)(2,1)S(1)}, bf16[96,1280]{1,0:T(8,128)(2,1)}, u32[]{:S(2)}) %copy-start.1) | copy-done | bytes 245784
  18.4 1.0 %pass.1.refs_4_.refs_3_ = bf16[96,1280]{1,0:T(8,128)(2,1)S(1)} custom-call(bf16[96,1280]{1,0:T(8,128)(2,1)} %collective-permute-done.4.refs_0_, bf16[96,1280]{1,0:T(8,128)(2,1)S(1)} %copy-done.1, bf16[96,1280]{1,0:T(8,128)(2,1)} %get-tuple-element.17.refs_2_), custom_call_target="tpu_custom_call" | custom-call | bytes 491520 | tf_op jit(solution)/shard_map/pass/pallas_call | solution.py:68
  19.4 1.0 %collective-permute-start.7 = (bf16[96,1280]{1,0:T(8,128)(2,1)S(1)}, bf16[96,1280]{1,0:T(8,128)(2,1)}, u32[]{:S(2)}, u32[]{:S(2)}) collective-permute-start(bf16[96,1280]{1,0:T(8,128)(2,1)S(1)} %pass.1.refs_4_.refs_3_), channel_id=1, source_target_pairs={{0,1},{1,0},{2,3},{3,2},{4,5},{5,4},{6,7},{7,6},{8,9},{9,8},{10,11... | collective-permute-start | bytes 737288 | tf_op jit(solution)/shard_map/ppermute | solution.py:24
  20.4 2.3 %send_far.1.refs_5_ = bf16[96,1280]{1,0:T(8,128)(2,1)} custom-call(s32[1]{0:T(128)} %bitcast.5.refs_0_, bf16[1280,1280]{1,0:T(8,128)(2,1)S(1)} %get-tuple-element.16.refs_1_, bf16[96,1280]{1,0:T(8,128)(2,1)} %collective-permute-done.2.refs_2_.refs_3_, bf16[96,1280]{1,0:T(8,128)(2,1)} %collective-permute-done.3.refs_3_.refs_4_, ...), custom_call_target="tpu_custom_call" | custom-call | flops 314572800 | bytes 3522560 | tf_op jit(solution)/shard_map/send_far/pallas_call | solution.py:68
  22.8 1.1 %collective-permute-start.8 = (bf16[96,1280]{1,0:T(8,128)(2,1)}, bf16[96,1280]{1,0:T(8,128)(2,1)}, u32[]{:S(2)}, u32[]{:S(2)}) collective-permute-start(bf16[96,1280]{1,0:T(8,128)(2,1)} %send_far.1.refs_5_), channel_id=1, source_target_pairs={{0,1},{1,0},{2,3},{3,2},{4,5},{5,4},{6,7},{7,6},{8,9},{9,8},{10,11... | collective-permute-start | bytes 737288 | tf_op jit(solution)/shard_map/ppermute | solution.py:24
  24.0 2.6 %pair_near.1.refs_1_.refs_0_ = bf16[96,1280]{1,0:T(8,128)(2,1)S(1)} custom-call(s32[1]{0:T(128)} %bitcast.5.refs_0_, bf16[1280,1280]{1,0:T(8,128)(2,1)S(1)} %get-tuple-element.16.refs_1_, bf16[96,1280]{1,0:T(8,128)(2,1)} %collective-permute-done.1.refs_2_, bf16[96,1280]{1,0:T(8,128)(2,1)} %refs_3_.1, bf16[96,1280]{1,0:T(8,128)(2,1)} %copy-done.4, ...), custom_call_target="tpu_custom_call" | custom-call | flops 314572800 | bytes 3768320 | tf_op jit(solution)/shard_map/pair_near/pallas_call | solution.py:68
  26.6 1.4 %collective-permute-start.6 = (bf16[96,1280]{1,0:T(8,128)(2,1)S(1)}, bf16[96,1280]{1,0:T(8,128)(2,1)S(1)}, u32[]{:S(2)}, u32[]{:S(2)}) collective-permute-start(bf16[96,1280]{1,0:T(8,128)(2,1)S(1)} %pair_near.1.refs_1_.refs_0_), channel_id=1, source_target_pairs={{0,2},{1,3},{2,0},{3,1},{4,6},{5,7},{6,4},{7,5},{8,10},{9,11},{10,... | collective-permute-start | bytes 737288 | tf_op jit(solution)/shard_map/ppermute | solution.py:24
  28.0 1.9 %load_out.1.refs_5_.refs_6_ = bf16[1280,1280]{1,0:T(8,128)(2,1)S(1)} custom-call(bf16[1280,1280]{1,0:T(8,128)(2,1)} %refs_0_.1, bf16[96,1280]{1,0:T(8,128)(2,1)S(1)} %pair_near.1.refs_1_.refs_0_), custom_call_target="tpu_custom_call" | custom-call | bytes 6553600 | tf_op jit(solution)/shard_map/load_out/pallas_call | solution.py:68
  29.9 2.4 %rotate.1 = (f32[96,1280]{1,0:T(8,128)S(1)}, f32[96,1280]{1,0:T(8,128)S(1)}, bf16[96,1280]{1,0:T(8,128)(2,1)S(1)}, bf16[96,1280]{1,0:T(8,128)(2,1)S(1)}) custom-call(s32[5]{0:T(128)S(1)} %stack.51.refs_0_, bf16[96,1280]{1,0:T(8,128)(2,1)S(1)} %copy-done.3, bf16[96,1280]{1,0:T(8,128)(2,1)S(1)} %copy-done.2, bf16[96,1280]{1,0:T(8,128)(2,1)S(1)} %pass.1.refs_4_.refs_3_, ...), custom_call_target="tpu_custom_call" | custom-call | flops 1258291200 | bytes 5734400 | tf_op jit(solution)/shard_map/rotate/pallas_call | solution.py:68
  32.4 3.7 %collective-permute-done.8.refs_2_ = bf16[96,1280]{1,0:T(8,128)(2,1)} collective-permute-done((bf16[96,1280]{1,0:T(8,128)(2,1)}, bf16[96,1280]{1,0:T(8,128)(2,1)}, u32[]{:S(2)}, u32[]{:S(2)}) %collective-permute-start.8) | collective-permute-done | bytes 245792 | tf_op jit(solution)/shard_map/ppermute | solution.py:24
  36.0 2.6 %pair_far.1.refs_4_.refs_0_ = bf16[96,1280]{1,0:T(8,128)(2,1)S(1)} custom-call(s32[1]{0:T(128)} %bitcast.5.refs_0_, bf16[1280,1280]{1,0:T(8,128)(2,1)S(1)} %get-tuple-element.16.refs_1_, bf16[96,1280]{1,0:T(8,128)(2,1)} %collective-permute-done.8.refs_2_, bf16[96,1280]{1,0:T(8,128)(2,1)} %collective-permute-done.2.refs_2_.refs_3_, ...), custom_call_target="tpu_custom_call" | custom-call | flops 314572800 | bytes 3768320 | tf_op jit(solution)/shard_map/pair_far/pallas_call | solution.py:68
  38.7 2.2 %all_gather.6.refs_2_ = bf16[192,1280]{1,0:T(8,128)(2,1)S(1)} all-gather(bf16[96,1280]{1,0:T(8,128)(2,1)S(1)} %get-tuple-element.19), channel_id=1, replica_groups={{0,4},{8,12},{1,5},{9,13},{2,6},{10,14},{3,7},{11,15},{16,20},{24,28},{..., dimensions={0}, use_global_device_ids=true | all-gather | bytes 737280 | tf_op jit(solution)/shard_map/all_gather | solution.py:311
  40.9 2.2 %all_gather.7.refs_2_ = bf16[192,1280]{1,0:T(8,128)(2,1)S(1)} all-gather(bf16[96,1280]{1,0:T(8,128)(2,1)S(1)} %get-tuple-element.21.refs_2_), channel_id=1, replica_groups={{0,4},{8,12},{1,5},{9,13},{2,6},{10,14},{3,7},{11,15},{16,20},{24,28},{..., dimensions={0}, use_global_device_ids=true | all-gather | bytes 737280 | tf_op jit(solution)/shard_map/all_gather | solution.py:311
  43.1 1.5 %collective-permute-start.12 = (bf16[96,1280]{1,0:T(8,128)(2,1)S(1)}, bf16[96,1280]{1,0:T(8,128)(2,1)S(1)}, u32[]{:S(2)}, u32[]{:S(2)}) collective-permute-start(bf16[96,1280]{1,0:T(8,128)(2,1)S(1)} %get-tuple-element.25), channel_id=1, source_target_pairs={{0,8},{4,12},{8,0},{12,4},{1,9},{5,13},{9,1},{13,5},{2,10},{6,14},... | collective-permute-start | bytes 737288 | tf_op jit(solution)/shard_map/ppermute | solution.py:24
  44.7 0.6 collective-permute-start.13
  45.3 2.4 %collective-permute-start.9 = (bf16[96,1280]{1,0:T(8,128)(2,1)S(1)}, bf16[96,1280]{1,0:T(8,128)(2,1)S(1)}, u32[]{:S(2)}, u32[]{:S(2)}) collective-permute-start(bf16[96,1280]{1,0:T(8,128)(2,1)S(1)} %total_near.1.refs_3_.refs_1_), channel_id=1, source_target_pairs={{0,1},{1,0},{2,3},{3,2},{4,5},{5,4},{6,7},{7,6},{8,9},{9,8},{10,11... | collective-permute-start | bytes 737288 | tf_op jit(solution)/shard_map/ppermute | solution.py:24
  47.7 2.9 %collective-permute-done.10.refs_1_ = bf16[96,1280]{1,0:T(8,128)(2,1)S(1)} collective-permute-done((bf16[96,1280]{1,0:T(8,128)(2,1)S(1)}, bf16[96,1280]{1,0:T(8,128)(2,1)S(1)}, u32[]{:S(2)}, u32[]{:S(2)}) %collective-permute-start.10) | collective-permute-done | bytes 245792 | tf_op jit(solution)/shard_map/ppermute | solution.py:24
  50.8 1.1 %collective-permute-done.12.refs_1_ = bf16[96,1280]{1,0:T(8,128)(2,1)S(1)} collective-permute-done((bf16[96,1280]{1,0:T(8,128)(2,1)S(1)}, bf16[96,1280]{1,0:T(8,128)(2,1)S(1)}, u32[]{:S(2)}, u32[]{:S(2)}) %collective-permute-start.12) | collective-permute-done | bytes 245792 | tf_op jit(solution)/shard_map/ppermute | solution.py:24
  52.0 4.3 %collective-permute-done.13.refs_1_ = bf16[96,1280]{1,0:T(8,128)(2,1)S(1)} collective-permute-done((bf16[96,1280]{1,0:T(8,128)(2,1)S(1)}, bf16[96,1280]{1,0:T(8,128)(2,1)S(1)}, u32[]{:S(2)}, u32[]{:S(2)}) %collective-permute-start.13) | collective-permute-done | bytes 245792 | tf_op jit(solution)/shard_map/ppermute | solution.py:24
  56.6 4.5 %collective-permute-done.11.refs_1_.refs_4_ = bf16[96,1280]{1,0:T(8,128)(2,1)S(1)} collective-permute-done((bf16[96,1280]{1,0:T(8,128)(2,1)S(1)}, bf16[96,1280]{1,0:T(8,128)(2,1)S(1)}, u32[]{:S(2)}, u32[]{:S(2)}) %collective-permute-start.11) | collective-permute-done | bytes 245792 | tf_op jit(solution)/shard_map/ppermute | solution.py:24
  61.1 16.2 %scores.1.refs_1_ = f32[16,8,128]{2,1,0:T(8,128)S(1)} custom-call(s32[5]{0:T(128)S(1)} %stack.45.refs_0_, bf16[96,1280]{1,0:T(8,128)(2,1)S(1)} %total_near.1.refs_3_.refs_1_, bf16[96,1280]{1,0:T(8,128)(2,1)S(1)} %collective-permute-done.9.refs_0_.refs_2_, bf16[96,1280]{1,0:T(8,128)(2,1)S(1)} %total_far.1.refs_2_.refs_3_, ...), custom_call_target="tpu_custom_call" | custom-call | flops 10066329600 | bytes 34799616 | tf_op jit(solution)/shard_map/scores/pallas_call | solution.py:68
  77.3 10.9 %all_to_all.5.refs_0_ = f32[16,8,128]{2,1,0:T(8,128)S(1)} all-to-all(f32[16,8,128]{2,1,0:T(8,128)S(1)} %scores.1.refs_1_), channel_id=1, replica_groups=mesh['groups'=2,'panel'=4,'tok'=4] {'panel','tok'}, dimensions={0} | all-to-all | bytes 131072 | tf_op jit(solution)/shard_map/all_to_all | solution.py:343
  88.3 0.6 final.1
  (31 shorter events, 1.3 us)
Async XLA Ops:
  0.0 7.1 %collective-permute-start = (bf16[96,1280]{1,0:T(8,128)(2,1)}, bf16[96,1280]{1,0:T(8,128)(2,1)S(1)}, u32[]{:S(2)}, u32[]{:S(2)}) collective-permute-start(bf16[96,1280]{1,0:T(8,128)(2,1)} %refs_3_.1), channel_id=1, source_target_pairs={{0,4},{4,0},{8,12},{12,8},{1,5},{5,1},{9,13},{13,9},{2,6},{6,2},{1... | collective-permute-start | bytes 737288 | tf_op jit(solution)/shard_map/ppermute | solution.py:24
  0.5 14.5 %collective-permute-start.5 = (bf16[96,1280]{1,0:T(8,128)(2,1)}, bf16[96,1280]{1,0:T(8,128)(2,1)S(1)}, u32[]{:S(2)}, u32[]{:S(2)}) collective-permute-start(bf16[96,1280]{1,0:T(8,128)(2,1)} %refs_1_.3), channel_id=1, source_target_pairs={{0,1},{1,0},{2,3},{3,2},{4,5},{5,4},{6,7},{7,6},{8,9},{9,8},{10,11... | collective-permute-start | bytes 737288 | tf_op jit(solution)/shard_map/ppermute | solution.py:24
  3.0 14.4 %collective-permute-start.4 = (bf16[96,1280]{1,0:T(8,128)(2,1)}, bf16[96,1280]{1,0:T(8,128)(2,1)}, u32[]{:S(2)}, u32[]{:S(2)}) collective-permute-start(bf16[96,1280]{1,0:T(8,128)(2,1)} %refs_1_.3), channel_id=1, source_target_pairs={{0,2},{1,3},{2,0},{3,1},{4,6},{5,7},{6,4},{7,5},{8,10},{9,11},{10,... | collective-permute-start | bytes 737288 | tf_op jit(solution)/shard_map/ppermute | solution.py:24
  5.6 14.8 %collective-permute-start.2 = (bf16[96,1280]{1,0:T(8,128)(2,1)}, bf16[96,1280]{1,0:T(8,128)(2,1)}, u32[]{:S(2)}, u32[]{:S(2)}) collective-permute-start(bf16[96,1280]{1,0:T(8,128)(2,1)} %refs_3_.1), channel_id=1, source_target_pairs={{0,8},{4,12},{8,0},{12,4},{1,9},{5,13},{9,1},{13,5},{2,10},{6,14},... | collective-permute-start | bytes 737288 | tf_op jit(solution)/shard_map/ppermute | solution.py:24
  7.1 13.3 %collective-permute-start.3 = (bf16[96,1280]{1,0:T(8,128)(2,1)}, bf16[96,1280]{1,0:T(8,128)(2,1)}, u32[]{:S(2)}, u32[]{:S(2)}) collective-permute-start(bf16[96,1280]{1,0:T(8,128)(2,1)} %refs_3_.1), channel_id=1, source_target_pairs={{0,12},{4,8},{8,4},{12,0},{1,13},{5,9},{9,5},{13,1},{2,14},{6,10},... | collective-permute-start | bytes 737288 | tf_op jit(solution)/shard_map/ppermute | solution.py:24
  7.1 0.7 copy-start.4
  11.6 12.4 %collective-permute-start.1 = (bf16[96,1280]{1,0:T(8,128)(2,1)}, bf16[96,1280]{1,0:T(8,128)(2,1)}, u32[]{:S(2)}, u32[]{:S(2)}) collective-permute-start(bf16[96,1280]{1,0:T(8,128)(2,1)} %get-tuple-element.17.refs_2_), channel_id=1, source_target_pairs={{0,1},{1,0},{2,3},{3,2},{4,5},{5,4},{6,7},{7,6},{8,9},{9,8},{10,11... | collective-permute-start | bytes 737288 | tf_op jit(solution)/shard_map/ppermute | solution.py:24
  15.0 0.7 copy-start
  17.5 0.9 %copy-start.1 = (bf16[96,1280]{1,0:T(8,128)(2,1)S(1)}, bf16[96,1280]{1,0:T(8,128)(2,1)}, u32[]{:S(2)}) copy-start(bf16[96,1280]{1,0:T(8,128)(2,1)} %copy-done) | copy-start | bytes 737284
  19.4 10.5 %collective-permute-start.7 = (bf16[96,1280]{1,0:T(8,128)(2,1)S(1)}, bf16[96,1280]{1,0:T(8,128)(2,1)}, u32[]{:S(2)}, u32[]{:S(2)}) collective-permute-start(bf16[96,1280]{1,0:T(8,128)(2,1)S(1)} %pass.1.refs_4_.refs_3_), channel_id=1, source_target_pairs={{0,1},{1,0},{2,3},{3,2},{4,5},{5,4},{6,7},{7,6},{8,9},{9,8},{10,11... | collective-permute-start | bytes 737288 | tf_op jit(solution)/shard_map/ppermute | solution.py:24
  22.8 13.3 %collective-permute-start.8 = (bf16[96,1280]{1,0:T(8,128)(2,1)}, bf16[96,1280]{1,0:T(8,128)(2,1)}, u32[]{:S(2)}, u32[]{:S(2)}) collective-permute-start(bf16[96,1280]{1,0:T(8,128)(2,1)} %send_far.1.refs_5_), channel_id=1, source_target_pairs={{0,1},{1,0},{2,3},{3,2},{4,5},{5,4},{6,7},{7,6},{8,9},{9,8},{10,11... | collective-permute-start | bytes 737288 | tf_op jit(solution)/shard_map/ppermute | solution.py:24
  26.5 3.4 %copy-start.2 = (bf16[96,1280]{1,0:T(8,128)(2,1)S(1)}, bf16[96,1280]{1,0:T(8,128)(2,1)}, u32[]{:S(2)}) copy-start(bf16[96,1280]{1,0:T(8,128)(2,1)} %copy-done) | copy-start | bytes 737284
  26.5 3.4 %copy-start.3 = (bf16[96,1280]{1,0:T(8,128)(2,1)S(1)}, bf16[96,1280]{1,0:T(8,128)(2,1)}, u32[]{:S(2)}) copy-start(bf16[96,1280]{1,0:T(8,128)(2,1)} %refs_1_.3) | copy-start | bytes 737284
  26.6 18.0 %collective-permute-start.6 = (bf16[96,1280]{1,0:T(8,128)(2,1)S(1)}, bf16[96,1280]{1,0:T(8,128)(2,1)S(1)}, u32[]{:S(2)}, u32[]{:S(2)}) collective-permute-start(bf16[96,1280]{1,0:T(8,128)(2,1)S(1)} %pair_near.1.refs_1_.refs_0_), channel_id=1, source_target_pairs={{0,2},{1,3},{2,0},{3,1},{4,6},{5,7},{6,4},{7,5},{8,10},{9,11},{10,... | collective-permute-start | bytes 737288 | tf_op jit(solution)/shard_map/ppermute | solution.py:24
  38.6 12.0 %collective-permute-start.10 = (bf16[96,1280]{1,0:T(8,128)(2,1)S(1)}, bf16[96,1280]{1,0:T(8,128)(2,1)S(1)}, u32[]{:S(2)}, u32[]{:S(2)}) collective-permute-start(bf16[96,1280]{1,0:T(8,128)(2,1)S(1)} %pair_far.1.refs_4_.refs_0_), channel_id=1, source_target_pairs={{0,2},{1,3},{2,0},{3,1},{4,6},{5,7},{6,4},{7,5},{8,10},{9,11},{10,... | collective-permute-start | bytes 737288 | tf_op jit(solution)/shard_map/ppermute | solution.py:24
  43.1 8.8 %collective-permute-start.12 = (bf16[96,1280]{1,0:T(8,128)(2,1)S(1)}, bf16[96,1280]{1,0:T(8,128)(2,1)S(1)}, u32[]{:S(2)}, u32[]{:S(2)}) collective-permute-start(bf16[96,1280]{1,0:T(8,128)(2,1)S(1)} %get-tuple-element.25), channel_id=1, source_target_pairs={{0,8},{4,12},{8,0},{12,4},{1,9},{5,13},{9,1},{13,5},{2,10},{6,14},... | collective-permute-start | bytes 737288 | tf_op jit(solution)/shard_map/ppermute | solution.py:24
  44.7 11.6 %collective-permute-start.13 = (bf16[96,1280]{1,0:T(8,128)(2,1)S(1)}, bf16[96,1280]{1,0:T(8,128)(2,1)S(1)}, u32[]{:S(2)}, u32[]{:S(2)}) collective-permute-start(bf16[96,1280]{1,0:T(8,128)(2,1)S(1)} %get-tuple-element.23.refs_2_), channel_id=1, source_target_pairs={{0,8},{4,12},{8,0},{12,4},{1,9},{5,13},{9,1},{13,5},{2,10},{6,14},... | collective-permute-start | bytes 737288 | tf_op jit(solution)/shard_map/ppermute | solution.py:24
  45.3 15.7 %collective-permute-start.9 = (bf16[96,1280]{1,0:T(8,128)(2,1)S(1)}, bf16[96,1280]{1,0:T(8,128)(2,1)S(1)}, u32[]{:S(2)}, u32[]{:S(2)}) collective-permute-start(bf16[96,1280]{1,0:T(8,128)(2,1)S(1)} %total_near.1.refs_3_.refs_1_), channel_id=1, source_target_pairs={{0,1},{1,0},{2,3},{3,2},{4,5},{5,4},{6,7},{7,6},{8,9},{9,8},{10,11... | collective-permute-start | bytes 737288 | tf_op jit(solution)/shard_map/ppermute | solution.py:24
  50.7 10.4 %collective-permute-start.11 = (bf16[96,1280]{1,0:T(8,128)(2,1)S(1)}, bf16[96,1280]{1,0:T(8,128)(2,1)S(1)}, u32[]{:S(2)}, u32[]{:S(2)}) collective-permute-start(bf16[96,1280]{1,0:T(8,128)(2,1)S(1)} %total_far.1.refs_2_.refs_3_), channel_id=1, source_target_pairs={{0,1},{1,0},{2,3},{3,2},{4,5},{5,4},{6,7},{7,6},{8,9},{9,8},{10,11... | collective-permute-start | bytes 737288 | tf_op jit(solution)/shard_map/ppermute | solution.py:24
  52.0 9.1 %collective-permute-start.14 = (bf16[96,1280]{1,0:T(8,128)(2,1)S(1)}, bf16[96,1280]{1,0:T(8,128)(2,1)S(1)}, u32[]{:S(2)}, u32[]{:S(2)}) collective-permute-start(bf16[96,1280]{1,0:T(8,128)(2,1)S(1)} %panel_sum_top.1.refs_2_.refs_5_), channel_id=1, source_target_pairs={{0,4},{4,0},{8,12},{12,8},{1,5},{5,1},{9,13},{13,9},{2,6},{6,2},{1... | collective-permute-start | bytes 737288 | tf_op jit(solution)/shard_map/ppermute | solution.py:24
  56.4 4.7 %collective-permute-start.15 = (bf16[96,1280]{1,0:T(8,128)(2,1)S(1)}, bf16[96,1280]{1,0:T(8,128)(2,1)S(1)}, u32[]{:S(2)}, u32[]{:S(2)}) collective-permute-start(bf16[96,1280]{1,0:T(8,128)(2,1)S(1)} %panel_sum_low.1.refs_2_.refs_6_), channel_id=1, source_target_pairs={{0,4},{4,0},{8,12},{12,8},{1,5},{5,1},{9,13},{13,9},{2,6},{6,2},{1... | collective-permute-start | bytes 737288 | tf_op jit(solution)/shard_map/ppermute | solution.py:24

commit v5 on v4

--- a/solution.py
+++ b/solution.py
@@ -259,7 +259,7 @@
     size, feats = grads.shape
     depth, queries, cols = query_rot.shape
     panel, tok = lax.axis_index("panel"), lax.axis_index("tok")
-    core, turn = panel % 2, tok % 2
+    core, turn = panel % 2, (tok ^ tok // 2) % 2
     steps = Steps()
 
     def wide(*shape):
@@ -296,15 +296,13 @@
     (send2,) = steps("send_far", send_body, [in_basis], [narrow(size, cols)], where=[far, most], **options)
     got2 = swap(send2, "tok", 1)
     (pair1,) = steps("pair_near", pair_body, [in_basis, got1], [narrow(size, cols)], where=[acts, pltpu.with_memory_space_constraint(near, pltpu.HBM)], **options)
-    got1 = swap(pair1, "tok", 2)
+    got1 = swap(pair1, "tok", 3)
     (out_basis,) = loaded("load_out", out_basis)
     mine_top, mine_low, top, low = steps(
         "rotate", rotate_body, [grads, g1, g3, g2, out_basis], [wide(size, depth)] * 2 + [narrow(size, depth)] * 2,
         scalars=scalars(tok, tok ^ 1, tok ^ 2, tok ^ 3, core),
         scratch=[pltpu.VMEM((4 * size, feats), NARROW)], flops=8 * size * feats * depth,
     )
-    (pair2,) = steps("pair_far", pair_body, [in_basis, got2], [narrow(size, cols)], where=[far, most], **options)
-    got2 = swap(pair2, "tok", 2)
     chips = [[2 * k, 2 * k + 1] for k in range(2)]
 
     def chip_sum(name, mine, other, *handed):
@@ -316,16 +314,19 @@
         return mine, swap(other, "panel", 2), *handed
 
     mine_top, top, low = chip_sum("chip_sum_top", mine_top, top, low)
+    (pair2,) = steps("pair_far", pair_body, [in_basis, got2], [narrow(size, cols)], where=[far, most], **options)
+    got2 = swap(pair2, "tok", 3)
     (total1,) = steps("total_near", add_body, [pair1, got1], [narrow(size, cols)])
     back1 = swap(total1, "tok", 1)
     mine_low, low = chip_sum("chip_sum_low", mine_low, low)
     (total2,) = steps("total_far", add_body, [pair2, got2], [narrow(size, cols)])
     back2 = swap(total2, "tok", 1)
+    steps("mark_near", mark_body, [], [wide(8, LANES)], after=[back1])
     (mine_top,) = steps("panel_sum_top", panel_sum_body, [mine_top, top], [narrow(size, depth)], weight=8_000_000)
     other_top = swap(mine_top, "panel", 1)
     (mine_low,) = steps("panel_sum_low", panel_sum_body, [mine_low, low], [narrow(size, depth)])
     other_low = swap(mine_low, "panel", 1)
-    steps("mark", mark_body, [], [wide(8, LANES)], after=[back1, back2])
+    steps("mark_far", mark_body, [], [wide(8, LANES)], after=[back2])
     owners = lax.axis_size("panel") * lax.axis_size("tok")
     (partial,) = steps(
         "scores", score_body, [total1, back1, total2, back2, mine_top, mine_low, other_top, other_low],

time: 89.3 us -> 84.6 us (0.947)
  waiting for transfers between devices: 21.2 us -> 16.8 us
  starting transfers between devices: 15.9 us -> 18.4 us
  Pallas kernels: 33.8 us -> 32.1 us
  blocking collectives: 15.2 us -> 14.2 us
    ppermute x16, waiting for transfers between devices: 21.2 us -> 16.8 us  [swap(): lax.ppermute(value, axis, [(i, i ^ mask) for i in range(lax.axis_size(axi...]
    ppermute x16, starting transfers between devices: 15.9 us -> 18.4 us  [swap(): lax.ppermute(value, axis, [(i, i ^ mask) for i in range(lax.axis_size(axi...]
    pallas_call x16 -> x17, Pallas kernels: 33.8 us -> 32.1 us  [__call__(): pl.pallas_call(kernel, grid=(1,), in_specs=specs, out_specs=[block(x) for...]
    all_to_all x1, blocking collectives: 10.9 us -> 9.92 us  [on_lines_of_four(): lax.all_to_all(partial, ('panel', 'tok'), split_axis=0, concat_axis=0, ti...]
  transfers between devices with their start and end apart: 16 -> 16, of which waited for: 7 -> 6; matrix products, arithmetic and copies ran while one was open for 0% -> 0% of each run, Pallas kernels for 19% -> 18%
where the time goes in v5:
time: 84.6 us; the launch traced here: 84.2 us
  Pallas kernels  32.1 us (38%)
  starting transfers between devices  18.4 us (22%)
  waiting for transfers between devices  16.8 us (20%)
  blocking collectives  14.2 us (17%)
  local copies, waits for them, and re-layouts  2.54 us (3%)
    pallas_call x17, Pallas kernels, __call__(): pl.pallas_call(kernel, grid=(1,), in_specs=specs, out_specs=[block(x) for...  32.1 us
    ppermute x16, starting transfers between devices, swap(): lax.ppermute(value, axis, [(i, i ^ mask) for i in range(lax.axis_size(axi...  18.4 us
    ppermute x16, waiting for transfers between devices, swap(): lax.ppermute(value, axis, [(i, i ^ mask) for i in range(lax.axis_size(axi...  16.8 us
    all_to_all x1, blocking collectives, on_lines_of_four(): lax.all_to_all(partial, ('panel', 'tok'), split_axis=0, concat_axis=0, ti...  9.92 us
    all_gather x2, blocking collectives, chip_sum(): lax.all_gather(other, 'panel', axis=0, tiled=True, axis_index_groups=chips)  4.3 us
    unnamed x10, local copies, waits for them, and re-layouts  2.37 us
  transfers between devices with their start and end apart: 16, of which 6 were waited for; matrix products, arithmetic and copies ran while one was open for 0% of the time, Pallas kernels for 18%

profile of v5, /device:TPU:0, one launch (start us, length us, event | category | flops | bytes accessed | tf_op | source)
XLA Modules:
  0.0 84.2 jit_solution(5000871269229102765)
XLA Ops:
  0.5 2.6 %collective-permute-start.5 = (bf16[96,1280]{1,0:T(8,128)(2,1)}, bf16[96,1280]{1,0:T(8,128)(2,1)S(1)}, u32[]{:S(2)}, u32[]{:S(2)}) collective-permute-start(bf16[96,1280]{1,0:T(8,128)(2,1)} %refs_1_.3), channel_id=1, source_target_pairs={{0,1},{1,0},{2,3},{3,2},{4,5},{5,4},{6,7},{7,6},{8,9},{9,8},{10,11... | collective-permute-start | bytes 737288 | tf_op jit(solution)/shard_map/ppermute | solution.py:24
  3.0 2.6 %collective-permute-start.4 = (bf16[96,1280]{1,0:T(8,128)(2,1)}, bf16[96,1280]{1,0:T(8,128)(2,1)}, u32[]{:S(2)}, u32[]{:S(2)}) collective-permute-start(bf16[96,1280]{1,0:T(8,128)(2,1)} %refs_1_.3), channel_id=1, source_target_pairs={{0,2},{1,3},{2,0},{3,1},{4,6},{5,7},{6,4},{7,5},{8,10},{9,11},{10,... | collective-permute-start | bytes 737288 | tf_op jit(solution)/shard_map/ppermute | solution.py:24
  5.6 1.5 %collective-permute-start.2 = (bf16[96,1280]{1,0:T(8,128)(2,1)}, bf16[96,1280]{1,0:T(8,128)(2,1)}, u32[]{:S(2)}, u32[]{:S(2)}) collective-permute-start(bf16[96,1280]{1,0:T(8,128)(2,1)} %refs_3_.1), channel_id=1, source_target_pairs={{0,8},{4,12},{8,0},{12,4},{1,9},{5,13},{9,1},{13,5},{2,10},{6,14},... | collective-permute-start | bytes 737288 | tf_op jit(solution)/shard_map/ppermute | solution.py:24
  7.1 0.7 copy-done.4
  7.8 3.8 %send_near.1 = (bf16[1280,1280]{1,0:T(8,128)(2,1)S(1)}, bf16[96,1280]{1,0:T(8,128)(2,1)}) custom-call(s32[1]{0:T(128)} %bitcast.5.refs_0_, bf16[1280,1280]{1,0:T(8,128)(2,1)} %refs_1_.2, bf16[96,1280]{1,0:T(8,128)(2,1)} %refs_3_.1, bf16[96,1280]{1,0:T(8,128)(2,1)} %copy-done.4), custom_call_target="tpu_custom_call" | custom-call | flops 314572800 | bytes 6799360 | tf_op jit(solution)/shard_map/send_near/pallas_call | solution.py:68
  11.6 0.5 collective-permute-start.1
  12.1 2.9 %collective-permute-done.5.refs_1_.refs_2_ = bf16[96,1280]{1,0:T(8,128)(2,1)S(1)} collective-permute-done((bf16[96,1280]{1,0:T(8,128)(2,1)}, bf16[96,1280]{1,0:T(8,128)(2,1)S(1)}, u32[]{:S(2)}, u32[]{:S(2)}) %collective-permute-start.5) | collective-permute-done | bytes 245792 | tf_op jit(solution)/shard_map/ppermute | solution.py:24
  15.0 0.7 copy-done
  15.7 1.7 %collective-permute-done.4.refs_0_ = bf16[96,1280]{1,0:T(8,128)(2,1)} collective-permute-done((bf16[96,1280]{1,0:T(8,128)(2,1)}, bf16[96,1280]{1,0:T(8,128)(2,1)}, u32[]{:S(2)}, u32[]{:S(2)}) %collective-permute-start.4) | collective-permute-done | bytes 245792 | tf_op jit(solution)/shard_map/ppermute | solution.py:24
  17.5 0.9 %copy-done.1 = bf16[96,1280]{1,0:T(8,128)(2,1)S(1)} copy-done((bf16[96,1280]{1,0:T(8,128)(2,1)S(1)}, bf16[96,1280]{1,0:T(8,128)(2,1)}, u32[]{:S(2)}) %copy-start.1) | copy-done | bytes 245784
  18.4 1.0 %pass.1.refs_4_.refs_3_ = bf16[96,1280]{1,0:T(8,128)(2,1)S(1)} custom-call(bf16[96,1280]{1,0:T(8,128)(2,1)} %collective-permute-done.4.refs_0_, bf16[96,1280]{1,0:T(8,128)(2,1)S(1)} %copy-done.1, bf16[96,1280]{1,0:T(8,128)(2,1)} %get-tuple-element.17.refs_2_), custom_call_target="tpu_custom_call" | custom-call | bytes 491520 | tf_op jit(solution)/shard_map/pass/pallas_call | solution.py:68
  19.4 1.0 %collective-permute-start.8 = (bf16[96,1280]{1,0:T(8,128)(2,1)S(1)}, bf16[96,1280]{1,0:T(8,128)(2,1)}, u32[]{:S(2)}, u32[]{:S(2)}) collective-permute-start(bf16[96,1280]{1,0:T(8,128)(2,1)S(1)} %pass.1.refs_4_.refs_3_), channel_id=1, source_target_pairs={{0,1},{1,0},{2,3},{3,2},{4,5},{5,4},{6,7},{7,6},{8,9},{9,8},{10,11... | collective-permute-start | bytes 737288 | tf_op jit(solution)/shard_map/ppermute | solution.py:24
  20.5 1.6 %send_far.1.refs_5_ = bf16[96,1280]{1,0:T(8,128)(2,1)S(1)} custom-call(s32[1]{0:T(128)} %bitcast.5.refs_0_, bf16[1280,1280]{1,0:T(8,128)(2,1)S(1)} %get-tuple-element.16.refs_1_, bf16[96,1280]{1,0:T(8,128)(2,1)} %collective-permute-done.2.refs_2_.refs_3_, bf16[96,1280]{1,0:T(8,128)(2,1)} %collective-permute-done.3.refs_3_.refs_4_, ...), custom_call_target="tpu_custom_call" | custom-call | flops 314572800 | bytes 3522560 | tf_op jit(solution)/shard_map/send_far/pallas_call | solution.py:68
  22.1 1.1 %collective-permute-start.7 = (bf16[96,1280]{1,0:T(8,128)(2,1)S(1)}, bf16[96,1280]{1,0:T(8,128)(2,1)S(1)}, u32[]{:S(2)}, u32[]{:S(2)}) collective-permute-start(bf16[96,1280]{1,0:T(8,128)(2,1)S(1)} %send_far.1.refs_5_), channel_id=1, source_target_pairs={{0,1},{1,0},{2,3},{3,2},{4,5},{5,4},{6,7},{7,6},{8,9},{9,8},{10,11... | collective-permute-start | bytes 737288 | tf_op jit(solution)/shard_map/ppermute | solution.py:24
  23.2 2.6 %pair_near.1.refs_1_.refs_0_ = bf16[96,1280]{1,0:T(8,128)(2,1)S(1)} custom-call(s32[1]{0:T(128)} %bitcast.5.refs_0_, bf16[1280,1280]{1,0:T(8,128)(2,1)S(1)} %get-tuple-element.16.refs_1_, bf16[96,1280]{1,0:T(8,128)(2,1)} %collective-permute-done.1.refs_2_, bf16[96,1280]{1,0:T(8,128)(2,1)} %refs_3_.1, bf16[96,1280]{1,0:T(8,128)(2,1)} %copy-done.4, ...), custom_call_target="tpu_custom_call" | custom-call | flops 314572800 | bytes 3768320 | tf_op jit(solution)/shard_map/pair_near/pallas_call | solution.py:68
  25.8 2.8 %collective-permute-start.6 = (bf16[96,1280]{1,0:T(8,128)(2,1)S(1)}, bf16[96,1280]{1,0:T(8,128)(2,1)S(1)}, u32[]{:S(2)}, u32[]{:S(2)}) collective-permute-start(bf16[96,1280]{1,0:T(8,128)(2,1)S(1)} %pair_near.1.refs_1_.refs_0_), channel_id=1, source_target_pairs={{0,3},{1,2},{2,1},{3,0},{4,7},{5,6},{6,5},{7,4},{8,11},{9,10},{10,... | collective-permute-start | bytes 737288 | tf_op jit(solution)/shard_map/ppermute | solution.py:24
  28.7 1.9 %load_out.1.refs_5_.refs_6_ = bf16[1280,1280]{1,0:T(8,128)(2,1)S(1)} custom-call(bf16[1280,1280]{1,0:T(8,128)(2,1)} %refs_0_.1, bf16[96,1280]{1,0:T(8,128)(2,1)S(1)} %pair_near.1.refs_1_.refs_0_), custom_call_target="tpu_custom_call" | custom-call | bytes 6553600 | tf_op jit(solution)/shard_map/load_out/pallas_call | solution.py:68
  30.6 2.4 %rotate.1 = (f32[96,1280]{1,0:T(8,128)S(1)}, f32[96,1280]{1,0:T(8,128)S(1)}, bf16[96,1280]{1,0:T(8,128)(2,1)S(1)}, bf16[96,1280]{1,0:T(8,128)(2,1)S(1)}) custom-call(s32[5]{0:T(128)S(1)} %stack.51.refs_0_, bf16[96,1280]{1,0:T(8,128)(2,1)S(1)} %copy-done.3, bf16[96,1280]{1,0:T(8,128)(2,1)S(1)} %copy-done.2, bf16[96,1280]{1,0:T(8,128)(2,1)S(1)} %pass.1.refs_4_.refs_3_, ...), custom_call_target="tpu_custom_call" | custom-call | flops 1258291200 | bytes 5734400 | tf_op jit(solution)/shard_map/rotate/pallas_call | solution.py:68
  33.1 2.2 %all_gather.6.refs_2_ = bf16[192,1280]{1,0:T(8,128)(2,1)S(1)} all-gather(bf16[96,1280]{1,0:T(8,128)(2,1)S(1)} %get-tuple-element.19), channel_id=1, replica_groups={{0,4},{8,12},{1,5},{9,13},{2,6},{10,14},{3,7},{11,15},{16,20},{24,28},{..., dimensions={0}, use_global_device_ids=true | all-gather | bytes 737280 | tf_op jit(solution)/shard_map/all_gather | solution.py:309
  35.3 1.6 %pair_far.1.refs_2_.refs_0_ = bf16[96,1280]{1,0:T(8,128)(2,1)S(1)} custom-call(s32[1]{0:T(128)} %bitcast.5.refs_0_, bf16[1280,1280]{1,0:T(8,128)(2,1)S(1)} %get-tuple-element.16.refs_1_, bf16[96,1280]{1,0:T(8,128)(2,1)S(1)} %collective-permute-done.7.refs_2_, bf16[96,1280]{1,0:T(8,128)(2,1)} %collective-permute-done.2.refs_2_.refs_3_, ...), custom_call_target="tpu_custom_call" | custom-call | flops 314572800 | bytes 3768320 | tf_op jit(solution)/shard_map/pair_far/pallas_call | solution.py:68
  37.0 1.1 %collective-permute-start.10 = (bf16[96,1280]{1,0:T(8,128)(2,1)S(1)}, bf16[96,1280]{1,0:T(8,128)(2,1)S(1)}, u32[]{:S(2)}, u32[]{:S(2)}) collective-permute-start(bf16[96,1280]{1,0:T(8,128)(2,1)S(1)} %pair_far.1.refs_2_.refs_0_), channel_id=1, source_target_pairs={{0,3},{1,2},{2,1},{3,0},{4,7},{5,6},{6,5},{7,4},{8,11},{9,10},{10,... | collective-permute-start | bytes 737288 | tf_op jit(solution)/shard_map/ppermute | solution.py:24
  38.1 2.1 %all_gather.7.refs_2_ = bf16[192,1280]{1,0:T(8,128)(2,1)S(1)} all-gather(bf16[96,1280]{1,0:T(8,128)(2,1)S(1)} %get-tuple-element.21.refs_5_), channel_id=1, replica_groups={{0,4},{8,12},{1,5},{9,13},{2,6},{10,14},{3,7},{11,15},{16,20},{24,28},{..., dimensions={0}, use_global_device_ids=true | all-gather | bytes 737280 | tf_op jit(solution)/shard_map/all_gather | solution.py:309
  40.4 1.6 %collective-permute-start.12 = (bf16[96,1280]{1,0:T(8,128)(2,1)S(1)}, bf16[96,1280]{1,0:T(8,128)(2,1)S(1)}, u32[]{:S(2)}, u32[]{:S(2)}) collective-permute-start(bf16[96,1280]{1,0:T(8,128)(2,1)S(1)} %get-tuple-element.25), channel_id=1, source_target_pairs={{0,8},{4,12},{8,0},{12,4},{1,9},{5,13},{9,1},{13,5},{2,10},{6,14},... | collective-permute-start | bytes 737288 | tf_op jit(solution)/shard_map/ppermute | solution.py:24
  42.0 0.6 collective-permute-start.13
  42.6 5.1 %collective-permute-done.10.refs_1_ = bf16[96,1280]{1,0:T(8,128)(2,1)S(1)} collective-permute-done((bf16[96,1280]{1,0:T(8,128)(2,1)S(1)}, bf16[96,1280]{1,0:T(8,128)(2,1)S(1)}, u32[]{:S(2)}, u32[]{:S(2)}) %collective-permute-start.10) | collective-permute-done | bytes 245792 | tf_op jit(solution)/shard_map/ppermute | solution.py:24
  47.8 1.9 %collective-permute-start.11 = (bf16[96,1280]{1,0:T(8,128)(2,1)S(1)}, bf16[96,1280]{1,0:T(8,128)(2,1)S(1)}, u32[]{:S(2)}, u32[]{:S(2)}) collective-permute-start(bf16[96,1280]{1,0:T(8,128)(2,1)S(1)} %total_far.1.refs_1_.refs_3_), channel_id=1, source_target_pairs={{0,1},{1,0},{2,3},{3,2},{4,5},{5,4},{6,7},{7,6},{8,9},{9,8},{10,11... | collective-permute-start | bytes 737288 | tf_op jit(solution)/shard_map/ppermute | solution.py:24
  49.7 2.6 %collective-permute-done.9.refs_0_.refs_2_ = bf16[96,1280]{1,0:T(8,128)(2,1)S(1)} collective-permute-done((bf16[96,1280]{1,0:T(8,128)(2,1)S(1)}, bf16[96,1280]{1,0:T(8,128)(2,1)S(1)}, u32[]{:S(2)}, u32[]{:S(2)}) %collective-permute-start.9) | collective-permute-done | bytes 245792 | tf_op jit(solution)/shard_map/ppermute | solution.py:24
  52.3 1.4 %collective-permute-done.13.refs_1_ = bf16[96,1280]{1,0:T(8,128)(2,1)S(1)} collective-permute-done((bf16[96,1280]{1,0:T(8,128)(2,1)S(1)}, bf16[96,1280]{1,0:T(8,128)(2,1)S(1)}, u32[]{:S(2)}, u32[]{:S(2)}) %collective-permute-start.13) | collective-permute-done | bytes 245792 | tf_op jit(solution)/shard_map/ppermute | solution.py:24
  54.4 3.0 %collective-permute-done.11.refs_0_.refs_4_ = bf16[96,1280]{1,0:T(8,128)(2,1)S(1)} collective-permute-done((bf16[96,1280]{1,0:T(8,128)(2,1)S(1)}, bf16[96,1280]{1,0:T(8,128)(2,1)S(1)}, u32[]{:S(2)}, u32[]{:S(2)}) %collective-permute-start.11) | collective-permute-done | bytes 245792 | tf_op jit(solution)/shard_map/ppermute | solution.py:24
  57.5 16.2 %scores.1.refs_1_ = f32[16,8,128]{2,1,0:T(8,128)S(1)} custom-call(s32[5]{0:T(128)S(1)} %stack.45.refs_0_, bf16[96,1280]{1,0:T(8,128)(2,1)S(1)} %total_near.1.refs_3_.refs_1_, bf16[96,1280]{1,0:T(8,128)(2,1)S(1)} %collective-permute-done.9.refs_0_.refs_2_, bf16[96,1280]{1,0:T(8,128)(2,1)S(1)} %total_far.1.refs_1_.refs_3_, ...), custom_call_target="tpu_custom_call" | custom-call | flops 10066329600 | bytes 34799616 | tf_op jit(solution)/shard_map/scores/pallas_call | solution.py:68
  73.7 9.9 %all_to_all.5.refs_0_ = f32[16,8,128]{2,1,0:T(8,128)S(1)} all-to-all(f32[16,8,128]{2,1,0:T(8,128)S(1)} %scores.1.refs_1_), channel_id=1, replica_groups=mesh['groups'=2,'panel'=4,'tok'=4] {'panel','tok'}, dimensions={0} | all-to-all | bytes 131072 | tf_op jit(solution)/shard_map/all_to_all | solution.py:344
  83.6 0.6 final.1
  (32 shorter events, 1.7 us)
Async XLA Ops:
  0.0 7.1 %collective-permute-start = (bf16[96,1280]{1,0:T(8,128)(2,1)}, bf16[96,1280]{1,0:T(8,128)(2,1)S(1)}, u32[]{:S(2)}, u32[]{:S(2)}) collective-permute-start(bf16[96,1280]{1,0:T(8,128)(2,1)} %refs_3_.1), channel_id=1, source_target_pairs={{0,4},{4,0},{8,12},{12,8},{1,5},{5,1},{9,13},{13,9},{2,6},{6,2},{1... | collective-permute-start | bytes 737288 | tf_op jit(solution)/shard_map/ppermute | solution.py:24
  0.5 14.5 %collective-permute-start.5 = (bf16[96,1280]{1,0:T(8,128)(2,1)}, bf16[96,1280]{1,0:T(8,128)(2,1)S(1)}, u32[]{:S(2)}, u32[]{:S(2)}) collective-permute-start(bf16[96,1280]{1,0:T(8,128)(2,1)} %refs_1_.3), channel_id=1, source_target_pairs={{0,1},{1,0},{2,3},{3,2},{4,5},{5,4},{6,7},{7,6},{8,9},{9,8},{10,11... | collective-permute-start | bytes 737288 | tf_op jit(solution)/shard_map/ppermute | solution.py:24
  3.0 14.4 %collective-permute-start.4 = (bf16[96,1280]{1,0:T(8,128)(2,1)}, bf16[96,1280]{1,0:T(8,128)(2,1)}, u32[]{:S(2)}, u32[]{:S(2)}) collective-permute-start(bf16[96,1280]{1,0:T(8,128)(2,1)} %refs_1_.3), channel_id=1, source_target_pairs={{0,2},{1,3},{2,0},{3,1},{4,6},{5,7},{6,4},{7,5},{8,10},{9,11},{10,... | collective-permute-start | bytes 737288 | tf_op jit(solution)/shard_map/ppermute | solution.py:24
  5.6 14.9 %collective-permute-start.2 = (bf16[96,1280]{1,0:T(8,128)(2,1)}, bf16[96,1280]{1,0:T(8,128)(2,1)}, u32[]{:S(2)}, u32[]{:S(2)}) collective-permute-start(bf16[96,1280]{1,0:T(8,128)(2,1)} %refs_3_.1), channel_id=1, source_target_pairs={{0,8},{4,12},{8,0},{12,4},{1,9},{5,13},{9,1},{13,5},{2,10},{6,14},... | collective-permute-start | bytes 737288 | tf_op jit(solution)/shard_map/ppermute | solution.py:24
  7.1 13.4 %collective-permute-start.3 = (bf16[96,1280]{1,0:T(8,128)(2,1)}, bf16[96,1280]{1,0:T(8,128)(2,1)}, u32[]{:S(2)}, u32[]{:S(2)}) collective-permute-start(bf16[96,1280]{1,0:T(8,128)(2,1)} %refs_3_.1), channel_id=1, source_target_pairs={{0,12},{4,8},{8,4},{12,0},{1,13},{5,9},{9,5},{13,1},{2,14},{6,10},... | collective-permute-start | bytes 737288 | tf_op jit(solution)/shard_map/ppermute | solution.py:24
  7.1 0.7 copy-start.4
  11.6 11.7 %collective-permute-start.1 = (bf16[96,1280]{1,0:T(8,128)(2,1)}, bf16[96,1280]{1,0:T(8,128)(2,1)}, u32[]{:S(2)}, u32[]{:S(2)}) collective-permute-start(bf16[96,1280]{1,0:T(8,128)(2,1)} %get-tuple-element.17.refs_2_), channel_id=1, source_target_pairs={{0,1},{1,0},{2,3},{3,2},{4,5},{5,4},{6,7},{7,6},{8,9},{9,8},{10,11... | collective-permute-start | bytes 737288 | tf_op jit(solution)/shard_map/ppermute | solution.py:24
  15.0 0.7 copy-start
  17.5 0.9 %copy-start.1 = (bf16[96,1280]{1,0:T(8,128)(2,1)S(1)}, bf16[96,1280]{1,0:T(8,128)(2,1)}, u32[]{:S(2)}) copy-start(bf16[96,1280]{1,0:T(8,128)(2,1)} %copy-done) | copy-start | bytes 737284
  19.4 11.2 %collective-permute-start.8 = (bf16[96,1280]{1,0:T(8,128)(2,1)S(1)}, bf16[96,1280]{1,0:T(8,128)(2,1)}, u32[]{:S(2)}, u32[]{:S(2)}) collective-permute-start(bf16[96,1280]{1,0:T(8,128)(2,1)S(1)} %pass.1.refs_4_.refs_3_), channel_id=1, source_target_pairs={{0,1},{1,0},{2,3},{3,2},{4,5},{5,4},{6,7},{7,6},{8,9},{9,8},{10,11... | collective-permute-start | bytes 737288 | tf_op jit(solution)/shard_map/ppermute | solution.py:24
  22.1 13.2 %collective-permute-start.7 = (bf16[96,1280]{1,0:T(8,128)(2,1)S(1)}, bf16[96,1280]{1,0:T(8,128)(2,1)S(1)}, u32[]{:S(2)}, u32[]{:S(2)}) collective-permute-start(bf16[96,1280]{1,0:T(8,128)(2,1)S(1)} %send_far.1.refs_5_), channel_id=1, source_target_pairs={{0,1},{1,0},{2,3},{3,2},{4,5},{5,4},{6,7},{7,6},{8,9},{9,8},{10,11... | collective-permute-start | bytes 737288 | tf_op jit(solution)/shard_map/ppermute | solution.py:24
  25.8 4.8 %copy-start.2 = (bf16[96,1280]{1,0:T(8,128)(2,1)S(1)}, bf16[96,1280]{1,0:T(8,128)(2,1)}, u32[]{:S(2)}) copy-start(bf16[96,1280]{1,0:T(8,128)(2,1)} %copy-done) | copy-start | bytes 737284
  25.8 4.8 %copy-start.3 = (bf16[96,1280]{1,0:T(8,128)(2,1)S(1)}, bf16[96,1280]{1,0:T(8,128)(2,1)}, u32[]{:S(2)}) copy-start(bf16[96,1280]{1,0:T(8,128)(2,1)} %refs_1_.3) | copy-start | bytes 737284
  25.8 14.4 %collective-permute-start.6 = (bf16[96,1280]{1,0:T(8,128)(2,1)S(1)}, bf16[96,1280]{1,0:T(8,128)(2,1)S(1)}, u32[]{:S(2)}, u32[]{:S(2)}) collective-permute-start(bf16[96,1280]{1,0:T(8,128)(2,1)S(1)} %pair_near.1.refs_1_.refs_0_), channel_id=1, source_target_pairs={{0,3},{1,2},{2,1},{3,0},{4,7},{5,6},{6,5},{7,4},{8,11},{9,10},{10,... | collective-permute-start | bytes 737288 | tf_op jit(solution)/shard_map/ppermute | solution.py:24
  37.0 10.8 %collective-permute-start.10 = (bf16[96,1280]{1,0:T(8,128)(2,1)S(1)}, bf16[96,1280]{1,0:T(8,128)(2,1)S(1)}, u32[]{:S(2)}, u32[]{:S(2)}) collective-permute-start(bf16[96,1280]{1,0:T(8,128)(2,1)S(1)} %pair_far.1.refs_2_.refs_0_), channel_id=1, source_target_pairs={{0,3},{1,2},{2,1},{3,0},{4,7},{5,6},{6,5},{7,4},{8,11},{9,10},{10,... | collective-permute-start | bytes 737288 | tf_op jit(solution)/shard_map/ppermute | solution.py:24
  40.3 12.0 %collective-permute-start.9 = (bf16[96,1280]{1,0:T(8,128)(2,1)S(1)}, bf16[96,1280]{1,0:T(8,128)(2,1)S(1)}, u32[]{:S(2)}, u32[]{:S(2)}) collective-permute-start(bf16[96,1280]{1,0:T(8,128)(2,1)S(1)} %total_near.1.refs_3_.refs_1_), channel_id=1, source_target_pairs={{0,1},{1,0},{2,3},{3,2},{4,5},{5,4},{6,7},{7,6},{8,9},{9,8},{10,11... | collective-permute-start | bytes 737288 | tf_op jit(solution)/shard_map/ppermute | solution.py:24
  40.4 11.9 %collective-permute-start.12 = (bf16[96,1280]{1,0:T(8,128)(2,1)S(1)}, bf16[96,1280]{1,0:T(8,128)(2,1)S(1)}, u32[]{:S(2)}, u32[]{:S(2)}) collective-permute-start(bf16[96,1280]{1,0:T(8,128)(2,1)S(1)} %get-tuple-element.25), channel_id=1, source_target_pairs={{0,8},{4,12},{8,0},{12,4},{1,9},{5,13},{9,1},{13,5},{2,10},{6,14},... | collective-permute-start | bytes 737288 | tf_op jit(solution)/shard_map/ppermute | solution.py:24
  42.0 11.7 %collective-permute-start.13 = (bf16[96,1280]{1,0:T(8,128)(2,1)S(1)}, bf16[96,1280]{1,0:T(8,128)(2,1)S(1)}, u32[]{:S(2)}, u32[]{:S(2)}) collective-permute-start(bf16[96,1280]{1,0:T(8,128)(2,1)S(1)} %get-tuple-element.23.refs_2_), channel_id=1, source_target_pairs={{0,8},{4,12},{8,0},{12,4},{1,9},{5,13},{9,1},{13,5},{2,10},{6,14},... | collective-permute-start | bytes 737288 | tf_op jit(solution)/shard_map/ppermute | solution.py:24
  47.8 9.7 %collective-permute-start.11 = (bf16[96,1280]{1,0:T(8,128)(2,1)S(1)}, bf16[96,1280]{1,0:T(8,128)(2,1)S(1)}, u32[]{:S(2)}, u32[]{:S(2)}) collective-permute-start(bf16[96,1280]{1,0:T(8,128)(2,1)S(1)} %total_far.1.refs_1_.refs_3_), channel_id=1, source_target_pairs={{0,1},{1,0},{2,3},{3,2},{4,5},{5,4},{6,7},{7,6},{8,9},{9,8},{10,11... | collective-permute-start | bytes 737288 | tf_op jit(solution)/shard_map/ppermute | solution.py:24
  53.8 3.7 %collective-permute-start.15 = (bf16[96,1280]{1,0:T(8,128)(2,1)S(1)}, bf16[96,1280]{1,0:T(8,128)(2,1)S(1)}, u32[]{:S(2)}, u32[]{:S(2)}) collective-permute-start(bf16[96,1280]{1,0:T(8,128)(2,1)S(1)} %panel_sum_low.1.refs_1_.refs_6_), channel_id=1, source_target_pairs={{0,4},{4,0},{8,12},{12,8},{1,5},{5,1},{9,13},{13,9},{2,6},{6,2},{1... | collective-permute-start | bytes 737288 | tf_op jit(solution)/shard_map/ppermute | solution.py:24
  53.8 3.6 %collective-permute-start.14 = (bf16[96,1280]{1,0:T(8,128)(2,1)S(1)}, bf16[96,1280]{1,0:T(8,128)(2,1)S(1)}, u32[]{:S(2)}, u32[]{:S(2)}) collective-permute-start(bf16[96,1280]{1,0:T(8,128)(2,1)S(1)} %panel_sum_top.1.refs_2_.refs_5_), channel_id=1, source_target_pairs={{0,4},{4,0},{8,12},{12,8},{1,5},{5,1},{9,13},{13,9},{2,6},{6,2},{1... | collective-permute-start | bytes 737288 | tf_op jit(solution)/shard_map/ppermute | solution.py:24

commit v6 on v5

--- a/solution.py
+++ b/solution.py
@@ -316,9 +316,9 @@
     mine_top, top, low = chip_sum("chip_sum_top", mine_top, top, low)
     (pair2,) = steps("pair_far", pair_body, [in_basis, got2], [narrow(size, cols)], where=[far, most], **options)
     got2 = swap(pair2, "tok", 3)
+    mine_low, low = chip_sum("chip_sum_low", mine_low, low)
     (total1,) = steps("total_near", add_body, [pair1, got1], [narrow(size, cols)])
     back1 = swap(total1, "tok", 1)
-    mine_low, low = chip_sum("chip_sum_low", mine_low, low)
     (total2,) = steps("total_far", add_body, [pair2, got2], [narrow(size, cols)])
     back2 = swap(total2, "tok", 1)
     steps("mark_near", mark_body, [], [wide(8, LANES)], after=[back1])

time: 84.6 us -> 84.8 us (level)
  no operation moved by 1% of the time
where the time goes in v6:
time: 84.8 us; the launch traced here: 84.3 us
  Pallas kernels  32.1 us (38%)
  starting transfers between devices  18.3 us (22%)
  waiting for transfers between devices  16.9 us (20%)
  blocking collectives  14.3 us (17%)
  local copies, waits for them, and re-layouts  2.54 us (3%)
    pallas_call x17, Pallas kernels, __call__(): pl.pallas_call(kernel, grid=(1,), in_specs=specs, out_specs=[block(x) for...  32.1 us
    ppermute x16, starting transfers between devices, swap(): lax.ppermute(value, axis, [(i, i ^ mask) for i in range(lax.axis_size(axi...  18.3 us
    ppermute x16, waiting for transfers between devices, swap(): lax.ppermute(value, axis, [(i, i ^ mask) for i in range(lax.axis_size(axi...  16.9 us
    all_to_all x1, blocking collectives, on_lines_of_four(): lax.all_to_all(partial, ('panel', 'tok'), split_axis=0, concat_axis=0, ti...  10 us
    all_gather x2, blocking collectives, chip_sum(): lax.all_gather(other, 'panel', axis=0, tiled=True, axis_index_groups=chips)  4.3 us
    unnamed x10, local copies, waits for them, and re-layouts  2.37 us
  transfers between devices with their start and end apart: 16, of which 6 were waited for; matrix products, arithmetic and copies ran while one was open for 0% of the time, Pallas kernels for 18%

profile of v6, /device:TPU:0, one launch (start us, length us, event | category | flops | bytes accessed | tf_op | source)
XLA Modules:
  0.0 84.3 jit_solution(15074321974897685784)
XLA Ops:
  0.5 2.6 %collective-permute-start.5 = (bf16[96,1280]{1,0:T(8,128)(2,1)}, bf16[96,1280]{1,0:T(8,128)(2,1)S(1)}, u32[]{:S(2)}, u32[]{:S(2)}) collective-permute-start(bf16[96,1280]{1,0:T(8,128)(2,1)} %refs_1_.3), channel_id=1, source_target_pairs={{0,1},{1,0},{2,3},{3,2},{4,5},{5,4},{6,7},{7,6},{8,9},{9,8},{10,11... | collective-permute-start | bytes 737288 | tf_op jit(solution)/shard_map/ppermute | solution.py:24
  3.0 2.6 %collective-permute-start.4 = (bf16[96,1280]{1,0:T(8,128)(2,1)}, bf16[96,1280]{1,0:T(8,128)(2,1)}, u32[]{:S(2)}, u32[]{:S(2)}) collective-permute-start(bf16[96,1280]{1,0:T(8,128)(2,1)} %refs_1_.3), channel_id=1, source_target_pairs={{0,2},{1,3},{2,0},{3,1},{4,6},{5,7},{6,4},{7,5},{8,10},{9,11},{10,... | collective-permute-start | bytes 737288 | tf_op jit(solution)/shard_map/ppermute | solution.py:24
  5.6 1.5 %collective-permute-start.2 = (bf16[96,1280]{1,0:T(8,128)(2,1)}, bf16[96,1280]{1,0:T(8,128)(2,1)}, u32[]{:S(2)}, u32[]{:S(2)}) collective-permute-start(bf16[96,1280]{1,0:T(8,128)(2,1)} %refs_3_.1), channel_id=1, source_target_pairs={{0,8},{4,12},{8,0},{12,4},{1,9},{5,13},{9,1},{13,5},{2,10},{6,14},... | collective-permute-start | bytes 737288 | tf_op jit(solution)/shard_map/ppermute | solution.py:24
  7.1 0.7 copy-done.4
  7.8 3.8 %send_near.1 = (bf16[1280,1280]{1,0:T(8,128)(2,1)S(1)}, bf16[96,1280]{1,0:T(8,128)(2,1)}) custom-call(s32[1]{0:T(128)} %bitcast.5.refs_0_, bf16[1280,1280]{1,0:T(8,128)(2,1)} %refs_1_.2, bf16[96,1280]{1,0:T(8,128)(2,1)} %refs_3_.1, bf16[96,1280]{1,0:T(8,128)(2,1)} %copy-done.4), custom_call_target="tpu_custom_call" | custom-call | flops 314572800 | bytes 6799360 | tf_op jit(solution)/shard_map/send_near/pallas_call | solution.py:68
  11.6 0.5 collective-permute-start.1
  12.1 2.9 %collective-permute-done.5.refs_1_.refs_2_ = bf16[96,1280]{1,0:T(8,128)(2,1)S(1)} collective-permute-done((bf16[96,1280]{1,0:T(8,128)(2,1)}, bf16[96,1280]{1,0:T(8,128)(2,1)S(1)}, u32[]{:S(2)}, u32[]{:S(2)}) %collective-permute-start.5) | collective-permute-done | bytes 245792 | tf_op jit(solution)/shard_map/ppermute | solution.py:24
  15.0 0.7 copy-done
  15.7 1.7 %collective-permute-done.4.refs_0_ = bf16[96,1280]{1,0:T(8,128)(2,1)} collective-permute-done((bf16[96,1280]{1,0:T(8,128)(2,1)}, bf16[96,1280]{1,0:T(8,128)(2,1)}, u32[]{:S(2)}, u32[]{:S(2)}) %collective-permute-start.4) | collective-permute-done | bytes 245792 | tf_op jit(solution)/shard_map/ppermute | solution.py:24
  17.5 0.9 %copy-done.1 = bf16[96,1280]{1,0:T(8,128)(2,1)S(1)} copy-done((bf16[96,1280]{1,0:T(8,128)(2,1)S(1)}, bf16[96,1280]{1,0:T(8,128)(2,1)}, u32[]{:S(2)}) %copy-start.1) | copy-done | bytes 245784
  18.4 1.0 %pass.1.refs_4_.refs_3_ = bf16[96,1280]{1,0:T(8,128)(2,1)S(1)} custom-call(bf16[96,1280]{1,0:T(8,128)(2,1)} %collective-permute-done.4.refs_0_, bf16[96,1280]{1,0:T(8,128)(2,1)S(1)} %copy-done.1, bf16[96,1280]{1,0:T(8,128)(2,1)} %get-tuple-element.17.refs_2_), custom_call_target="tpu_custom_call" | custom-call | bytes 491520 | tf_op jit(solution)/shard_map/pass/pallas_call | solution.py:68
  19.4 1.0 %collective-permute-start.7 = (bf16[96,1280]{1,0:T(8,128)(2,1)S(1)}, bf16[96,1280]{1,0:T(8,128)(2,1)}, u32[]{:S(2)}, u32[]{:S(2)}) collective-permute-start(bf16[96,1280]{1,0:T(8,128)(2,1)S(1)} %pass.1.refs_4_.refs_3_), channel_id=1, source_target_pairs={{0,1},{1,0},{2,3},{3,2},{4,5},{5,4},{6,7},{7,6},{8,9},{9,8},{10,11... | collective-permute-start | bytes 737288 | tf_op jit(solution)/shard_map/ppermute | solution.py:24
  20.5 1.6 %send_far.1.refs_5_ = bf16[96,1280]{1,0:T(8,128)(2,1)S(1)} custom-call(s32[1]{0:T(128)} %bitcast.5.refs_0_, bf16[1280,1280]{1,0:T(8,128)(2,1)S(1)} %get-tuple-element.16.refs_1_, bf16[96,1280]{1,0:T(8,128)(2,1)} %collective-permute-done.2.refs_2_.refs_3_, bf16[96,1280]{1,0:T(8,128)(2,1)} %collective-permute-done.3.refs_3_.refs_4_, ...), custom_call_target="tpu_custom_call" | custom-call | flops 314572800 | bytes 3522560 | tf_op jit(solution)/shard_map/send_far/pallas_call | solution.py:68
  22.1 1.1 %collective-permute-start.8 = (bf16[96,1280]{1,0:T(8,128)(2,1)S(1)}, bf16[96,1280]{1,0:T(8,128)(2,1)S(1)}, u32[]{:S(2)}, u32[]{:S(2)}) collective-permute-start(bf16[96,1280]{1,0:T(8,128)(2,1)S(1)} %send_far.1.refs_5_), channel_id=1, source_target_pairs={{0,1},{1,0},{2,3},{3,2},{4,5},{5,4},{6,7},{7,6},{8,9},{9,8},{10,11... | collective-permute-start | bytes 737288 | tf_op jit(solution)/shard_map/ppermute | solution.py:24
  23.2 2.6 %pair_near.1.refs_1_.refs_0_ = bf16[96,1280]{1,0:T(8,128)(2,1)S(1)} custom-call(s32[1]{0:T(128)} %bitcast.5.refs_0_, bf16[1280,1280]{1,0:T(8,128)(2,1)S(1)} %get-tuple-element.16.refs_1_, bf16[96,1280]{1,0:T(8,128)(2,1)} %collective-permute-done.1.refs_2_, bf16[96,1280]{1,0:T(8,128)(2,1)} %refs_3_.1, bf16[96,1280]{1,0:T(8,128)(2,1)} %copy-done.4, ...), custom_call_target="tpu_custom_call" | custom-call | flops 314572800 | bytes 3768320 | tf_op jit(solution)/shard_map/pair_near/pallas_call | solution.py:68
  25.8 2.8 %collective-permute-start.6 = (bf16[96,1280]{1,0:T(8,128)(2,1)S(1)}, bf16[96,1280]{1,0:T(8,128)(2,1)S(1)}, u32[]{:S(2)}, u32[]{:S(2)}) collective-permute-start(bf16[96,1280]{1,0:T(8,128)(2,1)S(1)} %pair_near.1.refs_1_.refs_0_), channel_id=1, source_target_pairs={{0,3},{1,2},{2,1},{3,0},{4,7},{5,6},{6,5},{7,4},{8,11},{9,10},{10,... | collective-permute-start | bytes 737288 | tf_op jit(solution)/shard_map/ppermute | solution.py:24
  28.7 1.9 %load_out.1.refs_5_.refs_6_ = bf16[1280,1280]{1,0:T(8,128)(2,1)S(1)} custom-call(bf16[1280,1280]{1,0:T(8,128)(2,1)} %refs_0_.1, bf16[96,1280]{1,0:T(8,128)(2,1)S(1)} %pair_near.1.refs_1_.refs_0_), custom_call_target="tpu_custom_call" | custom-call | bytes 6553600 | tf_op jit(solution)/shard_map/load_out/pallas_call | solution.py:68
  30.6 2.4 %rotate.1 = (f32[96,1280]{1,0:T(8,128)S(1)}, f32[96,1280]{1,0:T(8,128)S(1)}, bf16[96,1280]{1,0:T(8,128)(2,1)S(1)}, bf16[96,1280]{1,0:T(8,128)(2,1)S(1)}) custom-call(s32[5]{0:T(128)S(1)} %stack.51.refs_0_, bf16[96,1280]{1,0:T(8,128)(2,1)S(1)} %copy-done.3, bf16[96,1280]{1,0:T(8,128)(2,1)S(1)} %copy-done.2, bf16[96,1280]{1,0:T(8,128)(2,1)S(1)} %pass.1.refs_4_.refs_3_, ...), custom_call_target="tpu_custom_call" | custom-call | flops 1258291200 | bytes 5734400 | tf_op jit(solution)/shard_map/rotate/pallas_call | solution.py:68
  33.1 2.2 %all_gather.6.refs_2_ = bf16[192,1280]{1,0:T(8,128)(2,1)S(1)} all-gather(bf16[96,1280]{1,0:T(8,128)(2,1)S(1)} %get-tuple-element.20), channel_id=1, replica_groups={{0,4},{8,12},{1,5},{9,13},{2,6},{10,14},{3,7},{11,15},{16,20},{24,28},{..., dimensions={0}, use_global_device_ids=true | all-gather | bytes 737280 | tf_op jit(solution)/shard_map/all_gather | solution.py:309
  35.3 1.6 %pair_far.1.refs_3_.refs_0_ = bf16[96,1280]{1,0:T(8,128)(2,1)S(1)} custom-call(s32[1]{0:T(128)} %bitcast.5.refs_0_, bf16[1280,1280]{1,0:T(8,128)(2,1)S(1)} %get-tuple-element.16.refs_1_, bf16[96,1280]{1,0:T(8,128)(2,1)S(1)} %collective-permute-done.8.refs_2_, bf16[96,1280]{1,0:T(8,128)(2,1)} %collective-permute-done.2.refs_2_.refs_3_, ...), custom_call_target="tpu_custom_call" | custom-call | flops 314572800 | bytes 3768320 | tf_op jit(solution)/shard_map/pair_far/pallas_call | solution.py:68
  37.0 1.1 %collective-permute-start.10 = (bf16[96,1280]{1,0:T(8,128)(2,1)S(1)}, bf16[96,1280]{1,0:T(8,128)(2,1)S(1)}, u32[]{:S(2)}, u32[]{:S(2)}) collective-permute-start(bf16[96,1280]{1,0:T(8,128)(2,1)S(1)} %pair_far.1.refs_3_.refs_0_), channel_id=1, source_target_pairs={{0,3},{1,2},{2,1},{3,0},{4,7},{5,6},{6,5},{7,4},{8,11},{9,10},{10,... | collective-permute-start | bytes 737288 | tf_op jit(solution)/shard_map/ppermute | solution.py:24
  38.1 2.1 %all_gather.7.refs_2_ = bf16[192,1280]{1,0:T(8,128)(2,1)S(1)} all-gather(bf16[96,1280]{1,0:T(8,128)(2,1)S(1)} %get-tuple-element.22.refs_5_), channel_id=1, replica_groups={{0,4},{8,12},{1,5},{9,13},{2,6},{10,14},{3,7},{11,15},{16,20},{24,28},{..., dimensions={0}, use_global_device_ids=true | all-gather | bytes 737280 | tf_op jit(solution)/shard_map/all_gather | solution.py:309
  40.5 1.6 %collective-permute-start.12 = (bf16[96,1280]{1,0:T(8,128)(2,1)S(1)}, bf16[96,1280]{1,0:T(8,128)(2,1)S(1)}, u32[]{:S(2)}, u32[]{:S(2)}) collective-permute-start(bf16[96,1280]{1,0:T(8,128)(2,1)S(1)} %get-tuple-element.25), channel_id=1, source_target_pairs={{0,8},{4,12},{8,0},{12,4},{1,9},{5,13},{9,1},{13,5},{2,10},{6,14},... | collective-permute-start | bytes 737288 | tf_op jit(solution)/shard_map/ppermute | solution.py:24
  42.1 0.5 collective-permute-start.13
  42.6 5.2 %collective-permute-done.10.refs_1_ = bf16[96,1280]{1,0:T(8,128)(2,1)S(1)} collective-permute-done((bf16[96,1280]{1,0:T(8,128)(2,1)S(1)}, bf16[96,1280]{1,0:T(8,128)(2,1)S(1)}, u32[]{:S(2)}, u32[]{:S(2)}) %collective-permute-start.10) | collective-permute-done | bytes 245792 | tf_op jit(solution)/shard_map/ppermute | solution.py:24
  47.8 1.9 %collective-permute-start.11 = (bf16[96,1280]{1,0:T(8,128)(2,1)S(1)}, bf16[96,1280]{1,0:T(8,128)(2,1)S(1)}, u32[]{:S(2)}, u32[]{:S(2)}) collective-permute-start(bf16[96,1280]{1,0:T(8,128)(2,1)S(1)} %total_far.1.refs_1_.refs_3_), channel_id=1, source_target_pairs={{0,1},{1,0},{2,3},{3,2},{4,5},{5,4},{6,7},{7,6},{8,9},{9,8},{10,11... | collective-permute-start | bytes 737288 | tf_op jit(solution)/shard_map/ppermute | solution.py:24
  49.7 2.6 %collective-permute-done.9.refs_0_.refs_2_ = bf16[96,1280]{1,0:T(8,128)(2,1)S(1)} collective-permute-done((bf16[96,1280]{1,0:T(8,128)(2,1)S(1)}, bf16[96,1280]{1,0:T(8,128)(2,1)S(1)}, u32[]{:S(2)}, u32[]{:S(2)}) %collective-permute-start.9) | collective-permute-done | bytes 245792 | tf_op jit(solution)/shard_map/ppermute | solution.py:24
  52.3 1.5 %collective-permute-done.13.refs_1_ = bf16[96,1280]{1,0:T(8,128)(2,1)S(1)} collective-permute-done((bf16[96,1280]{1,0:T(8,128)(2,1)S(1)}, bf16[96,1280]{1,0:T(8,128)(2,1)S(1)}, u32[]{:S(2)}, u32[]{:S(2)}) %collective-permute-start.13) | collective-permute-done | bytes 245792 | tf_op jit(solution)/shard_map/ppermute | solution.py:24
  54.5 2.9 %collective-permute-done.11.refs_0_.refs_4_ = bf16[96,1280]{1,0:T(8,128)(2,1)S(1)} collective-permute-done((bf16[96,1280]{1,0:T(8,128)(2,1)S(1)}, bf16[96,1280]{1,0:T(8,128)(2,1)S(1)}, u32[]{:S(2)}, u32[]{:S(2)}) %collective-permute-start.11) | collective-permute-done | bytes 245792 | tf_op jit(solution)/shard_map/ppermute | solution.py:24
  57.5 16.2 %scores.1.refs_1_ = f32[16,8,128]{2,1,0:T(8,128)S(1)} custom-call(s32[5]{0:T(128)S(1)} %stack.45.refs_0_, bf16[96,1280]{1,0:T(8,128)(2,1)S(1)} %total_near.1.refs_2_.refs_1_, bf16[96,1280]{1,0:T(8,128)(2,1)S(1)} %collective-permute-done.9.refs_0_.refs_2_, bf16[96,1280]{1,0:T(8,128)(2,1)S(1)} %total_far.1.refs_1_.refs_3_, ...), custom_call_target="tpu_custom_call" | custom-call | flops 10066329600 | bytes 34799616 | tf_op jit(solution)/shard_map/scores/pallas_call | solution.py:68
  73.7 10.0 %all_to_all.5.refs_0_ = f32[16,8,128]{2,1,0:T(8,128)S(1)} all-to-all(f32[16,8,128]{2,1,0:T(8,128)S(1)} %scores.1.refs_1_), channel_id=1, replica_groups=mesh['groups'=2,'panel'=4,'tok'=4] {'panel','tok'}, dimensions={0} | all-to-all | bytes 131072 | tf_op jit(solution)/shard_map/all_to_all | solution.py:344
  83.7 0.6 final.1
  (32 shorter events, 1.7 us)
Async XLA Ops:
  0.0 7.1 %collective-permute-start = (bf16[96,1280]{1,0:T(8,128)(2,1)}, bf16[96,1280]{1,0:T(8,128)(2,1)S(1)}, u32[]{:S(2)}, u32[]{:S(2)}) collective-permute-start(bf16[96,1280]{1,0:T(8,128)(2,1)} %refs_3_.1), channel_id=1, source_target_pairs={{0,4},{4,0},{8,12},{12,8},{1,5},{5,1},{9,13},{13,9},{2,6},{6,2},{1... | collective-permute-start | bytes 737288 | tf_op jit(solution)/shard_map/ppermute | solution.py:24
  0.5 14.5 %collective-permute-start.5 = (bf16[96,1280]{1,0:T(8,128)(2,1)}, bf16[96,1280]{1,0:T(8,128)(2,1)S(1)}, u32[]{:S(2)}, u32[]{:S(2)}) collective-permute-start(bf16[96,1280]{1,0:T(8,128)(2,1)} %refs_1_.3), channel_id=1, source_target_pairs={{0,1},{1,0},{2,3},{3,2},{4,5},{5,4},{6,7},{7,6},{8,9},{9,8},{10,11... | collective-permute-start | bytes 737288 | tf_op jit(solution)/shard_map/ppermute | solution.py:24
  3.0 14.4 %collective-permute-start.4 = (bf16[96,1280]{1,0:T(8,128)(2,1)}, bf16[96,1280]{1,0:T(8,128)(2,1)}, u32[]{:S(2)}, u32[]{:S(2)}) collective-permute-start(bf16[96,1280]{1,0:T(8,128)(2,1)} %refs_1_.3), channel_id=1, source_target_pairs={{0,2},{1,3},{2,0},{3,1},{4,6},{5,7},{6,4},{7,5},{8,10},{9,11},{10,... | collective-permute-start | bytes 737288 | tf_op jit(solution)/shard_map/ppermute | solution.py:24
  5.6 14.9 %collective-permute-start.2 = (bf16[96,1280]{1,0:T(8,128)(2,1)}, bf16[96,1280]{1,0:T(8,128)(2,1)}, u32[]{:S(2)}, u32[]{:S(2)}) collective-permute-start(bf16[96,1280]{1,0:T(8,128)(2,1)} %refs_3_.1), channel_id=1, source_target_pairs={{0,8},{4,12},{8,0},{12,4},{1,9},{5,13},{9,1},{13,5},{2,10},{6,14},... | collective-permute-start | bytes 737288 | tf_op jit(solution)/shard_map/ppermute | solution.py:24
  7.1 13.4 %collective-permute-start.3 = (bf16[96,1280]{1,0:T(8,128)(2,1)}, bf16[96,1280]{1,0:T(8,128)(2,1)}, u32[]{:S(2)}, u32[]{:S(2)}) collective-permute-start(bf16[96,1280]{1,0:T(8,128)(2,1)} %refs_3_.1), channel_id=1, source_target_pairs={{0,12},{4,8},{8,4},{12,0},{1,13},{5,9},{9,5},{13,1},{2,14},{6,10},... | collective-permute-start | bytes 737288 | tf_op jit(solution)/shard_map/ppermute | solution.py:24
  7.1 0.7 copy-start.4
  11.6 11.7 %collective-permute-start.1 = (bf16[96,1280]{1,0:T(8,128)(2,1)}, bf16[96,1280]{1,0:T(8,128)(2,1)}, u32[]{:S(2)}, u32[]{:S(2)}) collective-permute-start(bf16[96,1280]{1,0:T(8,128)(2,1)} %get-tuple-element.17.refs_2_), channel_id=1, source_target_pairs={{0,1},{1,0},{2,3},{3,2},{4,5},{5,4},{6,7},{7,6},{8,9},{9,8},{10,11... | collective-permute-start | bytes 737288 | tf_op jit(solution)/shard_map/ppermute | solution.py:24
  15.0 0.7 copy-start
  17.5 0.9 %copy-start.1 = (bf16[96,1280]{1,0:T(8,128)(2,1)S(1)}, bf16[96,1280]{1,0:T(8,128)(2,1)}, u32[]{:S(2)}) copy-start(bf16[96,1280]{1,0:T(8,128)(2,1)} %copy-done) | copy-start | bytes 737284
  19.4 11.2 %collective-permute-start.7 = (bf16[96,1280]{1,0:T(8,128)(2,1)S(1)}, bf16[96,1280]{1,0:T(8,128)(2,1)}, u32[]{:S(2)}, u32[]{:S(2)}) collective-permute-start(bf16[96,1280]{1,0:T(8,128)(2,1)S(1)} %pass.1.refs_4_.refs_3_), channel_id=1, source_target_pairs={{0,1},{1,0},{2,3},{3,2},{4,5},{5,4},{6,7},{7,6},{8,9},{9,8},{10,11... | collective-permute-start | bytes 737288 | tf_op jit(solution)/shard_map/ppermute | solution.py:24
  22.1 13.2 %collective-permute-start.8 = (bf16[96,1280]{1,0:T(8,128)(2,1)S(1)}, bf16[96,1280]{1,0:T(8,128)(2,1)S(1)}, u32[]{:S(2)}, u32[]{:S(2)}) collective-permute-start(bf16[96,1280]{1,0:T(8,128)(2,1)S(1)} %send_far.1.refs_5_), channel_id=1, source_target_pairs={{0,1},{1,0},{2,3},{3,2},{4,5},{5,4},{6,7},{7,6},{8,9},{9,8},{10,11... | collective-permute-start | bytes 737288 | tf_op jit(solution)/shard_map/ppermute | solution.py:24
  25.8 4.8 %copy-start.2 = (bf16[96,1280]{1,0:T(8,128)(2,1)S(1)}, bf16[96,1280]{1,0:T(8,128)(2,1)}, u32[]{:S(2)}) copy-start(bf16[96,1280]{1,0:T(8,128)(2,1)} %copy-done) | copy-start | bytes 737284
  25.8 4.8 %copy-start.3 = (bf16[96,1280]{1,0:T(8,128)(2,1)S(1)}, bf16[96,1280]{1,0:T(8,128)(2,1)}, u32[]{:S(2)}) copy-start(bf16[96,1280]{1,0:T(8,128)(2,1)} %refs_1_.3) | copy-start | bytes 737284
  25.8 14.5 %collective-permute-start.6 = (bf16[96,1280]{1,0:T(8,128)(2,1)S(1)}, bf16[96,1280]{1,0:T(8,128)(2,1)S(1)}, u32[]{:S(2)}, u32[]{:S(2)}) collective-permute-start(bf16[96,1280]{1,0:T(8,128)(2,1)S(1)} %pair_near.1.refs_1_.refs_0_), channel_id=1, source_target_pairs={{0,3},{1,2},{2,1},{3,0},{4,7},{5,6},{6,5},{7,4},{8,11},{9,10},{10,... | collective-permute-start | bytes 737288 | tf_op jit(solution)/shard_map/ppermute | solution.py:24
  37.0 10.8 %collective-permute-start.10 = (bf16[96,1280]{1,0:T(8,128)(2,1)S(1)}, bf16[96,1280]{1,0:T(8,128)(2,1)S(1)}, u32[]{:S(2)}, u32[]{:S(2)}) collective-permute-start(bf16[96,1280]{1,0:T(8,128)(2,1)S(1)} %pair_far.1.refs_3_.refs_0_), channel_id=1, source_target_pairs={{0,3},{1,2},{2,1},{3,0},{4,7},{5,6},{6,5},{7,4},{8,11},{9,10},{10,... | collective-permute-start | bytes 737288 | tf_op jit(solution)/shard_map/ppermute | solution.py:24
  40.4 11.9 %collective-permute-start.9 = (bf16[96,1280]{1,0:T(8,128)(2,1)S(1)}, bf16[96,1280]{1,0:T(8,128)(2,1)S(1)}, u32[]{:S(2)}, u32[]{:S(2)}) collective-permute-start(bf16[96,1280]{1,0:T(8,128)(2,1)S(1)} %total_near.1.refs_2_.refs_1_), channel_id=1, source_target_pairs={{0,1},{1,0},{2,3},{3,2},{4,5},{5,4},{6,7},{7,6},{8,9},{9,8},{10,11... | collective-permute-start | bytes 737288 | tf_op jit(solution)/shard_map/ppermute | solution.py:24
  40.5 11.8 %collective-permute-start.12 = (bf16[96,1280]{1,0:T(8,128)(2,1)S(1)}, bf16[96,1280]{1,0:T(8,128)(2,1)S(1)}, u32[]{:S(2)}, u32[]{:S(2)}) collective-permute-start(bf16[96,1280]{1,0:T(8,128)(2,1)S(1)} %get-tuple-element.25), channel_id=1, source_target_pairs={{0,8},{4,12},{8,0},{12,4},{1,9},{5,13},{9,1},{13,5},{2,10},{6,14},... | collective-permute-start | bytes 737288 | tf_op jit(solution)/shard_map/ppermute | solution.py:24
  42.1 11.7 %collective-permute-start.13 = (bf16[96,1280]{1,0:T(8,128)(2,1)S(1)}, bf16[96,1280]{1,0:T(8,128)(2,1)S(1)}, u32[]{:S(2)}, u32[]{:S(2)}) collective-permute-start(bf16[96,1280]{1,0:T(8,128)(2,1)S(1)} %get-tuple-element.23.refs_2_), channel_id=1, source_target_pairs={{0,8},{4,12},{8,0},{12,4},{1,9},{5,13},{9,1},{13,5},{2,10},{6,14},... | collective-permute-start | bytes 737288 | tf_op jit(solution)/shard_map/ppermute | solution.py:24
  47.8 9.7 %collective-permute-start.11 = (bf16[96,1280]{1,0:T(8,128)(2,1)S(1)}, bf16[96,1280]{1,0:T(8,128)(2,1)S(1)}, u32[]{:S(2)}, u32[]{:S(2)}) collective-permute-start(bf16[96,1280]{1,0:T(8,128)(2,1)S(1)} %total_far.1.refs_1_.refs_3_), channel_id=1, source_target_pairs={{0,1},{1,0},{2,3},{3,2},{4,5},{5,4},{6,7},{7,6},{8,9},{9,8},{10,11... | collective-permute-start | bytes 737288 | tf_op jit(solution)/shard_map/ppermute | solution.py:24
  53.9 3.6 %collective-permute-start.15 = (bf16[96,1280]{1,0:T(8,128)(2,1)S(1)}, bf16[96,1280]{1,0:T(8,128)(2,1)S(1)}, u32[]{:S(2)}, u32[]{:S(2)}) collective-permute-start(bf16[96,1280]{1,0:T(8,128)(2,1)S(1)} %panel_sum_low.1.refs_1_.refs_6_), channel_id=1, source_target_pairs={{0,4},{4,0},{8,12},{12,8},{1,5},{5,1},{9,13},{13,9},{2,6},{6,2},{1... | collective-permute-start | bytes 737288 | tf_op jit(solution)/shard_map/ppermute | solution.py:24
  53.9 3.5 %collective-permute-start.14 = (bf16[96,1280]{1,0:T(8,128)(2,1)S(1)}, bf16[96,1280]{1,0:T(8,128)(2,1)S(1)}, u32[]{:S(2)}, u32[]{:S(2)}) collective-permute-start(bf16[96,1280]{1,0:T(8,128)(2,1)S(1)} %panel_sum_top.1.refs_2_.refs_5_), channel_id=1, source_target_pairs={{0,4},{4,0},{8,12},{12,8},{1,5},{5,1},{9,13},{13,9},{2,6},{6,2},{1... | collective-permute-start | bytes 737288 | tf_op jit(solution)/shard_map/ppermute | solution.py:24

commit v7 on v5

--- a/solution.py
+++ b/solution.py
@@ -321,8 +321,7 @@
     mine_low, low = chip_sum("chip_sum_low", mine_low, low)
     (total2,) = steps("total_far", add_body, [pair2, got2], [narrow(size, cols)])
     back2 = swap(total2, "tok", 1)
-    steps("mark_near", mark_body, [], [wide(8, LANES)], after=[back1])
-    (mine_top,) = steps("panel_sum_top", panel_sum_body, [mine_top, top], [narrow(size, depth)], weight=8_000_000)
+    (mine_top,) = steps("panel_sum_top", panel_sum_body, [mine_top, top], [narrow(size, depth)], after=[back1])
     other_top = swap(mine_top, "panel", 1)
     (mine_low,) = steps("panel_sum_low", panel_sum_body, [mine_low, low], [narrow(size, depth)])
     other_low = swap(mine_low, "panel", 1)

time: 84.6 us -> 84.5 us (level)
    pallas_call x17 -> x16, Pallas kernels: 32.1 us -> 32.1 us  [__call__(): pl.pallas_call(kernel, grid=(1,), in_specs=specs, out_specs=[block(x) for...]
where the time goes in v7:
time: 84.5 us; the launch traced here: 84.1 us
  Pallas kernels  32.1 us (38%)
  starting transfers between devices  18.4 us (22%)
  waiting for transfers between devices  16.8 us (20%)
  blocking collectives  14.1 us (17%)
  local copies, waits for them, and re-layouts  2.54 us (3%)
    pallas_call x16, Pallas kernels, __call__(): pl.pallas_call(kernel, grid=(1,), in_specs=specs, out_specs=[block(x) for...  32.1 us
    ppermute x16, starting transfers between devices, swap(): lax.ppermute(value, axis, [(i, i ^ mask) for i in range(lax.axis_size(axi...  18.4 us
    ppermute x16, waiting for transfers between devices, swap(): lax.ppermute(value, axis, [(i, i ^ mask) for i in range(lax.axis_size(axi...  16.8 us
    all_to_all x1, blocking collectives, on_lines_of_four(): lax.all_to_all(partial, ('panel', 'tok'), split_axis=0, concat_axis=0, ti...  9.8 us
    all_gather x2, blocking collectives, chip_sum(): lax.all_gather(other, 'panel', axis=0, tiled=True, axis_index_groups=chips)  4.3 us
    unnamed x10, local copies, waits for them, and re-layouts  2.37 us
  transfers between devices with their start and end apart: 16, of which 6 were waited for; matrix products, arithmetic and copies ran while one was open for 0% of the time, Pallas kernels for 18%

profile of v7, /device:TPU:0, one launch (start us, length us, event | category | flops | bytes accessed | tf_op | source)
XLA Modules:
  0.0 84.1 jit_solution(4727899632050400723)
XLA Ops:
  0.5 2.6 %collective-permute-start.5 = (bf16[96,1280]{1,0:T(8,128)(2,1)}, bf16[96,1280]{1,0:T(8,128)(2,1)S(1)}, u32[]{:S(2)}, u32[]{:S(2)}) collective-permute-start(bf16[96,1280]{1,0:T(8,128)(2,1)} %refs_1_.3), channel_id=1, source_target_pairs={{0,1},{1,0},{2,3},{3,2},{4,5},{5,4},{6,7},{7,6},{8,9},{9,8},{10,11... | collective-permute-start | bytes 737288 | tf_op jit(solution)/shard_map/ppermute | solution.py:24
  3.0 2.6 %collective-permute-start.4 = (bf16[96,1280]{1,0:T(8,128)(2,1)}, bf16[96,1280]{1,0:T(8,128)(2,1)}, u32[]{:S(2)}, u32[]{:S(2)}) collective-permute-start(bf16[96,1280]{1,0:T(8,128)(2,1)} %refs_1_.3), channel_id=1, source_target_pairs={{0,2},{1,3},{2,0},{3,1},{4,6},{5,7},{6,4},{7,5},{8,10},{9,11},{10,... | collective-permute-start | bytes 737288 | tf_op jit(solution)/shard_map/ppermute | solution.py:24
  5.6 1.5 %collective-permute-start.2 = (bf16[96,1280]{1,0:T(8,128)(2,1)}, bf16[96,1280]{1,0:T(8,128)(2,1)}, u32[]{:S(2)}, u32[]{:S(2)}) collective-permute-start(bf16[96,1280]{1,0:T(8,128)(2,1)} %refs_3_.1), channel_id=1, source_target_pairs={{0,8},{4,12},{8,0},{12,4},{1,9},{5,13},{9,1},{13,5},{2,10},{6,14},... | collective-permute-start | bytes 737288 | tf_op jit(solution)/shard_map/ppermute | solution.py:24
  7.1 0.7 copy-done.4
  7.8 3.8 %send_near.1 = (bf16[1280,1280]{1,0:T(8,128)(2,1)S(1)}, bf16[96,1280]{1,0:T(8,128)(2,1)}) custom-call(s32[1]{0:T(128)} %bitcast.5.refs_0_, bf16[1280,1280]{1,0:T(8,128)(2,1)} %refs_1_.2, bf16[96,1280]{1,0:T(8,128)(2,1)} %refs_3_.1, bf16[96,1280]{1,0:T(8,128)(2,1)} %copy-done.4), custom_call_target="tpu_custom_call" | custom-call | flops 314572800 | bytes 6799360 | tf_op jit(solution)/shard_map/send_near/pallas_call | solution.py:68
  11.6 0.5 collective-permute-start.1
  12.1 2.9 %collective-permute-done.5.refs_1_.refs_2_ = bf16[96,1280]{1,0:T(8,128)(2,1)S(1)} collective-permute-done((bf16[96,1280]{1,0:T(8,128)(2,1)}, bf16[96,1280]{1,0:T(8,128)(2,1)S(1)}, u32[]{:S(2)}, u32[]{:S(2)}) %collective-permute-start.5) | collective-permute-done | bytes 245792 | tf_op jit(solution)/shard_map/ppermute | solution.py:24
  15.0 0.7 copy-done
  15.7 1.7 %collective-permute-done.4.refs_0_ = bf16[96,1280]{1,0:T(8,128)(2,1)} collective-permute-done((bf16[96,1280]{1,0:T(8,128)(2,1)}, bf16[96,1280]{1,0:T(8,128)(2,1)}, u32[]{:S(2)}, u32[]{:S(2)}) %collective-permute-start.4) | collective-permute-done | bytes 245792 | tf_op jit(solution)/shard_map/ppermute | solution.py:24
  17.5 0.9 %copy-done.1 = bf16[96,1280]{1,0:T(8,128)(2,1)S(1)} copy-done((bf16[96,1280]{1,0:T(8,128)(2,1)S(1)}, bf16[96,1280]{1,0:T(8,128)(2,1)}, u32[]{:S(2)}) %copy-start.1) | copy-done | bytes 245784
  18.4 1.0 %pass.1.refs_4_.refs_3_ = bf16[96,1280]{1,0:T(8,128)(2,1)S(1)} custom-call(bf16[96,1280]{1,0:T(8,128)(2,1)} %collective-permute-done.4.refs_0_, bf16[96,1280]{1,0:T(8,128)(2,1)S(1)} %copy-done.1, bf16[96,1280]{1,0:T(8,128)(2,1)} %get-tuple-element.17.refs_2_), custom_call_target="tpu_custom_call" | custom-call | bytes 491520 | tf_op jit(solution)/shard_map/pass/pallas_call | solution.py:68
  19.4 1.0 %collective-permute-start.8 = (bf16[96,1280]{1,0:T(8,128)(2,1)S(1)}, bf16[96,1280]{1,0:T(8,128)(2,1)}, u32[]{:S(2)}, u32[]{:S(2)}) collective-permute-start(bf16[96,1280]{1,0:T(8,128)(2,1)S(1)} %pass.1.refs_4_.refs_3_), channel_id=1, source_target_pairs={{0,1},{1,0},{2,3},{3,2},{4,5},{5,4},{6,7},{7,6},{8,9},{9,8},{10,11... | collective-permute-start | bytes 737288 | tf_op jit(solution)/shard_map/ppermute | solution.py:24
  20.5 1.6 %send_far.1.refs_5_ = bf16[96,1280]{1,0:T(8,128)(2,1)S(1)} custom-call(s32[1]{0:T(128)} %bitcast.5.refs_0_, bf16[1280,1280]{1,0:T(8,128)(2,1)S(1)} %get-tuple-element.16.refs_1_, bf16[96,1280]{1,0:T(8,128)(2,1)} %collective-permute-done.2.refs_2_.refs_3_, bf16[96,1280]{1,0:T(8,128)(2,1)} %collective-permute-done.3.refs_3_.refs_4_, ...), custom_call_target="tpu_custom_call" | custom-call | flops 314572800 | bytes 3522560 | tf_op jit(solution)/shard_map/send_far/pallas_call | solution.py:68
  22.1 1.1 %collective-permute-start.7 = (bf16[96,1280]{1,0:T(8,128)(2,1)S(1)}, bf16[96,1280]{1,0:T(8,128)(2,1)S(1)}, u32[]{:S(2)}, u32[]{:S(2)}) collective-permute-start(bf16[96,1280]{1,0:T(8,128)(2,1)S(1)} %send_far.1.refs_5_), channel_id=1, source_target_pairs={{0,1},{1,0},{2,3},{3,2},{4,5},{5,4},{6,7},{7,6},{8,9},{9,8},{10,11... | collective-permute-start | bytes 737288 | tf_op jit(solution)/shard_map/ppermute | solution.py:24
  23.2 2.6 %pair_near.1.refs_1_.refs_0_ = bf16[96,1280]{1,0:T(8,128)(2,1)S(1)} custom-call(s32[1]{0:T(128)} %bitcast.5.refs_0_, bf16[1280,1280]{1,0:T(8,128)(2,1)S(1)} %get-tuple-element.16.refs_1_, bf16[96,1280]{1,0:T(8,128)(2,1)} %collective-permute-done.1.refs_2_, bf16[96,1280]{1,0:T(8,128)(2,1)} %refs_3_.1, bf16[96,1280]{1,0:T(8,128)(2,1)} %copy-done.4, ...), custom_call_target="tpu_custom_call" | custom-call | flops 314572800 | bytes 3768320 | tf_op jit(solution)/shard_map/pair_near/pallas_call | solution.py:68
  25.8 2.8 %collective-permute-start.6 = (bf16[96,1280]{1,0:T(8,128)(2,1)S(1)}, bf16[96,1280]{1,0:T(8,128)(2,1)S(1)}, u32[]{:S(2)}, u32[]{:S(2)}) collective-permute-start(bf16[96,1280]{1,0:T(8,128)(2,1)S(1)} %pair_near.1.refs_1_.refs_0_), channel_id=1, source_target_pairs={{0,3},{1,2},{2,1},{3,0},{4,7},{5,6},{6,5},{7,4},{8,11},{9,10},{10,... | collective-permute-start | bytes 737288 | tf_op jit(solution)/shard_map/ppermute | solution.py:24
  28.7 1.9 %load_out.1.refs_5_.refs_6_ = bf16[1280,1280]{1,0:T(8,128)(2,1)S(1)} custom-call(bf16[1280,1280]{1,0:T(8,128)(2,1)} %refs_0_.1, bf16[96,1280]{1,0:T(8,128)(2,1)S(1)} %pair_near.1.refs_1_.refs_0_), custom_call_target="tpu_custom_call" | custom-call | bytes 6553600 | tf_op jit(solution)/shard_map/load_out/pallas_call | solution.py:68
  30.6 2.4 %rotate.1 = (f32[96,1280]{1,0:T(8,128)S(1)}, f32[96,1280]{1,0:T(8,128)S(1)}, bf16[96,1280]{1,0:T(8,128)(2,1)S(1)}, bf16[96,1280]{1,0:T(8,128)(2,1)S(1)}) custom-call(s32[5]{0:T(128)S(1)} %stack.51.refs_0_, bf16[96,1280]{1,0:T(8,128)(2,1)S(1)} %copy-done.3, bf16[96,1280]{1,0:T(8,128)(2,1)S(1)} %copy-done.2, bf16[96,1280]{1,0:T(8,128)(2,1)S(1)} %pass.1.refs_4_.refs_3_, ...), custom_call_target="tpu_custom_call" | custom-call | flops 1258291200 | bytes 5734400 | tf_op jit(solution)/shard_map/rotate/pallas_call | solution.py:68
  33.1 2.2 %all_gather.6.refs_2_ = bf16[192,1280]{1,0:T(8,128)(2,1)S(1)} all-gather(bf16[96,1280]{1,0:T(8,128)(2,1)S(1)} %get-tuple-element.19), channel_id=1, replica_groups={{0,4},{8,12},{1,5},{9,13},{2,6},{10,14},{3,7},{11,15},{16,20},{24,28},{..., dimensions={0}, use_global_device_ids=true | all-gather | bytes 737280 | tf_op jit(solution)/shard_map/all_gather | solution.py:309
  35.3 1.6 %pair_far.1.refs_2_.refs_0_ = bf16[96,1280]{1,0:T(8,128)(2,1)S(1)} custom-call(s32[1]{0:T(128)} %bitcast.5.refs_0_, bf16[1280,1280]{1,0:T(8,128)(2,1)S(1)} %get-tuple-element.16.refs_1_, bf16[96,1280]{1,0:T(8,128)(2,1)S(1)} %collective-permute-done.7.refs_2_, bf16[96,1280]{1,0:T(8,128)(2,1)} %collective-permute-done.2.refs_2_.refs_3_, ...), custom_call_target="tpu_custom_call" | custom-call | flops 314572800 | bytes 3768320 | tf_op jit(solution)/shard_map/pair_far/pallas_call | solution.py:68
  37.0 1.1 %collective-permute-start.10 = (bf16[96,1280]{1,0:T(8,128)(2,1)S(1)}, bf16[96,1280]{1,0:T(8,128)(2,1)S(1)}, u32[]{:S(2)}, u32[]{:S(2)}) collective-permute-start(bf16[96,1280]{1,0:T(8,128)(2,1)S(1)} %pair_far.1.refs_2_.refs_0_), channel_id=1, source_target_pairs={{0,3},{1,2},{2,1},{3,0},{4,7},{5,6},{6,5},{7,4},{8,11},{9,10},{10,... | collective-permute-start | bytes 737288 | tf_op jit(solution)/shard_map/ppermute | solution.py:24
  38.1 2.1 %all_gather.7.refs_2_ = bf16[192,1280]{1,0:T(8,128)(2,1)S(1)} all-gather(bf16[96,1280]{1,0:T(8,128)(2,1)S(1)} %get-tuple-element.21.refs_5_), channel_id=1, replica_groups={{0,4},{8,12},{1,5},{9,13},{2,6},{10,14},{3,7},{11,15},{16,20},{24,28},{..., dimensions={0}, use_global_device_ids=true | all-gather | bytes 737280 | tf_op jit(solution)/shard_map/all_gather | solution.py:309
  40.2 1.5 %collective-permute-start.12 = (bf16[96,1280]{1,0:T(8,128)(2,1)S(1)}, bf16[96,1280]{1,0:T(8,128)(2,1)S(1)}, u32[]{:S(2)}, u32[]{:S(2)}) collective-permute-start(bf16[96,1280]{1,0:T(8,128)(2,1)S(1)} %get-tuple-element.25), channel_id=1, source_target_pairs={{0,8},{4,12},{8,0},{12,4},{1,9},{5,13},{9,1},{13,5},{2,10},{6,14},... | collective-permute-start | bytes 737288 | tf_op jit(solution)/shard_map/ppermute | solution.py:24
  42.0 0.6 collective-permute-start.13
  42.6 5.1 %collective-permute-done.10.refs_1_ = bf16[96,1280]{1,0:T(8,128)(2,1)S(1)} collective-permute-done((bf16[96,1280]{1,0:T(8,128)(2,1)S(1)}, bf16[96,1280]{1,0:T(8,128)(2,1)S(1)}, u32[]{:S(2)}, u32[]{:S(2)}) %collective-permute-start.10) | collective-permute-done | bytes 245792 | tf_op jit(solution)/shard_map/ppermute | solution.py:24
  47.7 1.9 %collective-permute-start.11 = (bf16[96,1280]{1,0:T(8,128)(2,1)S(1)}, bf16[96,1280]{1,0:T(8,128)(2,1)S(1)}, u32[]{:S(2)}, u32[]{:S(2)}) collective-permute-start(bf16[96,1280]{1,0:T(8,128)(2,1)S(1)} %total_far.1.refs_3_), channel_id=1, source_target_pairs={{0,1},{1,0},{2,3},{3,2},{4,5},{5,4},{6,7},{7,6},{8,9},{9,8},{10,11... | collective-permute-start | bytes 737288 | tf_op jit(solution)/shard_map/ppermute | solution.py:24
  49.7 2.6 %collective-permute-done.9.refs_2_ = bf16[96,1280]{1,0:T(8,128)(2,1)S(1)} collective-permute-done((bf16[96,1280]{1,0:T(8,128)(2,1)S(1)}, bf16[96,1280]{1,0:T(8,128)(2,1)S(1)}, u32[]{:S(2)}, u32[]{:S(2)}) %collective-permute-start.9) | collective-permute-done | bytes 245792 | tf_op jit(solution)/shard_map/ppermute | solution.py:24
  52.3 1.2 %collective-permute-done.13.refs_1_ = bf16[96,1280]{1,0:T(8,128)(2,1)S(1)} collective-permute-done((bf16[96,1280]{1,0:T(8,128)(2,1)S(1)}, bf16[96,1280]{1,0:T(8,128)(2,1)S(1)}, u32[]{:S(2)}, u32[]{:S(2)}) %collective-permute-start.13) | collective-permute-done | bytes 245792 | tf_op jit(solution)/shard_map/ppermute | solution.py:24
  54.2 3.2 %collective-permute-done.11.refs_0_.refs_4_ = bf16[96,1280]{1,0:T(8,128)(2,1)S(1)} collective-permute-done((bf16[96,1280]{1,0:T(8,128)(2,1)S(1)}, bf16[96,1280]{1,0:T(8,128)(2,1)S(1)}, u32[]{:S(2)}, u32[]{:S(2)}) %collective-permute-start.11) | collective-permute-done | bytes 245792 | tf_op jit(solution)/shard_map/ppermute | solution.py:24
  57.5 16.2 %scores.1.refs_1_ = f32[16,8,128]{2,1,0:T(8,128)S(1)} custom-call(s32[5]{0:T(128)S(1)} %stack.45.refs_0_, bf16[96,1280]{1,0:T(8,128)(2,1)S(1)} %total_near.1.refs_3_.refs_1_, bf16[96,1280]{1,0:T(8,128)(2,1)S(1)} %collective-permute-done.9.refs_2_, bf16[96,1280]{1,0:T(8,128)(2,1)S(1)} %total_far.1.refs_3_, ...), custom_call_target="tpu_custom_call" | custom-call | flops 10066329600 | bytes 34799616 | tf_op jit(solution)/shard_map/scores/pallas_call | solution.py:68
  73.7 9.8 %all_to_all.5.refs_0_ = f32[16,8,128]{2,1,0:T(8,128)S(1)} all-to-all(f32[16,8,128]{2,1,0:T(8,128)S(1)} %scores.1.refs_1_), channel_id=1, replica_groups=mesh['groups'=2,'panel'=4,'tok'=4] {'panel','tok'}, dimensions={0} | all-to-all | bytes 131072 | tf_op jit(solution)/shard_map/all_to_all | solution.py:343
  83.5 0.6 final.1
  (31 shorter events, 1.7 us)
Async XLA Ops:
  0.0 7.1 %collective-permute-start = (bf16[96,1280]{1,0:T(8,128)(2,1)}, bf16[96,1280]{1,0:T(8,128)(2,1)S(1)}, u32[]{:S(2)}, u32[]{:S(2)}) collective-permute-start(bf16[96,1280]{1,0:T(8,128)(2,1)} %refs_3_.1), channel_id=1, source_target_pairs={{0,4},{4,0},{8,12},{12,8},{1,5},{5,1},{9,13},{13,9},{2,6},{6,2},{1... | collective-permute-start | bytes 737288 | tf_op jit(solution)/shard_map/ppermute | solution.py:24
  0.5 14.5 %collective-permute-start.5 = (bf16[96,1280]{1,0:T(8,128)(2,1)}, bf16[96,1280]{1,0:T(8,128)(2,1)S(1)}, u32[]{:S(2)}, u32[]{:S(2)}) collective-permute-start(bf16[96,1280]{1,0:T(8,128)(2,1)} %refs_1_.3), channel_id=1, source_target_pairs={{0,1},{1,0},{2,3},{3,2},{4,5},{5,4},{6,7},{7,6},{8,9},{9,8},{10,11... | collective-permute-start | bytes 737288 | tf_op jit(solution)/shard_map/ppermute | solution.py:24
  3.0 14.4 %collective-permute-start.4 = (bf16[96,1280]{1,0:T(8,128)(2,1)}, bf16[96,1280]{1,0:T(8,128)(2,1)}, u32[]{:S(2)}, u32[]{:S(2)}) collective-permute-start(bf16[96,1280]{1,0:T(8,128)(2,1)} %refs_1_.3), channel_id=1, source_target_pairs={{0,2},{1,3},{2,0},{3,1},{4,6},{5,7},{6,4},{7,5},{8,10},{9,11},{10,... | collective-permute-start | bytes 737288 | tf_op jit(solution)/shard_map/ppermute | solution.py:24
  5.6 14.9 %collective-permute-start.2 = (bf16[96,1280]{1,0:T(8,128)(2,1)}, bf16[96,1280]{1,0:T(8,128)(2,1)}, u32[]{:S(2)}, u32[]{:S(2)}) collective-permute-start(bf16[96,1280]{1,0:T(8,128)(2,1)} %refs_3_.1), channel_id=1, source_target_pairs={{0,8},{4,12},{8,0},{12,4},{1,9},{5,13},{9,1},{13,5},{2,10},{6,14},... | collective-permute-start | bytes 737288 | tf_op jit(solution)/shard_map/ppermute | solution.py:24
  7.1 13.4 %collective-permute-start.3 = (bf16[96,1280]{1,0:T(8,128)(2,1)}, bf16[96,1280]{1,0:T(8,128)(2,1)}, u32[]{:S(2)}, u32[]{:S(2)}) collective-permute-start(bf16[96,1280]{1,0:T(8,128)(2,1)} %refs_3_.1), channel_id=1, source_target_pairs={{0,12},{4,8},{8,4},{12,0},{1,13},{5,9},{9,5},{13,1},{2,14},{6,10},... | collective-permute-start | bytes 737288 | tf_op jit(solution)/shard_map/ppermute | solution.py:24
  7.1 0.7 copy-start.4
  11.6 11.7 %collective-permute-start.1 = (bf16[96,1280]{1,0:T(8,128)(2,1)}, bf16[96,1280]{1,0:T(8,128)(2,1)}, u32[]{:S(2)}, u32[]{:S(2)}) collective-permute-start(bf16[96,1280]{1,0:T(8,128)(2,1)} %get-tuple-element.17.refs_2_), channel_id=1, source_target_pairs={{0,1},{1,0},{2,3},{3,2},{4,5},{5,4},{6,7},{7,6},{8,9},{9,8},{10,11... | collective-permute-start | bytes 737288 | tf_op jit(solution)/shard_map/ppermute | solution.py:24
  15.0 0.7 copy-start
  17.5 0.9 %copy-start.1 = (bf16[96,1280]{1,0:T(8,128)(2,1)S(1)}, bf16[96,1280]{1,0:T(8,128)(2,1)}, u32[]{:S(2)}) copy-start(bf16[96,1280]{1,0:T(8,128)(2,1)} %copy-done) | copy-start | bytes 737284
  19.4 11.2 %collective-permute-start.8 = (bf16[96,1280]{1,0:T(8,128)(2,1)S(1)}, bf16[96,1280]{1,0:T(8,128)(2,1)}, u32[]{:S(2)}, u32[]{:S(2)}) collective-permute-start(bf16[96,1280]{1,0:T(8,128)(2,1)S(1)} %pass.1.refs_4_.refs_3_), channel_id=1, source_target_pairs={{0,1},{1,0},{2,3},{3,2},{4,5},{5,4},{6,7},{7,6},{8,9},{9,8},{10,11... | collective-permute-start | bytes 737288 | tf_op jit(solution)/shard_map/ppermute | solution.py:24
  22.1 13.2 %collective-permute-start.7 = (bf16[96,1280]{1,0:T(8,128)(2,1)S(1)}, bf16[96,1280]{1,0:T(8,128)(2,1)S(1)}, u32[]{:S(2)}, u32[]{:S(2)}) collective-permute-start(bf16[96,1280]{1,0:T(8,128)(2,1)S(1)} %send_far.1.refs_5_), channel_id=1, source_target_pairs={{0,1},{1,0},{2,3},{3,2},{4,5},{5,4},{6,7},{7,6},{8,9},{9,8},{10,11... | collective-permute-start | bytes 737288 | tf_op jit(solution)/shard_map/ppermute | solution.py:24
  25.8 4.8 %copy-start.2 = (bf16[96,1280]{1,0:T(8,128)(2,1)S(1)}, bf16[96,1280]{1,0:T(8,128)(2,1)}, u32[]{:S(2)}) copy-start(bf16[96,1280]{1,0:T(8,128)(2,1)} %copy-done) | copy-start | bytes 737284
  25.8 4.8 %copy-start.3 = (bf16[96,1280]{1,0:T(8,128)(2,1)S(1)}, bf16[96,1280]{1,0:T(8,128)(2,1)}, u32[]{:S(2)}) copy-start(bf16[96,1280]{1,0:T(8,128)(2,1)} %refs_1_.3) | copy-start | bytes 737284
  25.8 15.9 %collective-permute-start.6 = (bf16[96,1280]{1,0:T(8,128)(2,1)S(1)}, bf16[96,1280]{1,0:T(8,128)(2,1)S(1)}, u32[]{:S(2)}, u32[]{:S(2)}) collective-permute-start(bf16[96,1280]{1,0:T(8,128)(2,1)S(1)} %pair_near.1.refs_1_.refs_0_), channel_id=1, source_target_pairs={{0,3},{1,2},{2,1},{3,0},{4,7},{5,6},{6,5},{7,4},{8,11},{9,10},{10,... | collective-permute-start | bytes 737288 | tf_op jit(solution)/shard_map/ppermute | solution.py:24
  37.0 10.7 %collective-permute-start.10 = (bf16[96,1280]{1,0:T(8,128)(2,1)S(1)}, bf16[96,1280]{1,0:T(8,128)(2,1)S(1)}, u32[]{:S(2)}, u32[]{:S(2)}) collective-permute-start(bf16[96,1280]{1,0:T(8,128)(2,1)S(1)} %pair_far.1.refs_2_.refs_0_), channel_id=1, source_target_pairs={{0,3},{1,2},{2,1},{3,0},{4,7},{5,6},{6,5},{7,4},{8,11},{9,10},{10,... | collective-permute-start | bytes 737288 | tf_op jit(solution)/shard_map/ppermute | solution.py:24
  40.2 9.4 %collective-permute-start.12 = (bf16[96,1280]{1,0:T(8,128)(2,1)S(1)}, bf16[96,1280]{1,0:T(8,128)(2,1)S(1)}, u32[]{:S(2)}, u32[]{:S(2)}) collective-permute-start(bf16[96,1280]{1,0:T(8,128)(2,1)S(1)} %get-tuple-element.25), channel_id=1, source_target_pairs={{0,8},{4,12},{8,0},{12,4},{1,9},{5,13},{9,1},{13,5},{2,10},{6,14},... | collective-permute-start | bytes 737288 | tf_op jit(solution)/shard_map/ppermute | solution.py:24
  41.8 10.5 %collective-permute-start.9 = (bf16[96,1280]{1,0:T(8,128)(2,1)S(1)}, bf16[96,1280]{1,0:T(8,128)(2,1)S(1)}, u32[]{:S(2)}, u32[]{:S(2)}) collective-permute-start(bf16[96,1280]{1,0:T(8,128)(2,1)S(1)} %total_near.1.refs_3_.refs_1_), channel_id=1, source_target_pairs={{0,1},{1,0},{2,3},{3,2},{4,5},{5,4},{6,7},{7,6},{8,9},{9,8},{10,11... | collective-permute-start | bytes 737288 | tf_op jit(solution)/shard_map/ppermute | solution.py:24
  42.0 11.5 %collective-permute-start.13 = (bf16[96,1280]{1,0:T(8,128)(2,1)S(1)}, bf16[96,1280]{1,0:T(8,128)(2,1)S(1)}, u32[]{:S(2)}, u32[]{:S(2)}) collective-permute-start(bf16[96,1280]{1,0:T(8,128)(2,1)S(1)} %get-tuple-element.23.refs_2_), channel_id=1, source_target_pairs={{0,8},{4,12},{8,0},{12,4},{1,9},{5,13},{9,1},{13,5},{2,10},{6,14},... | collective-permute-start | bytes 737288 | tf_op jit(solution)/shard_map/ppermute | solution.py:24
  47.7 9.7 %collective-permute-start.11 = (bf16[96,1280]{1,0:T(8,128)(2,1)S(1)}, bf16[96,1280]{1,0:T(8,128)(2,1)S(1)}, u32[]{:S(2)}, u32[]{:S(2)}) collective-permute-start(bf16[96,1280]{1,0:T(8,128)(2,1)S(1)} %total_far.1.refs_3_), channel_id=1, source_target_pairs={{0,1},{1,0},{2,3},{3,2},{4,5},{5,4},{6,7},{7,6},{8,9},{9,8},{10,11... | collective-permute-start | bytes 737288 | tf_op jit(solution)/shard_map/ppermute | solution.py:24
  53.5 3.9 %collective-permute-start.15 = (bf16[96,1280]{1,0:T(8,128)(2,1)S(1)}, bf16[96,1280]{1,0:T(8,128)(2,1)S(1)}, u32[]{:S(2)}, u32[]{:S(2)}) collective-permute-start(bf16[96,1280]{1,0:T(8,128)(2,1)S(1)} %panel_sum_low.1.refs_1_.refs_6_), channel_id=1, source_target_pairs={{0,4},{4,0},{8,12},{12,8},{1,5},{5,1},{9,13},{13,9},{2,6},{6,2},{1... | collective-permute-start | bytes 737288 | tf_op jit(solution)/shard_map/ppermute | solution.py:24
  53.6 3.8 %collective-permute-start.14 = (bf16[96,1280]{1,0:T(8,128)(2,1)S(1)}, bf16[96,1280]{1,0:T(8,128)(2,1)S(1)}, u32[]{:S(2)}, u32[]{:S(2)}) collective-permute-start(bf16[96,1280]{1,0:T(8,128)(2,1)S(1)} %panel_sum_top.1.refs_2_.refs_5_), channel_id=1, source_target_pairs={{0,4},{4,0},{8,12},{12,8},{1,5},{5,1},{9,13},{13,9},{2,6},{6,2},{1... | collective-permute-start | bytes 737288 | tf_op jit(solution)/shard_map/ppermute | solution.py:24
